TPU v7x, 32 devices: a whole 2x2x4 slice. The times are simulated.
32 devices in a mesh: seq: 8 (over y, x, core), fsdp: 4 (over z).
Axes of the slice: x: 2, y: 2, z: 4, core: 2. Of those that a mesh axis runs over, the one named last changes fastest.
Arguments:
- inputs: bfloat16 [2, 4, 512, 2048], P(None, 'fsdp', 'seq'), may hold values from -6 to 6
- cotangent: bfloat16 [2, 4, 512, 2048], P(None, 'fsdp', 'seq'), may hold values from -6 to 6
- block_ids: int32 [2, 4, 512], P(None, 'fsdp'), may hold values from 0 to 3, never falling along the last dimension, each value on 1 to 256 neighbouring positions
- ln1_gain: bfloat16 [2048], P(('seq', 'fsdp')), may hold values from 0.5 to 1.5
- ln1_bias: bfloat16 [2048], P(('seq', 'fsdp')), may hold values from -1 to 1
- qkv_weight: bfloat16 [2048, 6144], P(('seq', 'fsdp')), may hold values from -0.125 to 0.125
- qkv_bias: bfloat16 [6144], P(('seq', 'fsdp')), may hold values from -0.5 to 0.5
- out_weight: bfloat16 [2048, 2048], P(('seq', 'fsdp')), may hold values from -1 to 1
- ln2_gain: bfloat16 [2048], P(('seq', 'fsdp')), may hold values from 0.5 to 1.5
- ln2_bias: bfloat16 [2048], P(('seq', 'fsdp')), may hold values from -1 to 1
- gate_weight: bfloat16 [2048, 5632], P(('seq', 'fsdp')), may hold values from -0.125 to 0.125
- up_weight: bfloat16 [2048, 5632], P(('seq', 'fsdp')), may hold values from -0.125 to 0.125
- down_weight: bfloat16 [5632, 2048], P(('seq', 'fsdp')), may hold values from -0.078125 to 0.078125
Outputs:
- layer_out: bfloat16 [2, 4, 512, 2048], P(None, 'fsdp', 'seq')
- input_grad: bfloat16 [2, 4, 512, 2048], P(None, 'fsdp', 'seq')
- ln1_gain_grad: float32 [2048], P(('seq', 'fsdp'))
- ln1_bias_grad: float32 [2048], P(('seq', 'fsdp'))
- qkv_weight_grad: float32 [2048, 6144], P(('seq', 'fsdp'))
- qkv_bias_grad: float32 [6144], P(('seq', 'fsdp'))
- out_weight_grad: float32 [2048, 2048], P(('seq', 'fsdp'))
- ln2_gain_grad: float32 [2048], P(('seq', 'fsdp'))
- ln2_bias_grad: float32 [2048], P(('seq', 'fsdp'))
- gate_weight_grad: float32 [2048, 5632], P(('seq', 'fsdp'))
- up_weight_grad: float32 [2048, 5632], P(('seq', 'fsdp'))
- down_weight_grad: float32 [5632, 2048], P(('seq', 'fsdp'))
Inputs may be any that keep to these rules, and one draw needn't show every extreme that they name: `block_ids`: along each sequence the block ids never fall; each block holds 1 to 256 tokens.
All inputs are finite; a program needn't handle non-finite values.
Results may differ from a plain program's by a relative error of at most 0.014.
Values may be sent and summed in bfloat16 or wider, within the bound.
No kernel may reach another device: no remote copies, remote signals or barrier semaphores. Data moves between devices by JAX's collectives and lax.ppermute only.
A program may use at most 448 MiB of HBM per device.

v0:
```python
import jax
import jax.numpy as jnp
from jax import lax
from jax.sharding import PartitionSpec as P

H = 32
HD = 64
ROT = 16


eps_norm = 1e-05
rope_base = 10000.0
masked_score = -1e30


def norm_stats(values):
    average = jnp.mean(values, axis=-1, keepdims=True)
    centered = values - average
    inv_std = lax.rsqrt(jnp.mean(centered * centered, axis=-1, keepdims=True) + eps_norm)
    return (centered * inv_std, inv_std)


def norm_back(grad_normed, normed, inv_std):
    first_mean = jnp.mean(grad_normed, axis=-1, keepdims=True)
    second_mean = jnp.mean(grad_normed * normed, axis=-1, keepdims=True)
    return inv_std * (grad_normed - first_mean - normed * second_mean)


def rope_tables(positions):
    half_rot = ROT // 2
    frequency = rope_base ** (-2.0 * jnp.arange(half_rot).astype(jnp.float32) / ROT)
    angles = positions.astype(jnp.float32)[:, None] * frequency[None, :]
    return (jnp.cos(angles)[:, None, :], jnp.sin(angles)[:, None, :])


def rotate(values, cosine, sine_part, direction):
    half_rot = ROT // 2
    front_part = values[..., :half_rot]
    back_part = values[..., half_rot:ROT]
    return jnp.concatenate(
        [
            front_part * cosine - direction * back_part * sine_part,
            back_part * cosine + direction * front_part * sine_part,
            values[..., ROT:],
        ],
        axis=-1,
    )


def fetch_attention(gain_one, offset_one, weight_qkv, bias_qkv, weight_out):
    return (
        lax.all_gather(gain_one, ("seq", "fsdp"), axis=0, tiled=True),
        lax.all_gather(offset_one, ("seq", "fsdp"), axis=0, tiled=True),
        lax.all_gather(weight_qkv, ("seq", "fsdp"), axis=0, tiled=True),
        lax.all_gather(bias_qkv, ("seq", "fsdp"), axis=0, tiled=True),
        lax.all_gather(weight_out, ("seq", "fsdp"), axis=0, tiled=True),
    )


def fetch_feedforward(gain_two, offset_two, weight_gate, weight_up, weight_down):
    return (
        lax.all_gather(gain_two, ("seq", "fsdp"), axis=0, tiled=True),
        lax.all_gather(offset_two, ("seq", "fsdp"), axis=0, tiled=True),
        lax.all_gather(weight_gate, ("seq", "fsdp"), axis=0, tiled=True),
        lax.all_gather(weight_up, ("seq", "fsdp"), axis=0, tiled=True),
        lax.all_gather(weight_down, ("seq", "fsdp"), axis=0, tiled=True),
    )


def block_scores(query_rows, keys_all, row_ids, blocks, scaling):
    scores = (
        jnp.einsum("qhd,khd->hqk", query_rows, keys_all, preferred_element_type=jnp.float32)
        * scaling
    )
    return jnp.where(row_ids[None, :, None] >= blocks[None, None, :], scores, masked_score)


def attend_forward(packed, blocks):
    length_all = packed.shape[0]
    head_count = packed.shape[1]
    block_rows = min(512, length_all)
    queries = packed[:, :, :HD]
    keys_all = packed[:, :, HD : 2 * HD]
    values = packed[:, :, 2 * HD :]
    scaling = HD ** (-0.5)

    def one_block(scan_state, block_index):
        row_start = block_index * block_rows
        query_rows = lax.dynamic_slice_in_dim(queries, row_start, block_rows, 0)
        row_ids = lax.dynamic_slice_in_dim(blocks, row_start, block_rows, 0)
        scores = block_scores(query_rows, keys_all, row_ids, blocks, scaling)
        peak_score = jnp.max(scores, axis=-1, keepdims=True)
        expo_values = jnp.exp(scores - peak_score)
        row_total = jnp.sum(expo_values, axis=-1, keepdims=True)
        weights = (expo_values / row_total).astype(jnp.bfloat16)
        output = jnp.einsum(
            "hqk,khd->qhd", weights, values, preferred_element_type=jnp.float32
        ).astype(jnp.bfloat16)
        return (scan_state, (output, peak_score[..., 0] + jnp.log(row_total[..., 0])))

    unused_state, (outputs, log_sums) = lax.scan(
        one_block, jnp.int32(0), jnp.arange(length_all // block_rows, dtype=jnp.int32)
    )
    return (outputs.reshape(length_all, head_count, HD), log_sums)


def attend_backward(packed, grad_heads, log_sums, blocks, full_cos, full_sin):
    length_all = packed.shape[0]
    head_count = packed.shape[1]
    block_rows = min(512, length_all)
    queries = packed[:, :, :HD]
    keys_all = packed[:, :, HD : 2 * HD]
    values = packed[:, :, 2 * HD :]
    scaling = HD ** (-0.5)

    def one_block(scan_state, pieces):
        key_grad, value_grad = scan_state
        block_index, row_lse = pieces
        row_start = block_index * block_rows
        query_rows = lax.dynamic_slice_in_dim(queries, row_start, block_rows, 0)
        row_ids = lax.dynamic_slice_in_dim(blocks, row_start, block_rows, 0)
        grad_rows = lax.dynamic_slice_in_dim(grad_heads, row_start, block_rows, 0)
        scores = block_scores(query_rows, keys_all, row_ids, blocks, scaling)
        probabilities = jnp.exp(scores - row_lse[..., None])
        grad_probs = jnp.einsum(
            "qhd,khd->hqk", grad_rows, values, preferred_element_type=jnp.float32
        )
        inner_sum = jnp.sum(probabilities * grad_probs, axis=-1, keepdims=True)
        grad_scores = (probabilities * (grad_probs - inner_sum)).astype(jnp.bfloat16)
        query_grad = (
            jnp.einsum("hqk,khd->qhd", grad_scores, keys_all, preferred_element_type=jnp.float32)
            * scaling
        )
        key_grad = (
            key_grad
            + jnp.einsum(
                "hqk,qhd->khd", grad_scores, query_rows, preferred_element_type=jnp.float32
            )
            * scaling
        )
        value_grad = value_grad + jnp.einsum(
            "hqk,qhd->khd",
            probabilities.astype(jnp.bfloat16),
            grad_rows,
            preferred_element_type=jnp.float32,
        )
        return ((key_grad, value_grad), query_grad)

    zero_grad = jnp.zeros(keys_all.shape, jnp.float32)
    (key_grad, value_grad), query_grad = lax.scan(
        one_block,
        (zero_grad, zero_grad),
        (jnp.arange(length_all // block_rows, dtype=jnp.int32), log_sums),
    )
    query_grad = query_grad.reshape(length_all, head_count, HD)
    query_lin = rotate(query_grad, full_cos, full_sin, -1.0)
    key_lin = rotate(key_grad, full_cos, full_sin, -1.0)
    return jnp.concatenate([query_lin, key_lin, value_grad], axis=-1).astype(jnp.bfloat16)


def shards(
    inputs,
    cotangent,
    block_ids,
    ln1_gain,
    ln1_bias,
    qkv_weight,
    qkv_bias,
    out_weight,
    ln2_gain,
    ln2_bias,
    gate_weight,
    up_weight,
    down_weight,
):
    batches = inputs.shape[0]
    tok_rows = inputs.shape[2]
    model_width = inputs.shape[3]
    length_all = block_ids.shape[2]
    local_pos = lax.axis_index("seq") * tok_rows + jnp.arange(tok_rows, dtype=jnp.int32)
    part_cos, part_sin = rope_tables(local_pos)
    full_cos, full_sin = rope_tables(jnp.arange(length_all, dtype=jnp.int32))
    attn_params = None
    attn_kept = []
    mixed_list = []
    for batch_index in range(batches):
        attn_params = fetch_attention(ln1_gain, ln1_bias, qkv_weight, qkv_bias, out_weight)
        gain_one, offset_one, weight_qkv, bias_qkv, weight_out = attn_params
        tokens = inputs[batch_index, 0].astype(jnp.float32)
        normed, inv_std = norm_stats(tokens)
        hidden = (normed * gain_one.astype(jnp.float32) + offset_one.astype(jnp.float32)).astype(
            jnp.bfloat16
        )
        linear = (
            jnp.dot(hidden, weight_qkv, preferred_element_type=jnp.float32)
            + bias_qkv.astype(jnp.float32)
        ).reshape(tok_rows, H, 3, HD)
        packed = jnp.concatenate(
            [
                rotate(linear[:, :, 0], part_cos, part_sin, 1.0),
                rotate(linear[:, :, 1], part_cos, part_sin, 1.0),
                linear[:, :, 2],
            ],
            axis=-1,
        ).astype(jnp.bfloat16)
        heads_packed = lax.all_to_all(packed, "seq", split_axis=1, concat_axis=0, tiled=True)
        out_heads, log_sums = attend_forward(heads_packed, block_ids[batch_index, 0])
        attended = lax.all_to_all(
            out_heads, "seq", split_axis=0, concat_axis=1, tiled=True
        ).reshape(tok_rows, model_width)
        mixed_sum = tokens + jnp.dot(attended, weight_out, preferred_element_type=jnp.float32)
        attn_kept.append((normed, inv_std, hidden, heads_packed, log_sums, attended))
        mixed_list.append(mixed_sum)
    ffn_params = None
    ffn_kept = []
    layer_outs = []
    for batch_index in range(batches):
        ffn_params = fetch_feedforward(ln2_gain, ln2_bias, gate_weight, up_weight, down_weight)
        gain_two, offset_two, weight_gate, weight_up, weight_down = ffn_params
        mixed_sum = mixed_list[batch_index]
        normed_two, inv_two = norm_stats(mixed_sum)
        hidden_two = (
            normed_two * gain_two.astype(jnp.float32) + offset_two.astype(jnp.float32)
        ).astype(jnp.bfloat16)
        gate_value = jnp.dot(hidden_two, weight_gate, preferred_element_type=jnp.float32)
        up_value = jnp.dot(hidden_two, weight_up, preferred_element_type=jnp.float32)
        active = (jax.nn.silu(gate_value) * up_value).astype(jnp.bfloat16)
        layer_outs.append(
            (mixed_sum + jnp.dot(active, weight_down, preferred_element_type=jnp.float32)).astype(
                jnp.bfloat16
            )
        )
        ffn_kept.append((normed_two, inv_two, hidden_two, gate_value, up_value, active))
    ffn_params = None
    grad_mixed_list = []
    grad_gates = []
    grad_ups = []
    gain_two_grad = jnp.zeros((model_width,), jnp.float32)
    offset_two_grad = jnp.zeros((model_width,), jnp.float32)
    for batch_index in range(batches):
        ffn_params = fetch_feedforward(ln2_gain, ln2_bias, gate_weight, up_weight, down_weight)
        gain_two, offset_two, weight_gate, weight_up, weight_down = ffn_params
        normed_two, inv_two, hidden_two, gate_value, up_value, active = ffn_kept[batch_index]
        grad_output = cotangent[batch_index, 0]
        grad_active = jnp.dot(grad_output, weight_down.T, preferred_element_type=jnp.float32)
        sigmoid_gate = jax.nn.sigmoid(gate_value)
        grad_gate = (
            grad_active * up_value * sigmoid_gate * (1.0 + gate_value * (1.0 - sigmoid_gate))
        ).astype(jnp.bfloat16)
        grad_up = (grad_active * (gate_value * sigmoid_gate)).astype(jnp.bfloat16)
        grad_hidden_two = jnp.dot(
            grad_gate, weight_gate.T, preferred_element_type=jnp.float32
        ) + jnp.dot(grad_up, weight_up.T, preferred_element_type=jnp.float32)
        gain_two_grad = gain_two_grad + jnp.sum(grad_hidden_two * normed_two, axis=0)
        offset_two_grad = offset_two_grad + jnp.sum(grad_hidden_two, axis=0)
        grad_mixed_list.append(
            grad_output.astype(jnp.float32)
            + norm_back(grad_hidden_two * gain_two.astype(jnp.float32), normed_two, inv_two)
        )
        grad_gates.append(grad_gate)
        grad_ups.append(grad_up)
    hidden_two_all = jnp.concatenate(
        [ffn_kept[batch_index][2] for batch_index in range(batches)], axis=0
    )
    active_all = jnp.concatenate(
        [ffn_kept[batch_index][5] for batch_index in range(batches)], axis=0
    )
    term_gate = jnp.einsum(
        "td,tf->df",
        hidden_two_all,
        jnp.concatenate(grad_gates, axis=0),
        preferred_element_type=jnp.float32,
    )
    term_up = jnp.einsum(
        "td,tf->df",
        hidden_two_all,
        jnp.concatenate(grad_ups, axis=0),
        preferred_element_type=jnp.float32,
    )
    term_down = jnp.einsum(
        "tf,td->fd",
        active_all,
        cotangent[:, 0].reshape(batches * tok_rows, model_width),
        preferred_element_type=jnp.float32,
    )
    attn_params = None
    grad_linears = []
    grad_attns = []
    input_grads = []
    gain_one_grad = jnp.zeros((model_width,), jnp.float32)
    offset_one_grad = jnp.zeros((model_width,), jnp.float32)
    for batch_index in range(batches):
        attn_params = fetch_attention(ln1_gain, ln1_bias, qkv_weight, qkv_bias, out_weight)
        gain_one, offset_one, weight_qkv, bias_qkv, weight_out = attn_params
        normed, inv_std, hidden, heads_packed, log_sums, attended = attn_kept[batch_index]
        grad_mixed = grad_mixed_list[batch_index]
        grad_attn = grad_mixed.astype(jnp.bfloat16)
        grad_attended = (
            jnp.dot(grad_attn, weight_out.T, preferred_element_type=jnp.float32)
            .astype(jnp.bfloat16)
            .reshape(tok_rows, H, HD)
        )
        grad_heads = lax.all_to_all(grad_attended, "seq", split_axis=1, concat_axis=0, tiled=True)
        grad_packed = attend_backward(
            heads_packed, grad_heads, log_sums, block_ids[batch_index, 0], full_cos, full_sin
        )
        grad_linear = lax.all_to_all(
            grad_packed, "seq", split_axis=0, concat_axis=1, tiled=True
        ).reshape(tok_rows, 3 * model_width)
        grad_hidden = jnp.dot(grad_linear, weight_qkv.T, preferred_element_type=jnp.float32)
        gain_one_grad = gain_one_grad + jnp.sum(grad_hidden * normed, axis=0)
        offset_one_grad = offset_one_grad + jnp.sum(grad_hidden, axis=0)
        input_grads.append(
            (
                grad_mixed + norm_back(grad_hidden * gain_one.astype(jnp.float32), normed, inv_std)
            ).astype(jnp.bfloat16)
        )
        grad_linears.append(grad_linear)
        grad_attns.append(grad_attn)
    hidden_all = jnp.concatenate(
        [attn_kept[batch_index][2] for batch_index in range(batches)], axis=0
    )
    attended_all = jnp.concatenate(
        [attn_kept[batch_index][5] for batch_index in range(batches)], axis=0
    )
    grad_linear_all = jnp.concatenate(grad_linears, axis=0)
    term_qkv = jnp.einsum(
        "td,tf->df", hidden_all, grad_linear_all, preferred_element_type=jnp.float32
    )
    term_bias = jnp.sum(grad_linear_all, axis=0, dtype=jnp.float32)
    term_out = jnp.einsum(
        "td,tf->df",
        attended_all,
        jnp.concatenate(grad_attns, axis=0),
        preferred_element_type=jnp.float32,
    )
    grad_shards = (
        lax.psum_scatter(gain_one_grad, ("seq", "fsdp"), scatter_dimension=0, tiled=True),
        lax.psum_scatter(offset_one_grad, ("seq", "fsdp"), scatter_dimension=0, tiled=True),
        lax.psum_scatter(term_qkv, ("seq", "fsdp"), scatter_dimension=0, tiled=True),
        lax.psum_scatter(term_bias, ("seq", "fsdp"), scatter_dimension=0, tiled=True),
        lax.psum_scatter(term_out, ("seq", "fsdp"), scatter_dimension=0, tiled=True),
        lax.psum_scatter(gain_two_grad, ("seq", "fsdp"), scatter_dimension=0, tiled=True),
        lax.psum_scatter(offset_two_grad, ("seq", "fsdp"), scatter_dimension=0, tiled=True),
        lax.psum_scatter(term_gate, ("seq", "fsdp"), scatter_dimension=0, tiled=True),
        lax.psum_scatter(term_up, ("seq", "fsdp"), scatter_dimension=0, tiled=True),
        lax.psum_scatter(term_down, ("seq", "fsdp"), scatter_dimension=0, tiled=True),
    )
    layer_out = jnp.stack(layer_outs)[:, None]
    input_grad = jnp.stack(input_grads)[:, None]
    return (
        layer_out,
        input_grad,
        grad_shards[0],
        grad_shards[1],
        grad_shards[2],
        grad_shards[3],
        grad_shards[4],
        grad_shards[5],
        grad_shards[6],
        grad_shards[7],
        grad_shards[8],
        grad_shards[9],
    )


def solution(mesh):
    in_specs = (
        P(None, "fsdp", "seq", None),
        P(None, "fsdp", "seq", None),
        P(None, "fsdp", None),
        P(("seq", "fsdp")),
        P(("seq", "fsdp")),
        P(("seq", "fsdp"), None),
        P(("seq", "fsdp")),
        P(("seq", "fsdp"), None),
        P(("seq", "fsdp")),
        P(("seq", "fsdp")),
        P(("seq", "fsdp"), None),
        P(("seq", "fsdp"), None),
        P(("seq", "fsdp"), None),
    )
    out_specs = (
        P(None, "fsdp", "seq", None),
        P(None, "fsdp", "seq", None),
        P(("seq", "fsdp")),
        P(("seq", "fsdp")),
        P(("seq", "fsdp"), None),
        P(("seq", "fsdp")),
        P(("seq", "fsdp"), None),
        P(("seq", "fsdp")),
        P(("seq", "fsdp")),
        P(("seq", "fsdp"), None),
        P(("seq", "fsdp"), None),
        P(("seq", "fsdp"), None),
    )
    return jax.shard_map(shards, mesh=mesh, in_specs=in_specs, out_specs=out_specs, check_vma=False)
```

profile of v0, /device:TPU:0, one launch (start us, length us, event | category | flops | bytes accessed | tf_op | source)
XLA Modules:
  0.0 4515.2 jit_solution(13522739989750618782)
XLA Ops:
  14.8 43.2 all-reduce.11
  60.4 109.4 %all-gather.6.cloned.1.call-done = bf16[2048,6144]{1,0:T(8,128)(2,1)} async-done(((bf16[64,6144]{1,0:T(8,128)(2,1)}), bf16[2048,6144]{1,0:T(8,128)(2,1)}) %all-gather.6.cloned.1.call-update) | async-done | bytes 25165840 | tf_op jit(solution)/shard_map/all_gather | solution.py:54
  300.2 105.2 %all-gather.10.cloned.1.call-done = bf16[2048,5632]{1,0:T(8,128)(2,1)} async-done(((bf16[64,5632]{1,0:T(8,128)(2,1)}), bf16[2048,5632]{1,0:T(8,128)(2,1)}) %all-gather.10.cloned.1.call-update) | async-done | bytes 23068688 | tf_op jit(solution)/shard_map/all_gather | solution.py:64
  416.4 134.5 %all-gather.12.cloned.1.call-done = bf16[2048,5632]{1,0:T(8,128)(2,1)} async-done(((bf16[64,5632]{1,0:T(8,128)(2,1)}), bf16[2048,5632]{1,0:T(8,128)(2,1)}) %all-gather.12.cloned.1.call-update) | async-done | bytes 23068688 | tf_op jit(solution)/shard_map/all_gather | solution.py:65
  551.0 12.7 fusion.143
  579.9 116.6 %all-gather.14.cloned.1.call-done = bf16[5632,2048]{1,0:T(8,128)(2,1)} async-done(((bf16[176,2048]{1,0:T(8,128)(2,1)}), bf16[5632,2048]{1,0:T(8,128)(2,1)}) %all-gather.14.cloned.1.call-update) | async-done | bytes 23068688 | tf_op jit(solution)/shard_map/all_gather | solution.py:66
  696.4 12.7 multiply_convert_fusion.2
  709.1 12.5 fusion.145
  721.6 13.5 multiply_convert_fusion.4
  735.1 11.6 fusion.144
  758.2 13.6 multiply_reduce_fusion.3
  867.7 14.3 all-to-all-done.5
  889.6 21.0 fusion.88
  911.6 19.4 fusion.16
  931.1 18.2 fusion.20
  950.7 18.2 fusion.24
  991.9 12.6 fusion.146
  1004.5 12.9 fusion.86
  1019.1 41.1 all-reduce.10
  1065.6 80.6 %reduce-scatter.8.cloned.1.call-done = f32[64,2048]{1,0:T(8,128)} async-done(((f32[2048,2048]{1,0:T(8,128)}), f32[64,2048]{1,0:T(8,128)}) %reduce-scatter.8.cloned.1.call-update) | async-done | bytes 524304 | tf_op jit(solution)/shard_map/reduce_scatter | solution.py:342
  1146.1 436.5 %reduce-scatter.6.cloned.1.call-done = f32[64,6144]{1,0:T(8,128)} async-done(((f32[2048,6144]{1,0:T(8,128)}), f32[64,6144]{1,0:T(8,128)}) %reduce-scatter.6.cloned.1.call-update) | async-done | bytes 1572880 | tf_op jit(solution)/shard_map/reduce_scatter | solution.py:340
  1582.7 974.3 %reduce-scatter.10.cloned.1.call-done = f32[64,5632]{1,0:T(8,128)} async-done(((f32[2048,5632]{1,0:T(8,128)}), f32[64,5632]{1,0:T(8,128)}) %reduce-scatter.10.cloned.1.call-update) | async-done | bytes 1441808 | tf_op jit(solution)/shard_map/reduce_scatter | solution.py:345
  2556.9 975.7 %reduce-scatter.12.cloned.1.call-done = f32[64,5632]{1,0:T(8,128)} async-done(((f32[2048,5632]{1,0:T(8,128)}), f32[64,5632]{1,0:T(8,128)}) %reduce-scatter.12.cloned.1.call-update) | async-done | bytes 1441808 | tf_op jit(solution)/shard_map/reduce_scatter | solution.py:346
  3532.6 975.5 %reduce-scatter.14.cloned.1.call-done = f32[176,2048]{1,0:T(8,128)} async-done(((f32[5632,2048]{1,0:T(8,128)}), f32[176,2048]{1,0:T(8,128)}) %reduce-scatter.14.cloned.1.call-update) | async-done | bytes 1441808 | tf_op jit(solution)/shard_map/reduce_scatter | solution.py:347
  (334 shorter events, 313.9 us)
Async XLA Ops:
  7.2 162.6 %all-gather.6.cloned.1.call-start = ((), (), s32[]{:S(2)}) async-start(), calls=%async_computation.13 | async-start | bytes 25952256 | tf_op jit(solution)/shard_map/all_gather | solution.py:54
  7.9 283.5 %all-gather.8.cloned.1.call-start = ((), (), s32[]{:S(2)}) async-start(), calls=%async_computation.14 | async-start | bytes 8650752 | tf_op jit(solution)/shard_map/all_gather | solution.py:56
  8.7 396.8 %all-gather.10.cloned.1.call-start = ((), (), s32[]{:S(2)}) async-start(), calls=%async_computation.15 | async-start | bytes 23789568 | tf_op jit(solution)/shard_map/all_gather | solution.py:64
  9.4 541.5 %all-gather.12.cloned.1.call-start = ((), (), s32[]{:S(2)}) async-start(), calls=%async_computation.16 | async-start | bytes 23789568 | tf_op jit(solution)/shard_map/all_gather | solution.py:65
  10.0 686.5 %all-gather.14.cloned.1.call-start = ((), (), s32[]{:S(2)}) async-start(), calls=%async_computation.17 | async-start | bytes 23789568 | tf_op jit(solution)/shard_map/all_gather | solution.py:66
  58.0 122.3 %copy-start.44 = (f32[2048]{0:T(1024)}, f32[2048]{0:T(1024)S(1)}, u32[]{:S(2)}) copy-start(f32[2048]{0:T(1024)S(1)} %convert_element_type.227) | copy-start | bytes 24580
  60.4 123.8 %copy-start.32 = (bf16[64,2048]{1,0:T(8,128)(2,1)}, bf16[64,2048]{1,0:T(8,128)(2,1)S(1)}, u32[]{:S(2)}) copy-start(bf16[64,2048]{1,0:T(8,128)(2,1)S(1)} %get-tuple-element.229) | copy-start | bytes 786436
  225.1 22.6 all-to-all-start.2
  247.7 19.1 all-to-all-start
  266.8 13.4 all-to-all-start.3
  280.1 10.3 all-to-all-start.1
  283.6 862.6 %reduce-scatter.8.cloned.1.call-start = ((), (), s32[]{:S(2)}) async-start(), calls=%async_computation.19 | async-start | bytes 17301504 | tf_op jit(solution)/shard_map/reduce_scatter | solution.py:342
  297.3 474.5 %copy-start.5 = (f32[64,2048]{1,0:T(8,128)}, f32[64,2048]{1,0:T(8,128)S(1)}, u32[]{:S(2)}) copy-start(f32[64,2048]{1,0:T(8,128)S(1)} %get-tuple-element.259) | copy-start | bytes 1572868
  299.6 472.2 %copy-start.7 = (f32[64,2048]{1,0:T(8,128)}, f32[64,2048]{1,0:T(8,128)S(1)}, u32[]{:S(2)}) copy-start(f32[64,2048]{1,0:T(8,128)S(1)} %get-tuple-element.261) | copy-start | bytes 1572868
  300.2 250.8 %copy-start.15 = (bf16[64,2048]{1,0:T(8,128)(2,1)}, bf16[64,2048]{1,0:T(8,128)(2,1)S(1)}, u32[]{:S(2)}) copy-start(bf16[64,2048]{1,0:T(8,128)(2,1)S(1)} %get-tuple-element.243) | copy-start | bytes 786436
  300.2 274.5 %copy-start.13 = (bf16[64,2048]{1,0:T(8,128)(2,1)}, bf16[64,2048]{1,0:T(8,128)(2,1)S(1)}, u32[]{:S(2)}) copy-start(bf16[64,2048]{1,0:T(8,128)(2,1)S(1)} %get-tuple-element.242) | copy-start | bytes 786436
  792.2 12.0 all-to-all-start.4
  804.2 12.6 all-to-all-start.6
  835.9 22.6 all-to-all-start.7
  858.5 23.5 all-to-all-start.5
  862.8 719.9 %reduce-scatter.6.cloned.1.call-start = ((), (), s32[]{:S(2)}) async-start(), calls=%async_computation.18 | async-start | bytes 51904512 | tf_op jit(solution)/shard_map/reduce_scatter | solution.py:340
  910.6 1646.3 %reduce-scatter.10.cloned.1.call-start = ((), (), s32[]{:S(2)}) async-start(), calls=%async_computation.20 | async-start | bytes 47579136 | tf_op jit(solution)/shard_map/reduce_scatter | solution.py:345
  931.0 2601.6 %reduce-scatter.12.cloned.1.call-start = ((), (), s32[]{:S(2)}) async-start(), calls=%async_computation.21 | async-start | bytes 47579136 | tf_op jit(solution)/shard_map/reduce_scatter | solution.py:346
  949.3 3558.9 %reduce-scatter.14.cloned.1.call-start = ((), (), s32[]{:S(2)}) async-start(), calls=%async_computation.22 | async-start | bytes 47579136 | tf_op jit(solution)/shard_map/reduce_scatter | solution.py:347
  (66 other events, 1510.8 us)
Sparse Core Ops, SparseCore 0:
  10.9 158.8 all-gather.5
  172.7 81.0 all-gather.7
  256.6 148.7 all-gather.9
  408.1 142.7 all-gather.11
  553.6 142.7 all-gather.13
  782.8 363.3 reduce-scatter.7
  1153.1 429.4 reduce-scatter.5
  1585.5 971.3 reduce-scatter.9
  2559.8 972.7 reduce-scatter.11
  3535.3 972.7 reduce-scatter.13
where the time goes:
time: 4520 us
  waiting for transfers between devices  3960 us (88%)
  matrix products  301 us (7%)
  local copies, waits for them, and re-layouts  93.4 us (2%)
  blocking collectives  84.2 us (2%)
    reduce_scatter x1, waiting for transfers between devices, shards(): lax.psum_scatter(term_up, ('seq', 'fsdp'), scatter_dimension=0, tiled=True)  976 us
    reduce_scatter x1, waiting for transfers between devices, shards(): lax.psum_scatter(term_down, ('seq', 'fsdp'), scatter_dimension=0, tiled=T...  976 us
    reduce_scatter x1, waiting for transfers between devices, shards(): lax.psum_scatter(term_gate, ('seq', 'fsdp'), scatter_dimension=0, tiled=T...  974 us
    reduce_scatter x1, waiting for transfers between devices, shards(): lax.psum_scatter(term_qkv, ('seq', 'fsdp'), scatter_dimension=0, tiled=True)  437 us
    all_gather x1, waiting for transfers between devices, fetch_feedforward(): lax.all_gather(weight_up, ('seq', 'fsdp'), axis=0, tiled=True)  135 us
    all_gather x1, waiting for transfers between devices, fetch_feedforward(): lax.all_gather(weight_down, ('seq', 'fsdp'), axis=0, tiled=True)  117 us
    all_gather x1, waiting for transfers between devices, fetch_attention(): lax.all_gather(weight_qkv, ('seq', 'fsdp'), axis=0, tiled=True)  109 us
    all_gather x1, waiting for transfers between devices, fetch_feedforward(): lax.all_gather(weight_gate, ('seq', 'fsdp'), axis=0, tiled=True)  105 us
  transfers between devices with their start and end apart: 18, of which 16 were waited for; matrix products, arithmetic and copies ran while one was open for 7% of the time, Pallas kernels for 0%

commit v1 on v0

v1 whole, which is shorter than its diff:
```python
import jax
import jax.numpy as jnp
import numpy as np
from jax import lax
from jax.sharding import Mesh
from jax.sharding import PartitionSpec as P

H = 32
HD = 64
ROT = 16

eps_norm = 1e-05
rope_base = 10000.0
masked_score = -1e30

F32 = jnp.float32
BF16 = jnp.bfloat16

SWAP = [(0, 1), (1, 0)]
EVERY = ("sb", "sr", "fh", "fl")
MEMBERS = ("sr", "fl")


def swap_sb(v):
    return lax.ppermute(v, "sb", SWAP)


def swap_fh(v):
    return lax.ppermute(v, "fh", SWAP)


def swap_fl(v):
    return lax.ppermute(v, "fl", SWAP)


def swap_sr(v, bit):
    n = lax.axis_size("sr")
    return lax.ppermute(v, "sr", [(i, i ^ bit) for i in range(n)])


def norm_stats(values):
    average = jnp.mean(values, axis=-1, keepdims=True)
    centered = values - average
    inv_std = lax.rsqrt(jnp.mean(centered * centered, axis=-1, keepdims=True) + eps_norm)
    return (centered * inv_std, inv_std)


def norm_back(grad_normed, normed, inv_std):
    first_mean = jnp.mean(grad_normed, axis=-1, keepdims=True)
    second_mean = jnp.mean(grad_normed * normed, axis=-1, keepdims=True)
    return inv_std * (grad_normed - first_mean - normed * second_mean)


def gather_tokens(x):
    m = x.shape[0]
    h = m // 2
    a = swap_sr(x, 2)
    b = swap_fl(x)
    xo = swap_sr(x, 1)
    d1 = swap_fl(a[:h])
    d2 = swap_sr(b[h:], 2)
    ao = swap_sr(a, 1)
    bo = swap_sr(b, 1)
    d = jnp.concatenate([d1, d2], 0)
    do = swap_sr(d, 1)
    got = jnp.stack([x, xo, a, ao, b, bo, d, do]).reshape((2, 4) + x.shape)
    bit = 4
    while bit < lax.axis_size("sr"):
        got = jnp.concatenate([got, swap_sr(got, bit)], axis=1)
        bit *= 2
    return got


def scatter_tokens(p):
    bit = lax.axis_size("sr") // 2
    while bit >= 4:
        p = (p[:, :bit].astype(F32) + swap_sr(p[:, bit:], bit).astype(F32)).astype(BF16)
        bit //= 2
    m, width = p.shape[2:]
    h = m // 2
    p = p.reshape(2, 2, 2, m, width)
    q = p[:, :, 0].astype(F32) + swap_sr(p[:, :, 1], 1).astype(F32)
    qb = q.astype(BF16)
    u = q[:, 0, :h] + swap_sr(qb[:, 1, :h], 2).astype(F32)
    w = q[0, :, h:] + swap_fl(qb[1, :, h:]).astype(F32)
    top = u[0] + swap_fl(u[1].astype(BF16)).astype(F32)
    bottom = w[0] + swap_sr(w[1].astype(BF16), 2).astype(F32)
    return jnp.concatenate([top, bottom], 0)


def flip_if(bit, v, axis):
    return jnp.where(bit == 1, lax.rev(v, (axis,)), v)


def gather_groups(w):
    sb, fh = lax.axis_index("sb"), lax.axis_index("fh")
    z = swap_fh(w)
    yw = swap_sb(w)
    yz = swap_sb(z)
    low = jnp.where(fh == 1, z, w)
    high = jnp.where(fh == 1, w, z)
    ylow = jnp.where(fh == 1, yz, yw)
    yhigh = jnp.where(fh == 1, yw, yz)
    return jnp.stack(
        [
            jnp.stack([jnp.where(sb == 1, ylow, low), jnp.where(sb == 1, yhigh, high)]),
            jnp.stack([jnp.where(sb == 1, low, ylow), jnp.where(sb == 1, high, yhigh)]),
        ]
    )


def scatter_groups(part):
    fh = lax.axis_index("fh")
    got = swap_sb(part(1).astype(BF16))
    mine = part(0) + got.astype(F32)
    send = lax.dynamic_index_in_dim(mine, 1 - fh, 0, keepdims=False).astype(BF16)
    keep = lax.dynamic_index_in_dim(mine, fh, 0, keepdims=False)
    return keep + swap_fh(send).astype(F32)


def xor_order(v, axis, index, n):
    shape = v.shape
    bit = 1
    while bit < n:
        r = v.reshape(shape[:axis] + (n // (2 * bit), 2, bit) + shape[axis + 1 :])
        v = flip_if((index // bit) % 2, r, axis + 1).reshape(shape)
        bit *= 2
    return v


def attend(q, k, v, ids):
    s = jnp.einsum("qhd,khd->hqk", q, k, preferred_element_type=F32) * (HD**-0.5)
    s = jnp.where(ids[None, :, None] >= ids[None, None, :], s, masked_score)
    peak = jnp.max(s, axis=-1, keepdims=True)
    e = jnp.exp(s - peak)
    p = e / jnp.sum(e, axis=-1, keepdims=True)
    o = jnp.einsum("hqk,khd->qhd", p.astype(BF16), v, preferred_element_type=F32)
    return o.astype(BF16), p


def attend_back(q, k, v, p, do):
    dp = jnp.einsum("qhd,khd->hqk", do, v, preferred_element_type=F32)
    ds = (p * (dp - jnp.sum(p * dp, axis=-1, keepdims=True))).astype(BF16)
    dq = jnp.einsum("hqk,khd->qhd", ds, k, preferred_element_type=F32) * (HD**-0.5)
    dk = jnp.einsum("hqk,qhd->khd", ds, q, preferred_element_type=F32) * (HD**-0.5)
    dv = jnp.einsum("hqk,qhd->khd", p.astype(BF16), do, preferred_element_type=F32)
    return dq, dk, dv


def rotate(values, cosine, sine, direction):
    half = ROT // 2
    a = values[..., :half]
    b = values[..., half:ROT]
    return jnp.concatenate(
        [a * cosine - direction * b * sine, b * cosine + direction * a * sine, values[..., ROT:]],
        axis=-1,
    )


def shards(
    inputs,
    cotangent,
    block_ids,
    ln1_gain,
    ln1_bias,
    qkv_weight,
    qkv_bias,
    out_weight,
    ln2_gain,
    ln2_bias,
    gate_weight,
    up_weight,
    down_weight,
):
    sb, sr, fh, fl = (lax.axis_index(a) for a in EVERY)
    n_sr = lax.axis_size("sr")
    n_dev = 8 * n_sr
    members = 2 * n_sr
    tok = inputs.shape[2]
    D = inputs.shape[3]
    length = block_ids.shape[2]
    rows = qkv_weight.shape[0]
    ff_rows = down_weight.shape[0]
    FF = ff_rows * n_dev
    heads = H // members
    natural = H % n_dev == 0

    def pick(v, i):
        return lax.dynamic_index_in_dim(v, i, 0, keepdims=False)

    def whole_vector(v):
        return lax.all_gather(v, EVERY, axis=0, tiled=True).astype(F32)

    gain1, bias1, gain2, bias2, bias_qkv = (
        whole_vector(v) for v in (ln1_gain, ln1_bias, ln2_gain, ln2_bias, qkv_bias)
    )

    def by_member(v):
        lead = v.shape[:-1]
        nl = len(lead)
        if natural:
            v = v.reshape(lead + (2, n_sr, 2, 2, -1))
            v = v.transpose((nl + 1, nl + 3) + tuple(range(nl)) + (nl, nl + 2, nl + 4))
        else:
            v = v.reshape(lead + (n_sr, 2, -1))
            v = v.transpose((nl, nl + 1) + tuple(range(nl)) + (nl + 2,))
        return v.reshape((members,) + lead + (-1,))

    def from_members(v):
        lead = v.shape[1:-1]
        nl = len(lead)
        if natural:
            v = v.reshape((n_sr, 2) + lead + (2, 2, -1))
            back = tuple(range(2, 2 + nl)) + (2 + nl, 0, 3 + nl, 1, 4 + nl)
        else:
            v = v.reshape((n_sr, 2) + lead + (-1,))
            back = tuple(range(2, 2 + nl)) + (0, 1, 2 + nl)
        return v.transpose(back).reshape(lead + (-1,))

    def ff_by_member(v):
        lead = v.shape[0]
        v = v.reshape(lead, 2, n_sr, 2, 2, ff_rows).transpose(2, 4, 0, 1, 3, 5)
        return v.reshape(members, lead, 4 * ff_rows)

    def ff_from_members(v):
        lead = v.shape[1]
        v = v.reshape(n_sr, 2, lead, 2, 2, ff_rows).transpose(2, 3, 0, 4, 1, 5)
        return v.reshape(lead, FF)

    def exchange(v):
        return lax.all_to_all(v, MEMBERS, split_axis=0, concat_axis=0, tiled=True)

    def full_rows(w):
        w = gather_groups(w)
        x = w.shape[-1]
        w = w.reshape(2, 2, n_sr, 2, rows, x).transpose(0, 2, 1, 3, 4, 5)
        return w.reshape(D, x)

    own_x = pick(inputs, sb)[0]
    own_x = jnp.concatenate([own_x, swap_sb(pick(inputs, 1 - sb)[0])], 0)
    m = 2 * tok
    xg = gather_tokens(own_x).reshape(members * m, D)
    own_dy = pick(cotangent, sb)[0]
    own_dy = jnp.concatenate([own_dy, swap_sb(pick(cotangent, 1 - sb)[0])], 0)
    dyg = gather_tokens(own_dy).reshape(members * m, D)

    my_ids = pick(block_ids, sb)
    ids = jnp.concatenate([my_ids, swap_fl(my_ids)], 0)
    ids = xor_order(ids.reshape(2, 2, n_sr, tok), 1, sb, 2)
    ids = xor_order(ids, 2, sr, n_sr).transpose(0, 2, 1, 3).reshape(2, length)
    sr_of = (jnp.arange(n_sr, dtype=jnp.int32) ^ sr)[:, None, None]
    sb_of = (jnp.arange(2, dtype=jnp.int32) ^ sb)[None, :, None]
    pos = ((sb_of * n_sr + sr_of) * tok + jnp.arange(tok, dtype=jnp.int32)[None, None, :]).reshape(-1)
    frequency = rope_base ** (-2.0 * jnp.arange(ROT // 2).astype(F32) / ROT)
    angles = pos.astype(F32)[:, None] * frequency[None, :]
    cosine, sine = jnp.cos(angles)[:, None, :], jnp.sin(angles)[:, None, :]

    w_qkv = full_rows(exchange(by_member(qkv_weight)))
    my_bias = lax.dynamic_index_in_dim(by_member(bias_qkv), sr * 2 + fl, 0, keepdims=False)
    if natural:
        w_out_own = gather_groups(out_weight).reshape(heads * HD, D)
        w_out = gather_tokens(w_out_own)
    else:
        w_out_all = lax.all_gather(out_weight, EVERY, axis=0, tiled=True)
        w_out = by_member(w_out_all.T.reshape(D, H * HD)).transpose(0, 2, 1)
        w_out_own = pick(w_out, sr * 2 + fl)
        w_out = xor_order(xor_order(w_out.reshape(n_sr, 2, -1, D), 0, sr, n_sr), 1, fl, 2)
        w_out = w_out.transpose(1, 0, 2, 3)
    w_gu = full_rows(
        exchange(jnp.concatenate([ff_by_member(gate_weight), ff_by_member(up_weight)], -1))
    )
    w_gate, w_up = w_gu[:, : 4 * ff_rows], w_gu[:, 4 * ff_rows :]
    w_down = gather_groups(down_weight).reshape(4 * ff_rows, D)

    n1, _ = norm_stats(xg.astype(F32))
    h1 = (n1 * gain1 + bias1).astype(BF16)
    lin = (jnp.dot(h1, w_qkv, preferred_element_type=F32) + my_bias).reshape(2, length, heads, 3, HD)
    kept = []
    outs = []
    for i in range(2):
        q = rotate(lin[i, :, :, 0], cosine, sine, 1.0).astype(BF16)
        k = rotate(lin[i, :, :, 1], cosine, sine, 1.0).astype(BF16)
        v = lin[i, :, :, 2].astype(BF16)
        o, p = attend(q, k, v, ids[i])
        outs.append(o.reshape(length, heads * HD))
        kept.append((q, k, v, p))
    o_own = jnp.concatenate(outs, 0)
    o_all = gather_tokens(o_own)

    o_rel = o_all.reshape(2, n_sr, 2, n_sr, m, heads * HD)
    pieces = []
    for a in range(2):
        row = []
        for b in range(n_sr):
            block = o_rel[a, b]
            row.append(
                jnp.stack([jnp.stack([block[a ^ c, b ^ d] for d in range(n_sr)]) for c in range(2)])
            )
        pieces.append(jnp.stack(row))
    o_rel = jnp.stack(pieces)
    o_mat = o_rel.transpose(2, 3, 4, 0, 1, 5).reshape(members * m, D)
    x2 = xg.astype(F32) + jnp.dot(o_mat, w_out.reshape(D, D), preferred_element_type=F32)

    n2, r2 = norm_stats(x2)
    h2 = (n2 * gain2 + bias2).astype(BF16)
    g = jnp.dot(h2, w_gate, preferred_element_type=F32)
    u = jnp.dot(h2, w_up, preferred_element_type=F32)
    d_act = lax.dot_general(dyg, w_down, (((1,), (1,)), ((), ())), preferred_element_type=F32)
    s = jax.nn.sigmoid(g)
    act = (g * s * u).astype(BF16)
    d_g = (d_act * u * s * (1.0 + g * (1.0 - s))).astype(BF16)
    d_u = (d_act * (g * s)).astype(BF16)
    d_h2 = lax.dot_general(
        d_g, w_gate, (((1,), (1,)), ((), ())), preferred_element_type=F32
    ) + lax.dot_general(d_u, w_up, (((1,), (1,)), ((), ())), preferred_element_type=F32)
    d_h2 = scatter_tokens(d_h2.astype(BF16).reshape(2, n_sr, m, D))
    n2_own, r2_own, x2_own = n2[:m], r2[:m], x2[:m]
    gain2_grad = jnp.sum(d_h2 * n2_own, axis=0)
    bias2_grad = jnp.sum(d_h2, axis=0)
    d_x2 = own_dy.astype(F32) + norm_back(d_h2 * gain2, n2_own, r2_own)
    d_att = gather_tokens(d_x2.astype(BF16)).reshape(members * m, D)

    y = jnp.dot(act, w_down, preferred_element_type=F32).astype(BF16)
    y = x2_own + scatter_tokens(y.reshape(2, n_sr, m, D))

    def give_back(v):
        v = v.astype(BF16)
        other = swap_sb(v[tok:])
        first = jnp.where(sb == 0, v[:tok], other)
        second = jnp.where(sb == 0, other, v[:tok])
        return jnp.stack([first, second])[:, None]

    layer_out = give_back(y)

    d_o = lax.dot_general(d_att, w_out_own, (((1,), (1,)), ((), ())), preferred_element_type=F32)
    d_o = d_o.astype(BF16).reshape(2, length, heads, HD)
    d_lins = []
    for i in range(2):
        dq, dk, dv = attend_back(*kept[i], d_o[i])
        dq = rotate(dq, cosine, sine, -1.0)
        dk = rotate(dk, cosine, sine, -1.0)
        d_lins.append(jnp.stack([dq, dk, dv], 2).astype(BF16).reshape(length, heads * 3 * HD))
    d_lin = jnp.concatenate(d_lins, 0)
    d_h1 = lax.dot_general(d_lin, w_qkv, (((1,), (1,)), ((), ())), preferred_element_type=F32)
    d_h1 = scatter_tokens(d_h1.astype(BF16).reshape(2, n_sr, m, D))
    n1_own, r1_own = norm_stats(own_x.astype(F32))
    gain1_grad = jnp.sum(d_h1 * n1_own, axis=0)
    bias1_grad = jnp.sum(d_h1, axis=0)
    input_grad = give_back(d_x2 + norm_back(d_h1 * gain1, n1_own, r1_own))

    def grad_rows(h, d, width):
        def part(k):
            side = lax.dynamic_index_in_dim(h.reshape(-1, 2, D // 2), sb ^ k, 1, keepdims=False)
            t = lax.dot_general(side, d, (((0,), (0,)), ((), ())), preferred_element_type=F32)
            return t.reshape(n_sr, 2, 2 * rows, width).transpose(1, 0, 2, 3)

        total = scatter_groups(part).reshape(members, rows, width)
        return exchange(total.astype(BF16)).astype(F32)

    def down_part(k):
        side = lax.dynamic_index_in_dim(act.reshape(-1, 2, 2 * ff_rows), sb ^ k, 1, keepdims=False)
        t = lax.dot_general(side, dyg, (((0,), (0,)), ((), ())), preferred_element_type=F32)
        return t.reshape(2, ff_rows, D)

    down_grad = scatter_groups(down_part)
    gu = grad_rows(h2, jnp.concatenate([d_g, d_u], -1), 8 * ff_rows)
    gate_grad = ff_from_members(gu[..., : 4 * ff_rows])
    up_grad = ff_from_members(gu[..., 4 * ff_rows :])
    if natural:

        def out_part(k):
            side = lax.dynamic_index_in_dim(
                o_own.reshape(-1, 2, heads * HD // 2), sb ^ k, 1, keepdims=False
            )
            t = lax.dot_general(side, d_att, (((0,), (0,)), ((), ())), preferred_element_type=F32)
            return t.reshape(2, heads * HD // 4, D)

        out_grad = scatter_groups(out_part)
    else:
        t = lax.dot_general(o_own, d_att, (((0,), (0,)), ((), ())), preferred_element_type=F32)
        spread = jnp.where(
            jnp.arange(members)[:, None, None] == sr * 2 + fl, t[None], jnp.zeros((), F32)
        )
        spread = spread.reshape(H * HD, D)
        out_grad = lax.psum_scatter(spread, EVERY, scatter_dimension=0, tiled=True)
    qkv_grad = from_members(grad_rows(h1, d_lin, heads * 3 * HD))

    bias_term = jnp.sum(d_lin.astype(F32), axis=0)
    bias_term = jnp.where(jnp.arange(members)[:, None] == sr * 2 + fl, bias_term[None], 0.0)
    bias_term = from_members(bias_term)
    gain1_grad, bias1_grad, bias_grad, gain2_grad, bias2_grad = (
        lax.psum_scatter(v, EVERY, scatter_dimension=0, tiled=True)
        for v in (gain1_grad, bias1_grad, bias_term, gain2_grad, bias2_grad)
    )
    return (
        layer_out,
        input_grad,
        gain1_grad,
        bias1_grad,
        qkv_grad,
        bias_grad,
        out_grad,
        gain2_grad,
        bias2_grad,
        gate_grad,
        up_grad,
        down_grad,
    )


def solution(mesh):
    names = dict(mesh.shape)
    n_seq, n_fsdp = names["seq"], names["fsdp"]
    fine = Mesh(mesh.devices.reshape(2, n_seq // 2, 2, n_fsdp // 2), EVERY)
    tokens = P(None, ("fh", "fl"), ("sb", "sr"), None)
    vector = P(EVERY)
    matrix = P(EVERY, None)
    in_specs = (
        tokens,
        tokens,
        P(None, ("fh", "fl"), None),
        vector,
        vector,
        matrix,
        vector,
        matrix,
        vector,
        vector,
        matrix,
        matrix,
        matrix,
    )
    out_specs = (
        tokens,
        tokens,
        vector,
        vector,
        matrix,
        vector,
        matrix,
        vector,
        vector,
        matrix,
        matrix,
        matrix,
    )
    return jax.shard_map(shards, mesh=fine, in_specs=in_specs, out_specs=out_specs, check_vma=False)
```

time: 4520 us -> 828 us (0.18)
  waiting for transfers between devices: 3960 us -> 250 us
  matrix products: 301 us -> 100 us
  local copies, waits for them, and re-layouts: 93.4 us -> 220 us
  starting transfers between devices: 31.4 us -> 89.5 us
  other arithmetic: 25.6 us -> 76.5 us
    reduce_scatter x5 -> x0, waiting for transfers between devices: 3440 us -> none  [the longest x1 976 us: shards(): lax.psum_scatter(term_up, ('seq', 'fsdp'), scatter_dimension=0, tiled=True)]
    all_gather x5 -> x0, waiting for transfers between devices: 466 us -> none  [the longest x1 135 us: fetch_feedforward(): lax.all_gather(weight_up, ('seq', 'fsdp'), axis=0, tiled=True)]
    ppermute x0 -> x80, waiting for transfers between devices: none -> 250 us  [the longest x16 74.9 us: swap_sb(): return lax.ppermute(v, 'sb', SWAP)]
    dot_general x37 -> x28, matrix products: 301 us -> 93 us  [the longest x4 16.8 us: part(): lax.dot_general(side, d, (((0,), (0,)), ((), ())), preferred_element_type...]
    ppermute x0 -> x80, starting transfers between devices: none -> 72.6 us  [the longest x39 24.7 us: swap_sr(): return lax.ppermute(v, 'sr', [(i, i ^ bit) for i in range(n)])]
    reshape x10 -> x26, local copies, waits for them, and re-layouts: 16 us -> 77.6 us  [the longest x4 15.3 us: ff_from_members(): v = v.reshape(n_sr, 2, lead, 2, 2, ff_rows).transpose(2, 3, 0, 4, 1, 5)]
    all_to_all x8 -> x4, waiting for transfers between devices: 51.9 us -> 0.01 us  [exchange(): return lax.all_to_all(v, MEMBERS, split_axis=0, concat_axis=0, tiled=True)]
  transfers between devices with their start and end apart: 18 -> 84, of which waited for: 16 -> 32; matrix products, arithmetic and copies ran while one was open for 7% -> 43% of each run, Pallas kernels for 0% -> 0%
where the time goes in v1:
time: 828 us; the launch traced here: 820 us
  waiting for transfers between devices  250 us (30%)
  local copies, waits for them, and re-layouts  220 us (27%)
  matrix products  100 us (12%)
  starting transfers between devices  89.5 us (11%)
  blocking collectives  79.4 us (10%)
  other arithmetic  76.5 us (9%)
    unnamed x2, blocking collectives  79.4 us
    ppermute x16, waiting for transfers between devices, swap_sb(): return lax.ppermute(v, 'sb', SWAP)  74.9 us
    ppermute x17, waiting for transfers between devices, swap_fl(): return lax.ppermute(v, 'fl', SWAP)  73.6 us
    ppermute x8, waiting for transfers between devices, swap_fh(): return lax.ppermute(v, 'fh', SWAP)  52.9 us
    ppermute x39, waiting for transfers between devices, swap_sr(): return lax.ppermute(v, 'sr', [(i, i ^ bit) for i in range(n)])  48.9 us
    unnamed x247, local copies, waits for them, and re-layouts  45.5 us
    dot_general x5, local copies, waits for them, and re-layouts, part(): lax.dot_general(side, d, (((0,), (0,)), ((), ())), preferred_element_type...  27.7 us
    ppermute x39, starting transfers between devices, swap_sr(): return lax.ppermute(v, 'sr', [(i, i ^ bit) for i in range(n)])  24.7 us
  transfers between devices with their start and end apart: 84, of which 32 were waited for; matrix products, arithmetic and copies ran while one was open for 43% of the time, Pallas kernels for 0%

profile of v1, /device:TPU:0, one launch (start us, length us, event | category | flops | bytes accessed | tf_op | source)
XLA Modules:
  0.0 820.0 jit_solution(14954433420540234589)
XLA Ops:
  24.9 38.9 %all-reduce.11 = (bf16[2048]{0:T(1024)(128)(2,1)S(1)}, bf16[2048]{0:T(1024)(128)(2,1)S(1)}, bf16[6144]{0:T(1024)(128)(2,1)S(1)}, bf16[2048]{0:T(1024)(128)(2,1)S(1)}, bf16[2048]{0:T(1024)(128)(2,1)S(1)}) all-reduce(bf16[2048]{0:T(1024)(128)(2,1)S(1)} %dynamic-update-slice.1, ...), channel_id=1, replica_groups=mesh['sb'=2,'sr'=4,'fh'=2,'fl'=2] {'sb','sr','fh','fl'}, use_global_device_ids=true, to_apply=%add.1 | all-reduce | flops 14336 | bytes 57344
  103.7 10.5 %collective-permute-done.46 = bf16[128,2048]{1,0:T(8,128)(2,1)S(1)} collective-permute-done((bf16[128,2048]{1,0:T(8,128)(2,1)S(1)}, bf16[128,2048]{1,0:T(8,128)(2,1)S(1)}, u32[]{:S(2)}, u32[]{:S(2)}) %collective-permute-start.46) | collective-permute-done | bytes 524320 | tf_op jit(solution)/shard_map/ppermute | solution.py:38
  122.3 10.6 %collective-permute-done.48 = bf16[128,2048]{1,0:T(8,128)(2,1)S(1)} collective-permute-done((bf16[128,2048]{1,0:T(8,128)(2,1)S(1)}, bf16[128,2048]{1,0:T(8,128)(2,1)S(1)}, u32[]{:S(2)}, u32[]{:S(2)}) %collective-permute-start.48) | collective-permute-done | bytes 524320 | tf_op jit(solution)/shard_map/ppermute | solution.py:33
  153.8 16.8 %collective-permute-done.36 = bf16[176,2048]{1,0:T(8,128)(2,1)S(1)} collective-permute-done((bf16[176,2048]{1,0:T(8,128)(2,1)}, bf16[176,2048]{1,0:T(8,128)(2,1)S(1)}, u32[]{:S(2)}, u32[]{:S(2)}) %collective-permute-start.36) | collective-permute-done | bytes 720928 | tf_op jit(solution)/shard_map/ppermute | solution.py:25
  180.7 11.5 %reshape.656 = f32[1024,2,1024]{2,1,0:T(2,128)} reshape(bf16[8,128,2048]{2,1,0:T(8,128)(2,1)} %bitcast_dynamic-update-slice_fusion.31) | data formatting | bytes 12582912 | tf_op jit(solution)/shard_map/convert_element_type | solution.py:302
  229.1 8.8 %collective-permute-done.30 = bf16[128,2048]{1,0:T(8,128)(2,1)S(1)} collective-permute-done((bf16[128,2048]{1,0:T(8,128)(2,1)S(1)}, bf16[128,2048]{1,0:T(8,128)(2,1)S(1)}, u32[]{:S(2)}, u32[]{:S(2)}) %collective-permute-start.30) | collective-permute-done | bytes 524320 | tf_op jit(solution)/shard_map/ppermute | solution.py:38
  250.2 9.0 %collective-permute-done.10 = bf16[8,64,768]{2,1,0:T(8,128)(2,1)S(1)} collective-permute-done((bf16[8,64,768]{2,1,0:T(8,128)(2,1)}, bf16[8,64,768]{2,1,0:T(8,128)(2,1)S(1)}, u32[]{:S(2)}, u32[]{:S(2)}) %collective-permute-start.10) | collective-permute-done | bytes 786464 | tf_op jit(solution)/shard_map/ppermute | solution.py:25
  305.6 11.5 %collective-permute-done.16 = bf16[1024,256]{0,1:T(8,128)(2,1)S(1)} collective-permute-done((bf16[1024,256]{0,1:T(8,128)(2,1)S(1)}, bf16[1024,256]{0,1:T(8,128)(2,1)S(1)}, u32[]{:S(2)}, u32[]{:S(2)}) %collective-permute-start.16) | collective-permute-done | bytes 524320 | tf_op jit(solution)/shard_map/ppermute | solution.py:33
  347.4 7.8 reshape.633
  355.2 13.2 %fusion.102 = (f32[1024]{0:T(1024)S(1)}, f32[1024,2048]{1,0:T(8,128)S(1)}) fusion(bf16[8,128,2048]{2,1,0:T(8,128)(2,1)} %bitcast_dynamic-update-slice_fusion.31, bf16[1024,2048]{1,0:T(8,128)(2,1)} %reshape.633, bf16[2048,2048]{1,0:T(8,128)(2,1)} %bitcast.747), kind=kOutput, calls=%fused_computation.483 | convolution fusion | flops 8596225024 | bytes 25169920 | tf_op jit(solution)/shard_map/dot_general | solution.py:302
  377.4 7.8 reshape.644
  385.2 11.6 %constant_dynamic-slice_fusion.3 = (bf16[1024,1,1024]{2,1,0:T(2,128)(2,1)}, bf16[1024,1,1024]{2,1,0:T(2,128)(2,1)}) fusion(bf16[1024,2,1024]{2,1,0:T(2,128)(2,1)} %reshape.644, s32[]{:T(128)S(6)} %select_n.277, s32[]{:T(128)S(6)} %select_n.336), kind=kLoop, calls=%fused_computation.448 | loop fusion | bytes 8388616 | tf_op jit(solution)/shard_map/jit(dynamic_index_in_dim)/dynamic_slice | solution.py:353
  396.8 10.5 %copy.250 = bf16[1024,1,1024]{0,2,1:T(8,128)(2,1)} copy(bf16[1024,1,1024]{2,1,0:T(2,128)(2,1)} %get-tuple-element.99) | data formatting | bytes 4194304 | tf_op jit(solution)/shard_map/dot_general | solution.py:354
  407.4 9.0 %copy.249 = bf16[1024,1,1024]{0,2,1:T(8,128)(2,1)S(1)} copy(bf16[1024,1,1024]{2,1,0:T(2,128)(2,1)} %get-tuple-element.98) | data formatting | bytes 4194304 | tf_op jit(solution)/shard_map/dot_general | solution.py:354
  464.5 17.4 %collective-permute-done.78 = bf16[2,176,2048]{2,1,0:T(8,128)(2,1)S(1)} collective-permute-done((bf16[2,176,2048]{2,1,0:T(8,128)(2,1)}, bf16[2,176,2048]{2,1,0:T(8,128)(2,1)S(1)}, u32[]{:S(2)}, u32[]{:S(2)}) %collective-permute-start.78) | collective-permute-done | bytes 1441824 | tf_op jit(solution)/shard_map/ppermute | solution.py:25
  490.1 26.1 %collective-permute-done.79 = bf16[176,2048]{1,0:T(8,128)(2,1)S(1)} collective-permute-done((bf16[176,2048]{1,0:T(8,128)(2,1)S(1)}, bf16[176,2048]{1,0:T(8,128)(2,1)S(1)}, u32[]{:S(2)}, u32[]{:S(2)}) %collective-permute-start.79) | collective-permute-done | bytes 720928 | tf_op jit(solution)/shard_map/ppermute | solution.py:29
  521.9 9.2 %collective-permute-done.56 = bf16[2,64,2048]{2,1,0:T(8,128)(2,1)S(1)} collective-permute-done((bf16[2,64,2048]{2,1,0:T(8,128)(2,1)S(1)}, bf16[2,64,2048]{2,1,0:T(8,128)(2,1)S(1)}, u32[]{:S(2)}, u32[]{:S(2)}) %collective-permute-start.56) | collective-permute-done | bytes 524320 | tf_op jit(solution)/shard_map/ppermute | solution.py:33
  533.3 9.8 %collective-permute-done.76 = bf16[2,4,128,1408]{3,2,0,1:T(8,128)(2,1)S(1)} collective-permute-done((bf16[2,4,128,1408]{3,2,0,1:T(8,128)(2,1)}, bf16[2,4,128,1408]{3,2,0,1:T(8,128)(2,1)S(1)}, u32[]{:S(2)}, u32[]{:S(2)}) %collective-permute-start.76) | collective-permute-done | bytes 2883616 | tf_op jit(solution)/shard_map/ppermute | solution.py:25
  561.2 9.6 %collective-permute-done.59 = bf16[128,2048]{1,0:T(8,128)(2,1)S(1)} collective-permute-done((bf16[128,2048]{1,0:T(8,128)(2,1)S(1)}, bf16[128,2048]{1,0:T(8,128)(2,1)S(1)}, u32[]{:S(2)}, u32[]{:S(2)}) %collective-permute-start.59) | collective-permute-done | bytes 524320 | tf_op jit(solution)/shard_map/ppermute | solution.py:38
  572.4 19.1 %collective-permute-done.61 = bf16[128,2048]{1,0:T(8,128)(2,1)S(1)} collective-permute-done((bf16[128,2048]{1,0:T(8,128)(2,1)S(1)}, bf16[128,2048]{1,0:T(8,128)(2,1)S(1)}, u32[]{:S(2)}, u32[]{:S(2)}) %collective-permute-start.61) | collective-permute-done | bytes 524320 | tf_op jit(solution)/shard_map/ppermute | solution.py:33
  644.6 7.4 collective-permute-done.74
  676.5 8.6 %collective-permute-done.72 = bf16[2,4,128,768]{3,2,0,1:T(8,128)(2,1)} collective-permute-done((bf16[2,4,128,768]{3,2,0,1:T(8,128)(2,1)}, bf16[2,4,128,768]{3,2,0,1:T(8,128)(2,1)}, u32[]{:S(2)}, u32[]{:S(2)}) %collective-permute-start.72) | collective-permute-done | bytes 1572896 | tf_op jit(solution)/shard_map/ppermute | solution.py:25
  703.1 22.5 %collective-permute-done.73 = bf16[4,128,768]{2,1,0:T(8,128)(2,1)S(1)} collective-permute-done((bf16[4,128,768]{2,1,0:T(8,128)(2,1)S(1)}, bf16[4,128,768]{2,1,0:T(8,128)(2,1)S(1)}, u32[]{:S(2)}, u32[]{:S(2)}) %collective-permute-start.73) | collective-permute-done | bytes 786464 | tf_op jit(solution)/shard_map/ppermute | solution.py:29
  764.6 40.5 %all-reduce.10 = (f32[2048]{0:T(1024)S(1)}, f32[2048]{0:T(1024)S(1)}, f32[6144]{0:T(1024)S(1)}, f32[2048]{0:T(1024)S(1)}, f32[2048]{0:T(1024)S(1)}) all-reduce(f32[2048]{0:T(1024)S(1)} %copy-done.70, f32[2048]{0:T(1024)S(1)} %reduce_sum.204, ...), channel_id=2, replica_groups=mesh['sb'=2,'sr'=4,'fh'=2,'fl'=2] {'sb','sr','fh','fl'}, use_global_device_ids=true, to_apply=%region_17.18.clone | all-reduce | flops 14336 | bytes 114688
  (661 shorter events, 468.7 us)
Async XLA Ops:
  0.6 87.4 %collective-permute-start.21 = (bf16[64,2048]{1,0:T(8,128)(2,1)}, bf16[64,2048]{1,0:T(8,128)(2,1)}, u32[]{:S(2)}, u32[]{:S(2)}) collective-permute-start(bf16[64,2048]{1,0:T(8,128)(2,1)} %param.20), channel_id=1, source_target_pairs={{0,2},{2,0},{1,3},{3,1},{4,6},{6,4},{5,7},{7,5},{8,10},{10,8},{9,1... | collective-permute-start | bytes 786440 | tf_op jit(solution)/shard_map/ppermute | solution.py:29
  4.7 87.8 %collective-permute-start.23 = (bf16[64,2048]{1,0:T(8,128)(2,1)}, bf16[64,2048]{1,0:T(8,128)(2,1)}, u32[]{:S(2)}, u32[]{:S(2)}) collective-permute-start(bf16[64,2048]{1,0:T(8,128)(2,1)} %param.20), channel_id=1, source_target_pairs={{0,16},{16,0},{1,17},{17,1},{2,18},{18,2},{3,19},{19,3},{4,20},{20... | collective-permute-start | bytes 786440 | tf_op jit(solution)/shard_map/ppermute | solution.py:25
  8.1 78.5 %collective-permute-start = (bf16[64,2048]{1,0:T(8,128)(2,1)}, bf16[64,2048]{1,0:T(8,128)(2,1)S(1)}, u32[]{:S(2)}, u32[]{:S(2)}) collective-permute-start(bf16[64,2048]{1,0:T(8,128)(2,1)} %get-tuple-element.233), channel_id=1, source_target_pairs={{0,16},{16,0},{1,17},{17,1},{2,18},{18,2},{3,19},{19,3},{4,20},{20... | collective-permute-start | bytes 786440 | tf_op jit(solution)/shard_map/ppermute | solution.py:25
  14.6 159.6 %all-to-all-start = ((bf16[8,64,768]{2,1,0:T(8,128)(2,1)}), bf16[8,64,768]{2,1,0:T(8,128)(2,1)}, u32[]{:S(2)}, u32[]{:S(2)}) async-start(bf16[8,64,768]{2,1,0:T(8,128)(2,1)} %reshape.624), calls=%async_computation | async-start | bytes 1572864 | tf_op jit(solution)/shard_map/all_to_all | solution.py:231
  18.9 63.4 %collective-permute-start.12 = (s32[1,512]{1,0:T(1,128)S(1)}, s32[1,512]{1,0:T(1,128)S(1)}, u32[]{:S(2)}, u32[]{:S(2)}) collective-permute-start(s32[1,512]{1,0:T(1,128)S(1)} %get-tuple-element.252), channel_id=1, source_target_pairs={{0,1},{1,0},{2,3},{3,2},{4,5},{5,4},{6,7},{7,6},{8,9},{9,8},{10,11... | collective-permute-start | bytes 6152 | tf_op jit(solution)/shard_map/ppermute | solution.py:33
  21.6 68.8 %collective-permute-start.44 = (bf16[64,2048]{1,0:T(8,128)(2,1)}, bf16[64,2048]{1,0:T(8,128)(2,1)S(1)}, u32[]{:S(2)}, u32[]{:S(2)}) collective-permute-start(bf16[64,2048]{1,0:T(8,128)(2,1)} %get-tuple-element.167), channel_id=1, source_target_pairs={{0,16},{16,0},{1,17},{17,1},{2,18},{18,2},{3,19},{19,3},{4,20},{20... | collective-permute-start | bytes 786440 | tf_op jit(solution)/shard_map/ppermute | solution.py:25
  82.2 68.3 %collective-permute-start.35 = (bf16[176,2048]{1,0:T(8,128)(2,1)}, bf16[176,2048]{1,0:T(8,128)(2,1)}, u32[]{:S(2)}, u32[]{:S(2)}) collective-permute-start(bf16[176,2048]{1,0:T(8,128)(2,1)} %param.25), channel_id=1, source_target_pairs={{0,2},{2,0},{1,3},{3,1},{4,6},{6,4},{5,7},{7,5},{8,10},{10,8},{9,1... | collective-permute-start | bytes 2162696 | tf_op jit(solution)/shard_map/ppermute | solution.py:29
  143.9 66.7 %collective-permute-start.24 = (bf16[256,2048]{1,0:T(8,128)(2,1)S(1)}, bf16[256,2048]{1,0:T(8,128)(2,1)S(1)}, u32[]{:S(2)}, u32[]{:S(2)}) collective-permute-start(bf16[256,2048]{1,0:T(8,128)(2,1)S(1)} %bitcast.711), channel_id=1, source_target_pairs={{0,4},{4,0},{8,12},{12,8},{1,5},{5,1},{9,13},{13,9},{2,6},{6,2},{1... | collective-permute-start | bytes 3145736 | tf_op jit(solution)/shard_map/ppermute | solution.py:38
  144.9 53.7 %collective-permute-start.25 = (bf16[256,2048]{1,0:T(8,128)(2,1)S(1)}, bf16[256,2048]{1,0:T(8,128)(2,1)}, u32[]{:S(2)}, u32[]{:S(2)}) collective-permute-start(bf16[256,2048]{1,0:T(8,128)(2,1)S(1)} %bitcast.712), channel_id=1, source_target_pairs={{0,8},{4,12},{8,0},{12,4},{1,9},{5,13},{9,1},{13,5},{2,10},{6,14},... | collective-permute-start | bytes 3145736 | tf_op jit(solution)/shard_map/ppermute | solution.py:38
  150.6 71.6 %collective-permute-start.27 = (bf16[256,2048]{1,0:T(8,128)(2,1)S(1)}, bf16[256,2048]{1,0:T(8,128)(2,1)}, u32[]{:S(2)}, u32[]{:S(2)}) collective-permute-start(bf16[256,2048]{1,0:T(8,128)(2,1)S(1)} %bitcast.713), channel_id=1, source_target_pairs={{0,1},{1,0},{2,3},{3,2},{4,5},{5,4},{6,7},{7,6},{8,9},{9,8},{10,11... | collective-permute-start | bytes 3145736 | tf_op jit(solution)/shard_map/ppermute | solution.py:33
  170.7 53.1 %collective-permute-start.52 = (bf16[128,2048]{1,0:T(8,128)(2,1)}, bf16[128,2048]{1,0:T(8,128)(2,1)}, u32[]{:S(2)}, u32[]{:S(2)}) collective-permute-start(bf16[128,2048]{1,0:T(8,128)(2,1)} %constant_dynamic-update-slice_fusion.9), channel_id=1, source_target_pairs={{0,4},{4,0},{8,12},{12,8},{1,5},{5,1},{9,13},{13,9},{2,6},{6,2},{1... | collective-permute-start | bytes 1572872 | tf_op jit(solution)/shard_map/ppermute | solution.py:38
  174.2 66.1 %all-to-all-start.1 = ((bf16[8,64,1408]{2,1,0:T(8,128)(2,1)}), bf16[8,64,1408]{2,1,0:T(8,128)(2,1)}, u32[]{:S(2)}, u32[]{:S(2)}) async-start(bf16[8,64,1408]{2,1,0:T(8,128)(2,1)} %pad_maximum_fusion.2), calls=%async_computation.1 | async-start | bytes 2883584 | tf_op jit(solution)/shard_map/all_to_all | solution.py:231
  178.7 60.0 %collective-permute-start.9 = (bf16[8,64,768]{2,1,0:T(8,128)(2,1)}, bf16[8,64,768]{2,1,0:T(8,128)(2,1)}, u32[]{:S(2)}, u32[]{:S(2)}) collective-permute-start(bf16[8,64,768]{2,1,0:T(8,128)(2,1)} %all-to-all-done), channel_id=1, source_target_pairs={{0,2},{2,0},{1,3},{3,1},{4,6},{6,4},{5,7},{7,5},{8,10},{10,8},{9,1... | collective-permute-start | bytes 2359304 | tf_op jit(solution)/shard_map/ppermute | solution.py:29
  238.7 56.0 %collective-permute-start.31 = (bf16[256,2048]{1,0:T(8,128)(2,1)}, bf16[256,2048]{1,0:T(8,128)(2,1)}, u32[]{:S(2)}, u32[]{:S(2)}) collective-permute-start(bf16[256,2048]{1,0:T(8,128)(2,1)} %constant_dynamic-update-slice_fusion.6), channel_id=1, source_target_pairs={{0,4},{4,0},{8,12},{12,8},{1,5},{5,1},{9,13},{13,9},{2,6},{6,2},{1... | collective-permute-start | bytes 3145736 | tf_op jit(solution)/shard_map/ppermute | solution.py:38
  240.3 85.2 %collective-permute-start.32 = (bf16[8,64,1408]{2,1,0:T(8,128)(2,1)}, bf16[8,64,1408]{2,1,0:T(8,128)(2,1)}, u32[]{:S(2)}, u32[]{:S(2)}) collective-permute-start(bf16[8,64,1408]{2,1,0:T(8,128)(2,1)} %all-to-all-done.1), channel_id=1, source_target_pairs={{0,2},{2,0},{1,3},{3,1},{4,6},{6,4},{5,7},{7,5},{8,10},{10,8},{9,1... | collective-permute-start | bytes 4325384 | tf_op jit(solution)/shard_map/ppermute | solution.py:29
  294.7 121.7 %collective-permute-start.34 = (bf16[8,64,1408]{2,1,0:T(8,128)(2,1)}, bf16[8,64,1408]{2,1,0:T(8,128)(2,1)S(1)}, u32[]{:S(2)}, u32[]{:S(2)}) collective-permute-start(bf16[8,64,1408]{2,1,0:T(8,128)(2,1)} %all-to-all-done.1), channel_id=1, source_target_pairs={{0,16},{16,0},{1,17},{17,1},{2,18},{18,2},{3,19},{19,3},{4,20},{20... | collective-permute-start | bytes 4325384 | tf_op jit(solution)/shard_map/ppermute | solution.py:25
  325.4 90.9 %collective-permute-start.33 = (bf16[8,64,1408]{2,1,0:T(8,128)(2,1)}, bf16[8,64,1408]{2,1,0:T(8,128)(2,1)}, u32[]{:S(2)}, u32[]{:S(2)}) collective-permute-start(bf16[8,64,1408]{2,1,0:T(8,128)(2,1)} %collective-permute-done.32), channel_id=1, source_target_pairs={{0,16},{16,0},{1,17},{17,1},{2,18},{18,2},{3,19},{19,3},{4,20},{20... | collective-permute-start | bytes 4325384 | tf_op jit(solution)/shard_map/ppermute | solution.py:25
  438.3 45.5 %collective-permute-start.38 = (bf16[2,2,128,2048]{3,2,0,1:T(8,128)(2,1)S(1)}, bf16[2,2,128,2048]{3,2,0,1:T(8,128)(2,1)S(1)}, u32[]{:S(2)}, u32[]{:S(2)}) collective-permute-start(bf16[2,2,128,2048]{3,2,0,1:T(8,128)(2,1)S(1)} %bitcast.736), channel_id=1, source_target_pairs={{0,4},{4,0},{8,12},{12,8},{1,5},{5,1},{9,13},{13,9},{2,6},{6,2},{1... | collective-permute-start | bytes 6291464 | tf_op jit(solution)/shard_map/ppermute | solution.py:38
  463.9 79.2 %collective-permute-start.76 = (bf16[2,4,128,1408]{3,2,0,1:T(8,128)(2,1)}, bf16[2,4,128,1408]{3,2,0,1:T(8,128)(2,1)S(1)}, u32[]{:S(2)}, u32[]{:S(2)}) collective-permute-start(bf16[2,4,128,1408]{3,2,0,1:T(8,128)(2,1)} %fusion.6), channel_id=1, source_target_pairs={{0,16},{16,0},{1,17},{17,1},{2,18},{18,2},{3,19},{19,3},{4,20},{20... | collective-permute-start | bytes 8650760 | tf_op jit(solution)/shard_map/ppermute | solution.py:25
  548.0 110.4 %collective-permute-start.77 = (bf16[4,128,1408]{2,1,0:T(8,128)(2,1)}, bf16[4,128,1408]{2,1,0:T(8,128)(2,1)}, u32[]{:S(2)}, u32[]{:S(2)}) collective-permute-start(bf16[4,128,1408]{2,1,0:T(8,128)(2,1)} %fusion.30), channel_id=1, source_target_pairs={{0,2},{2,0},{1,3},{3,1},{4,6},{6,4},{5,7},{7,5},{8,10},{10,8},{9,1... | collective-permute-start | bytes 4325384 | tf_op jit(solution)/shard_map/ppermute | solution.py:29
  644.1 41.0 %collective-permute-start.72 = (bf16[2,4,128,768]{3,2,0,1:T(8,128)(2,1)}, bf16[2,4,128,768]{3,2,0,1:T(8,128)(2,1)}, u32[]{:S(2)}, u32[]{:S(2)}) collective-permute-start(bf16[2,4,128,768]{3,2,0,1:T(8,128)(2,1)} %fusion.27), channel_id=1, source_target_pairs={{0,16},{16,0},{1,17},{17,1},{2,18},{18,2},{3,19},{19,3},{4,20},{20... | collective-permute-start | bytes 4718600 | tf_op jit(solution)/shard_map/ppermute | solution.py:25
  662.1 68.0 %all-to-all-start.3 = ((bf16[8,64,1408]{2,1,0:T(8,128)(2,1)}), bf16[8,64,1408]{2,1,0:T(8,128)(2,1)S(1)}, u32[]{:S(2)}, u32[]{:S(2)}) async-start(bf16[8,64,1408]{2,1,0:T(8,128)(2,1)} %bitcast.702), calls=%async_computation.3 | async-start | bytes 2883584 | tf_op jit(solution)/shard_map/all_to_all | solution.py:231
  730.1 78.8 %all-to-all-start.2 = ((bf16[8,64,768]{2,1,0:T(8,128)(2,1)}), bf16[8,64,768]{2,1,0:T(8,128)(2,1)}, u32[]{:S(2)}, u32[]{:S(2)}) async-start(bf16[8,64,768]{2,1,0:T(8,128)(2,1)} %bitcast.723), calls=%async_computation.2 | async-start | bytes 1572864 | tf_op jit(solution)/shard_map/all_to_all | solution.py:231
  736.5 71.6 %collective-permute-start.71 = (bf16[64,2048]{1,0:T(8,128)(2,1)S(1)}, bf16[64,2048]{1,0:T(8,128)(2,1)S(1)}, u32[]{:S(2)}, u32[]{:S(2)}) collective-permute-start(bf16[64,2048]{1,0:T(8,128)(2,1)S(1)} %slice.804), channel_id=1, source_target_pairs={{0,16},{16,0},{1,17},{17,1},{2,18},{18,2},{3,19},{19,3},{4,20},{20... | collective-permute-start | bytes 786440 | tf_op jit(solution)/shard_map/ppermute | solution.py:25
  (157 other events, 2482.1 us)

commit v2 on v1

v2 whole, which is shorter than its diff:
```python
import functools

import jax
import jax.numpy as jnp
import numpy as np
from jax import lax
from jax.experimental import pallas as pl
from jax.experimental.pallas import tpu as pltpu
from jax.sharding import Mesh
from jax.sharding import PartitionSpec as P

H = 32
HD = 64
ROT = 16

eps_norm = 1e-05
rope_base = 10000.0
masked_score = -1e30

F32 = jnp.float32
BF16 = jnp.bfloat16

SWAP = [(0, 1), (1, 0)]
EVERY = ("sb", "sx", "c", "fh", "fl")
MEMBERS = ("sx", "c", "fl")
QUAD = ("fl", "sx")
ANY = pl.BlockSpec(memory_space=pl.ANY)
SMEM = pl.BlockSpec(memory_space=pltpu.SMEM)
VMEM = pl.BlockSpec(memory_space=pltpu.VMEM)
NT = (((1,), (1,)), ((), ()))
TN = (((0,), (0,)), ((), ()))
LIMIT = 60 * 1024 * 1024


def params():
    return pltpu.CompilerParams(vmem_limit_bytes=LIMIT)


def cost(microseconds):
    return pl.CostEstimate(flops=int(microseconds * 1e9), bytes_accessed=1024, transcendentals=0)


def dot(a, b, dims=(((1,), (0,)), ((), ()))):
    return lax.dot_general(a, b, dims, preferred_element_type=F32)


def swap_sb(v):
    return lax.ppermute(v, "sb", SWAP)


def swap_fh(v):
    return lax.ppermute(v, "fh", SWAP)


def swap_fl(v):
    return lax.ppermute(v, "fl", SWAP)


def swap_c(v):
    return lax.ppermute(v, "c", SWAP)


def over_quad(v):
    return lax.all_to_all(v, QUAD, split_axis=0, concat_axis=0, tiled=True)


class Live(dict):
    def __getattr__(self, name):
        return self[name]

    def done(self, **new):
        self.update(new)
        self.update(lax.optimization_barrier(dict(self)))

    def drop(self, *names):
        for name in names:
            del self[name]


def normalize(values):
    average = jnp.mean(values, axis=-1, keepdims=True)
    centered = values - average
    inv_std = lax.rsqrt(jnp.mean(centered * centered, axis=-1, keepdims=True) + eps_norm)
    return centered * inv_std, inv_std


def normalize_back(grad_normed, normed, inv_std):
    first_mean = jnp.mean(grad_normed, axis=-1, keepdims=True)
    second_mean = jnp.mean(grad_normed * normed, axis=-1, keepdims=True)
    return inv_std * (grad_normed - first_mean - normed * second_mean)


def in_order(pieces, sb, fh):
    w, z, y, yz = pieces
    a, b = jnp.where(fh == 1, z, w), jnp.where(fh == 1, w, z)
    c, d = jnp.where(fh == 1, yz, y), jnp.where(fh == 1, y, yz)
    first = jnp.stack([jnp.where(sb == 1, c, a), jnp.where(sb == 1, d, b)])
    second = jnp.stack([jnp.where(sb == 1, a, c), jnp.where(sb == 1, b, d)])
    return jnp.stack([first, second])


def flip_if(bit, v, axis):
    return jnp.where(bit == 1, lax.rev(v, (axis,)), v)


def xor_order(v, axis, index, n):
    shape = v.shape
    bit = 1
    while bit < n:
        r = v.reshape(shape[:axis] + (n // (2 * bit), 2, bit) + shape[axis + 1 :])
        v = flip_if((index // bit) % 2, r, axis + 1).reshape(shape)
        bit *= 2
    return v


def load_groups(sc, pieces, places, buf, sems):
    copies = []
    rows = buf.shape[4]
    for n, (piece, (k, r)) in enumerate(zip(pieces, places)):
        where = buf.at[sc[0] ^ (k // 2), pl.ds(r, piece.shape[0]), sc[1] ^ (k % 2)]
        copies.append(pltpu.make_async_copy(piece.at[:, :, pl.ds(0, rows)], where, sems.at[n]))
    for c in copies:
        c.start()
    return copies


def load_down(sc, pieces, places, buf, sems):
    copies = []
    for n, (piece, (k, r)) in enumerate(zip(pieces, places)):
        where = buf
        if len(places) > 1:
            where = buf.at[sc[0] ^ (k // 2), sc[1] ^ (k % 2), pl.ds(r, piece.shape[0])]
        copies.append(pltpu.make_async_copy(piece, where, sems.at[n]))
    for c in copies:
        c.start()
    return copies


class Rows:
    def __init__(self, mine, other):
        self.arrays = [mine, other]
        self.N, self.D = 2 * mine.shape[0], mine.shape[1]

    def scratch(self):
        return [pltpu.VMEM((self.N, self.D), BF16), pltpu.SemaphoreType.DMA((4,))]

    def load(self, refs, buf, sems):
        n = self.N // 4
        copies = [
            pltpu.make_async_copy(
                refs[k].at[pl.ds(f * n, n)], buf.at[pl.ds((2 * f + k) * n, n)], sems.at[2 * f + k]
            )
            for f in range(2)
            for k in range(2)
        ]
        for c in copies:
            c.start()
        return copies


def sides(nb):
    def keep(i):
        f, k, b = i // (2 * nb), lax.rem(i // nb, 2), lax.rem(i, nb)
        return f * nb + jnp.where(k == 0, b, nb - 1)

    def send(i):
        f, k, b = i // (2 * nb), lax.rem(i // nb, 2), lax.rem(i, nb)
        return f * nb + jnp.where(k == 0, 0, b)

    return keep, send


def columns_kernel(plan, n_in, *refs):
    ins, out = refs[:n_in], refs[-1]
    rows = ins[0].shape[0]
    for t, ranges in enumerate(plan):
        out[t, :rows] = jnp.concatenate([ins[i][:, a : a + n] for i, a, n in ranges], axis=-1)
        if len(refs) == n_in + 2:
            out[t, rows:] = refs[n_in][...]


def columns(arrays, plan, extra=None):
    width = sum(n for _, _, n in plan[0])
    more = [] if extra is None else [extra]
    rows = sum(v.shape[0] for v in [arrays[0]] + more)
    return pl.pallas_call(
        functools.partial(columns_kernel, plan, len(arrays)),
        out_shape=jax.ShapeDtypeStruct((len(plan), rows, width), arrays[0].dtype),
        in_specs=[VMEM] * (len(arrays) + len(more)),
        out_specs=VMEM,
        compiler_params=params(),
        cost_estimate=cost(3),
    )(*arrays, *more)


def uncolumns_kernel(plan, *refs):
    ins, out = refs[:-1], refs[-1]
    width = ins[0].shape[2]
    if True:
        at, group, size = 0, [], 0
        for t, b, n in plan:
            group.append(ins[b // width][t, :, b % width : b % width + n].astype(F32))
            size += n
            if size % 128 == 0:
                out[:, at : at + size] = jnp.concatenate(group, axis=-1)
                at, group, size = at + size, [], 0
        if group:
            out[:, at : at + size] = jnp.concatenate(group, axis=-1)


def uncolumns(arrays, plan):
    rows = arrays[0].shape[1]
    return pl.pallas_call(
        functools.partial(uncolumns_kernel, plan),
        out_shape=jax.ShapeDtypeStruct((rows, sum(n for _, _, n in plan)), F32),
        in_specs=[VMEM] * len(arrays),
        out_specs=VMEM,
        compiler_params=params(),
        cost_estimate=cost(3),
    )(*arrays)


def turn(v, c_ref_value, sa, sb_, direction):
    width = v.shape[1]
    back = pltpu.roll(v, ROT // 2, 1)
    front = pltpu.roll(v, width - ROT // 2, 1)
    return v * c_ref_value + direction * (back * sa + front * sb_)


def attention_kernel(dims, places, x_rows, sc, gain, bias, bias_q, tables, id_row, id_col, w_out, x0, x1, *refs):
    heads, length, block, D = dims
    w_refs, (h1, q, k, v, o, lse, keep, send, w, sems, x_buf, x_sems) = refs[: len(places)], refs[len(places) :]
    wide = heads * HD
    per = length // block
    i = pl.program_id(0)

    @pl.when(i == 0)
    def _():
        copies = x_rows.load((x0, x1), x_buf, x_sems)
        for c in load_groups(sc, w_refs, places, w, sems) + copies:
            c.wait()

    rows = pl.ds(pl.multiple_of(i * block, block), block)
    normed, _ = normalize(x_buf[rows, :].astype(F32))
    h = (normed * gain[...] + bias[...]).astype(BF16)
    h1[...] = h
    lin = dot(h, w[...].reshape(D, 3 * wide)) + bias_q[...]
    qk = turn(lin[:, : 2 * wide], tables[0], tables[1], tables[2], 1.0)
    q[rows, :] = qk[:, :wide].astype(BF16)
    k[rows, :] = qk[:, wide:].astype(BF16)
    v[rows, :] = lin[:, 2 * wide :].astype(BF16)

    @pl.when(lax.rem(i, per) == per - 1)
    def _():
        s = i // per
        start = pl.multiple_of(s * length, length)
        step = min(512, length)
        for r in range(length // step):
            part = pl.ds(pl.multiple_of(start + r * step, step), step)
            allowed = id_col[part, 0:1] >= id_row[pl.ds(s, 1), :]
            for hd in range(heads):
                lanes = slice(hd * HD, (hd + 1) * HD)
                kh = k[pl.ds(start, length), lanes]
                vh = v[pl.ds(start, length), lanes]
                score = dot(q[part, lanes], kh, NT) * (HD**-0.5)
                score = jnp.where(allowed, score, masked_score)
                peak = jnp.max(score, axis=-1, keepdims=True)
                e = jnp.exp(score - peak)
                total = jnp.sum(e, axis=-1, keepdims=True)
                p = (e * (1.0 / total)).astype(BF16)
                o[part, lanes] = dot(p, vh).astype(BF16)
                lse[part, hd : hd + 1] = peak + jnp.log(total)
        for side, out in enumerate((keep, send)):
            for b in range(per // 2):
                part = pl.ds(pl.multiple_of(start + (side * (per // 2) + b) * block, block), block)
                out[0, b * block : (b + 1) * block] = dot(o[part, :], w_out[...]).astype(BF16)


def attention(sc, x_rows, gain, bias, bias_q, tables, id_row, id_col, w_out, weight, heads, rows):
    N, D = x_rows.N, x_rows.D
    length = N // 2
    block = 256
    per = length // block
    wide = heads * HD
    n_sr, _, _, f = weight[0][0].shape
    places = [p[1:] for p in weight]
    whole = lambda shape: pl.BlockSpec(shape, lambda i, sc: (0,) * len(shape))
    side = pl.BlockSpec((1, length // 2, D), lambda i, sc: (i // per, 0, 0))
    spec = pltpu.PrefetchScalarGridSpec(
        num_scalar_prefetch=1,
        grid=(N // block,),
        in_specs=[
            whole((1, D)),
            whole((1, D)),
            whole((1, 3 * wide)),
            pl.BlockSpec((3, block, 2 * wide), lambda i, sc: (0, lax.rem(i, per), 0)),
            whole((2, length)),
            whole((N, 1)),
            whole((wide, D)),
            ANY,
            ANY,
        ]
        + [ANY] * len(places),
        out_specs=[pl.BlockSpec((block, D), lambda i, sc: (i, 0))]
        + [whole((N, wide))] * 4
        + [whole((N, heads)), side, side],
        scratch_shapes=[
            pltpu.VMEM((2, n_sr, 2, 2, rows, f), BF16),
            pltpu.SemaphoreType.DMA((len(places),)),
        ]
        + x_rows.scratch(),
    )
    return pl.pallas_call(
        functools.partial(attention_kernel, (heads, length, block, D), places, x_rows),
        grid_spec=spec,
        out_shape=[jax.ShapeDtypeStruct((N, D), BF16)]
        + [jax.ShapeDtypeStruct((N, wide), BF16)] * 4
        + [jax.ShapeDtypeStruct((N, heads), F32)]
        + [jax.ShapeDtypeStruct((2, length // 2, D), BF16)] * 2,
        compiler_params=params(),
        cost_estimate=cost(25),
    )(sc, gain, bias, bias_q, tables, id_row, id_col, w_out, *x_rows.arrays, *[p[0] for p in weight])


def ffn_kernel(dims, h_rows, dy_rows, sc, h0, h1, dy0, dy1, *refs):
    g_list, d_list, block, nb, D, ff = dims
    g_refs, refs = refs[: len(g_list)], refs[len(g_list) :]
    d_refs, refs = refs[: len(d_list)], refs[len(d_list) :]
    h2, act, d_gu, keep, send, g_buf, d_buf, sem_g, sem_d, h_buf, h_sems, dy_buf, dy_sems = refs
    i = pl.program_id(0)
    rows = pl.ds(pl.multiple_of(i * block, block), block)
    copies = []

    @pl.when(i == 0)
    def _():
        first = h_rows.load((h0, h1), h_buf, h_sems) + load_groups(sc, g_refs, g_list, g_buf, sem_g)
        second = dy_rows.load((dy0, dy1), dy_buf, dy_sems) + load_down(sc, d_refs, d_list, d_buf, sem_d)
        for c in first + second:
            c.wait()

    h = h_buf[rows, :]
    h2[...] = h
    w_gu = g_buf[...].reshape(D, 2 * ff)
    gu = dot(h, w_gu)
    g, u = gu[:, :ff], gu[:, ff:]
    s = jax.nn.sigmoid(g)
    silu = g * s
    act[...] = (silu * u).astype(BF16)
    d_act = dot(dy_buf[rows, :], d_buf[...].reshape(ff, D), NT)
    d_g = (d_act * u * s * (1.0 + g * (1.0 - s))).astype(BF16)
    d_u = (d_act * silu).astype(BF16)
    d = jnp.concatenate([d_g, d_u], axis=-1)
    d_gu[...] = d
    d_h = dot(d, w_gu, NT).astype(BF16)
    side = lax.rem(i // nb, 2)

    @pl.when(side == 0)
    def _():
        keep[...] = d_h

    @pl.when(side == 1)
    def _():
        send[...] = d_h


def ffn(sc, h_rows, dy_rows, gu, down, down_places, rows_):
    N, D = h_rows.N, h_rows.D
    block = 256
    nb = N // 4 // block
    n_sr, _, _, two_ff = gu[0][0].shape
    ff = two_ff // 2
    rows = lambda width: pl.BlockSpec((block, width), lambda i, sc: (i, 0))
    d_shape = (2, 2, ff // 4, D) if len(down) > 1 else (ff, D)
    keep, send = sides(nb)
    spec = pltpu.PrefetchScalarGridSpec(
        num_scalar_prefetch=1,
        grid=(N // block,),
        in_specs=[ANY] * (4 + len(gu) + len(down)),
        out_specs=[
            rows(D),
            rows(ff),
            rows(2 * ff),
            pl.BlockSpec((block, D), lambda i, sc: (keep(i), 0)),
            pl.BlockSpec((block, D), lambda i, sc: (send(i), 0)),
        ],
        scratch_shapes=[
            pltpu.VMEM((2, n_sr, 2, 2, rows_, two_ff), BF16),
            pltpu.VMEM(d_shape, BF16),
            pltpu.SemaphoreType.DMA((len(gu),)),
            pltpu.SemaphoreType.DMA((len(down),)),
        ]
        + h_rows.scratch()
        + dy_rows.scratch(),
    )
    dims = ([p[1:] for p in gu], down_places, block, nb, D, ff)
    return pl.pallas_call(
        functools.partial(ffn_kernel, dims, h_rows, dy_rows),
        grid_spec=spec,
        out_shape=[
            jax.ShapeDtypeStruct((N, D), BF16),
            jax.ShapeDtypeStruct((N, ff), BF16),
            jax.ShapeDtypeStruct((N, 2 * ff), BF16),
            jax.ShapeDtypeStruct((N // 2, D), BF16),
            jax.ShapeDtypeStruct((N // 2, D), BF16),
        ],
        compiler_params=params(),
        cost_estimate=cost(30),
    )(sc, *h_rows.arrays, *dy_rows.arrays, *[p[0] for p in gu], *down)


def down_kernel(d_list, nb, ff, D, sc, act, *refs):
    n_d = len(d_list)
    d_refs, (keep, send, d_buf, sem) = refs[:n_d], refs[n_d:]
    i = pl.program_id(0)

    @pl.when(i == 0)
    def _():
        for c in load_down(sc, d_refs, d_list, d_buf, sem):
            c.wait()

    y = dot(act[...], d_buf[...].reshape(ff, D)).astype(BF16)
    side = lax.rem(i // nb, 2)

    @pl.when(side == 0)
    def _():
        keep[...] = y

    @pl.when(side == 1)
    def _():
        send[...] = y


def down_product(sc, act, down, places):
    N, ff = act.shape
    D = down[0].shape[-1]
    block = 256
    nb = N // 4 // block
    d_shape = (2, 2, ff // 4, D) if len(down) > 1 else (ff, D)
    keep, send = sides(nb)
    spec = pltpu.PrefetchScalarGridSpec(
        num_scalar_prefetch=1,
        grid=(N // block,),
        in_specs=[pl.BlockSpec((block, ff), lambda i, sc: (i, 0))] + [ANY] * len(down),
        out_specs=[
            pl.BlockSpec((block, D), lambda i, sc: (keep(i), 0)),
            pl.BlockSpec((block, D), lambda i, sc: (send(i), 0)),
        ],
        scratch_shapes=[pltpu.VMEM(d_shape, BF16), pltpu.SemaphoreType.DMA((len(down),))],
    )
    return pl.pallas_call(
        functools.partial(down_kernel, places, nb, ff, D),
        grid_spec=spec,
        out_shape=[jax.ShapeDtypeStruct((N // 2, D), BF16)] * 2,
        compiler_params=params(),
        cost_estimate=cost(9),
    )(sc, act, *down)


def attention_back_kernel(dims, d_rows, sc, tables, id_row, id_col, q, k, v, lse, w_out, d0, d1, *refs):
    heads, length, N, D, w_list = dims
    w_refs, refs = refs[: len(w_list)], refs[len(w_list) :]
    d_lin, bias_grad, keep, send, w, d_o, d_qk, sem_w, d_att, sem_d = refs
    wide = heads * HD
    copies = d_rows.load((d0, d1), d_att, sem_d)
    loads = load_groups(sc, w_refs, w_list, w, sem_w)
    for c in copies:
        c.wait()
    step = min(512, length)
    scale = HD**-0.5
    bias_grad[...] = jnp.zeros_like(bias_grad)
    for s in range(2):
        start = s * length
        for r in range(length // step):
            at = pl.ds(start + r * step, step)
            d_o[pl.ds(r * step, step), :] = dot(d_att[at, :], w_out[...], NT).astype(BF16)
        d_qk[:, wide:] = jnp.zeros_like(d_qk[:, wide:])
        for hd in range(heads):
            lanes = slice(hd * HD, (hd + 1) * HD)
            k_lanes = slice(wide + hd * HD, wide + (hd + 1) * HD)
            v_lanes = slice(2 * wide + hd * HD, 2 * wide + (hd + 1) * HD)
            kh = k[pl.ds(start, length), lanes]
            vh = v[pl.ds(start, length), lanes]
            for r in range(length // step):
                part = pl.ds(start + r * step, step)
                local = pl.ds(r * step, step)
                allowed = id_col[part, 0:1] >= id_row[s : s + 1, :]
                qh = q[part, lanes]
                score = dot(qh, kh, NT) * scale
                p = jnp.where(allowed, jnp.exp(score - lse[part, hd : hd + 1]), 0.0)
                doh = d_o[local, lanes]
                dp = dot(doh, vh, NT)
                inner = jnp.sum(p * dp, axis=-1, keepdims=True)
                ds = (p * (dp - inner)).astype(BF16)
                d_qk[local, lanes] = dot(ds, kh) * scale
                dk = dot(ds, qh, TN) * scale
                dv = dot(p.astype(BF16), doh, TN)
                if length == step:
                    d_qk[:, k_lanes] = dk
                    d_qk[:, v_lanes] = dv
                else:
                    d_qk[:, k_lanes] += dk
                    d_qk[:, v_lanes] += dv
        if s == 0:
            for c in loads:
                c.wait()
        block = 256
        half = length // 2
        for b in range(length // block):
            local = pl.ds(b * block, block)
            at = pl.ds(start + b * block, block)
            qk = turn(d_qk[local, : 2 * wide], tables[0, local], tables[1, local], tables[2, local], -1.0)
            lin = jnp.concatenate([qk, d_qk[local, 2 * wide :]], axis=-1).astype(BF16)
            d_lin[at, :] = lin
            bias_grad[...] += jnp.sum(lin.astype(F32), axis=0, keepdims=True)
            d_h = dot(lin, w[...].reshape(D, 3 * wide), NT).astype(BF16)
            out = keep if b * block < half else send
            out[pl.ds(s * half + (b * block) % half, block), :] = d_h


def attention_back(sc, tables, id_row, id_col, q, k, v, lse, w_out, d_rows, weight):
    N, wide = q.shape
    D = w_out.shape[1]
    heads = wide // HD
    length = N // 2
    n_sr, _, _, f = weight[0][0].shape
    rows = D // (8 * n_sr)
    dims = (heads, length, N, D, [p[1:] for p in weight])
    return pl.pallas_call(
        functools.partial(attention_back_kernel, dims, d_rows),
        out_shape=[
            jax.ShapeDtypeStruct((N, 3 * wide), BF16),
            jax.ShapeDtypeStruct((1, 3 * wide), F32),
            jax.ShapeDtypeStruct((N // 2, D), BF16),
            jax.ShapeDtypeStruct((N // 2, D), BF16),
        ],
        in_specs=[SMEM] + [VMEM] * 8 + [ANY] * (2 + len(weight)),
        out_specs=[VMEM] * 4,
        scratch_shapes=[
            pltpu.VMEM((2, n_sr, 2, 2, rows, f), BF16),
            pltpu.VMEM((length, wide), BF16),
            pltpu.VMEM((length, 3 * wide), F32),
            pltpu.SemaphoreType.DMA((len(weight),)),
        ]
        + d_rows.scratch(),
        compiler_params=params(),
        cost_estimate=cost(23),
    )(sc, tables, id_row, id_col, q, k, v, lse, w_out, *d_rows.arrays, *[p[0] for p in weight])


def rows_kernel(dims, sc, h, d, other0, other1, same0, same1):
    n, two_rows = dims
    t = dot(h[...], d[...], TN).astype(BF16)
    i = pl.program_id(0)
    for f in range(2):
        for step_, other, same in ((0, other0, same0), (1, other1, same1)):
            for out, here in ((same, sc[1] == f), (other, sc[1] != f)):

                @pl.when(here & (i == step_))
                def _():
                    for j in range(n):
                        r = (2 * j + f) * two_rows
                        out[j * two_rows : (j + 1) * two_rows, :] = t[r : r + two_rows]


def grad_rows(sc, h, d, side, n_sr, rows):
    N, D = h.shape
    f = d.shape[1]
    cut = D // 4
    n = n_sr // 2
    spec = pltpu.PrefetchScalarGridSpec(
        num_scalar_prefetch=1,
        grid=(2,),
        in_specs=[
            pl.BlockSpec((N, cut), lambda i, sc: (0, (sc[0] ^ side) * 2 + i)),
            pl.BlockSpec((N, f), lambda i, sc: (0, 0)),
        ],
        out_specs=[pl.BlockSpec((cut // 2, f), lambda i, sc: (0, 0))] * 4,
    )
    return pl.pallas_call(
        functools.partial(rows_kernel, (n, 2 * rows)),
        grid_spec=spec,
        out_shape=[jax.ShapeDtypeStruct((cut // 2, f), BF16)] * 4,
        compiler_params=params(),
        cost_estimate=cost(7),
    )(sc, h, d)


def slices_kernel(rows, cut, d_rows, sc, a, d0, d1, *refs):
    outs, (buf, sems) = refs[:4], refs[4:]
    i = pl.program_id(0)

    @pl.when(i == 0)
    def _():
        for c in d_rows.load((d0, d1), buf, sems):
            c.wait()

    d = buf[:, pl.ds(pl.multiple_of(i * cut, cut), cut)]
    t = dot(a[...], d, TN).astype(BF16)
    for n in range(4):
        for k in range(4):

            @pl.when((sc[0] == (n // 2) ^ (k // 2)) & (sc[1] == (n % 2) ^ (k % 2)))
            def _():
                outs[k][...] = t[n * rows : (n + 1) * rows]


def grad_slices(sc, a, d_rows):
    N, f = a.shape
    D = d_rows.D
    cut = D // 4
    spec = pltpu.PrefetchScalarGridSpec(
        num_scalar_prefetch=1,
        grid=(D // cut,),
        in_specs=[pl.BlockSpec((N, f), lambda i, sc: (0, 0)), ANY, ANY],
        out_specs=[pl.BlockSpec((f // 4, cut), lambda i, sc: (0, i))] * 4,
        scratch_shapes=d_rows.scratch(),
    )
    return pl.pallas_call(
        functools.partial(slices_kernel, f // 4, cut, d_rows),
        grid_spec=spec,
        out_shape=[jax.ShapeDtypeStruct((f // 4, D), BF16)] * 4,
        compiler_params=params(),
        cost_estimate=cost(9),
    )(sc, a, *d_rows.arrays)


def total_of(terms):
    d = terms[0].astype(F32)
    for n in range(1, terms.shape[0]):
        d += terms[n].astype(F32)
    return d


def forward_kernel(terms, x, gain, bias, x2, copies):
    v = x[...].astype(F32) + total_of(terms)
    x2[...] = v
    normed, _ = normalize(v)
    h = (normed * gain[...] + bias[...]).astype(BF16)
    for n in range(copies.shape[0]):
        copies[n] = h


def norm_step(terms, x, gain, bias):
    n, m, D = terms.shape
    return pl.pallas_call(
        forward_kernel,
        out_shape=[jax.ShapeDtypeStruct((m, D), F32), jax.ShapeDtypeStruct((n, m, D), BF16)],
        in_specs=[VMEM] * 4,
        out_specs=[VMEM] * 2,
        compiler_params=params(),
        cost_estimate=cost(4),
    )(terms, x, gain, bias)


def back_kernel(terms, x, dy, gain, grad, copies, sums):
    d_h = total_of(terms)
    normed, inv_std = normalize(x[...].astype(F32))
    total = dy[...].astype(F32) + normalize_back(d_h * gain[...], normed, inv_std)
    grad[...] = total
    low = total.astype(BF16)
    for n in range(copies.shape[0]):
        copies[n] = low
    sums[0:1, :] = jnp.sum(d_h * normed, axis=0, keepdims=True)
    sums[1:2, :] = jnp.sum(d_h, axis=0, keepdims=True)


def norm_step_back(terms, x, dy, gain, copies):
    n, m, D = terms.shape
    return pl.pallas_call(
        back_kernel,
        out_shape=[
            jax.ShapeDtypeStruct((m, D), F32),
            jax.ShapeDtypeStruct((copies, m, D), BF16),
            jax.ShapeDtypeStruct((2, D), F32),
        ],
        in_specs=[VMEM] * 4,
        out_specs=[VMEM] * 3,
        compiler_params=params(),
        cost_estimate=cost(4),
    )(terms, x, dy, gain)


def shards(
    inputs,
    cotangent,
    block_ids,
    ln1_gain,
    ln1_bias,
    qkv_weight,
    qkv_bias,
    out_weight,
    ln2_gain,
    ln2_bias,
    gate_weight,
    up_weight,
    down_weight,
):
    sb, sx, c, fh, fl = (lax.axis_index(a).astype(jnp.int32) for a in EVERY)
    n_sx = lax.axis_size("sx")
    sr, n_sr = sx * 2 + c, 2 * n_sx
    quad = 2 * n_sx
    n_dev = 8 * n_sr
    members = 2 * n_sr
    tok = inputs.shape[2]
    m = 2 * tok
    D = inputs.shape[3]
    length = block_ids.shape[2]
    N = 2 * length
    rows = qkv_weight.shape[0]
    ff_rows = down_weight.shape[0]
    ff = 4 * ff_rows
    heads = H // members
    wide = heads * HD
    natural = H % n_dev == 0
    sc = jnp.stack([sb, fh])

    def pick(v, i):
        return lax.dynamic_index_in_dim(v, i, 0, keepdims=False)

    def device_of(t, a):
        return (((a // 2) * n_sr + t // 2) * 2 + a % 2) * 2 + t % 2

    def head_of(t, i):
        return device_of(t, i) if natural else t * heads + i

    qkv_plan = [
        [(0, (head_of(t, i) * 3 + part) * HD, HD) for part in range(3) for i in range(heads)]
        for t in range(members)
    ]
    gu_plan = [
        [(w, device_of(t, a) * ff_rows, ff_rows) for w in range(2) for a in range(4)]
        for t in range(members)
    ]
    head_place = {head_of(t, i): (t, i) for t in range(members) for i in range(heads)}
    qkv_back = [
        (head_place[h][0], part * wide + head_place[h][1] * HD, HD) for h in range(H) for part in range(3)
    ]
    ff_place = {device_of(t, a): (t, a) for t in range(members) for a in range(4)}
    gate_back = [(ff_place[d][0], ff_place[d][1] * ff_rows, ff_rows) for d in range(n_dev)]
    up_back = [(t, ff + b, n) for t, b, n in gate_back]

    def exchange(v):
        return lax.all_to_all(v, MEMBERS, split_axis=0, concat_axis=0, tiled=True)

    def of_rows(v):
        return v.reshape((n_sr, 2) + v.shape[1:])

    def both(bit, own, other):
        return jnp.stack([jnp.where(bit == 0, own, other), jnp.where(bit == 0, other, own)])

    my_ids = pick(block_ids, sb)
    c_of = (jnp.arange(2, dtype=jnp.int32) ^ c)[:, None, None, None]
    sx_of = jnp.arange(n_sx, dtype=jnp.int32)[None, :, None, None]
    sb_of = (jnp.arange(2, dtype=jnp.int32) ^ sb)[None, None, :, None]
    pos = ((sb_of * n_sx + sx_of) * 2 + c_of) * tok + jnp.arange(tok, dtype=jnp.int32)[None, None, None, :]
    pos = pos.reshape(-1)
    half = ROT // 2
    lane = np.arange(2 * wide) % HD
    turned = lane < ROT
    frequency = np.where(turned, rope_base ** (-2.0 * (lane % half).astype(np.float32) / ROT), 0.0)
    angles = pos.astype(F32)[:, None] * jnp.asarray(frequency, F32)[None, :]
    sine = jnp.sin(angles)
    to_back = jnp.asarray(np.where(turned & (lane >= half), 1.0, 0.0), F32)
    to_front = jnp.asarray(np.where(lane < half, -1.0, 0.0), F32)
    tables = jnp.stack([jnp.cos(angles), sine * to_back, sine * to_front])

    rep = lambda v_: jnp.broadcast_to(v_[None], (quad,) + v_.shape)
    flat = lambda v_: v_.reshape(-1, v_.shape[-1])
    by_member_of_quad = lambda v_: v_.reshape(quad, m, D)

    small = jnp.concatenate([ln1_gain, ln1_bias, ln2_gain, ln2_bias, qkv_bias])
    n_small = small.shape[0]
    small = jnp.pad(small[None], ((0, 7), (0, 3 * wide - n_small)))
    live = Live(
        sc=sc,
        inputs=inputs,
        cotangent=cotangent,
        my_ids=my_ids,
        out_w=out_weight,
        gate_w=gate_weight,
        up_w=up_weight,
        down_w=down_weight,
    )
    half_rows = ff_rows // 32 * 16 if ff_rows % 16 == 0 else ff_rows // 2
    live.done(qkv_c=columns([qkv_weight], qkv_plan, small))
    down_a, down_b = live.down_w[:half_rows], live.down_w[half_rows:]
    live.drop("down_w")
    give = jnp.concatenate([pick(live.inputs, 1 - sb)[0], pick(live.cotangent, 1 - sb)[0]], 0)
    live.done(
        w_qkv=of_rows(exchange(live.qkv_c)),
        got=swap_sb(give),
        out_1=swap_fh(live.out_w) if natural else live.out_w,
        ids_got=swap_fl(live.my_ids),
        gu_c=columns([live.gate_w, live.up_w], gu_plan),
        down_a=down_a,
        down_b=down_b,
        tables=tables,
    )

    own_x = jnp.concatenate([pick(live.inputs, sb)[0], live.got[:tok]], 0)
    own_dy = jnp.concatenate([pick(live.cotangent, sb)[0], live.got[tok:]], 0)
    ids = both(fl, live.my_ids, live.ids_got).reshape(2, 2, n_sx, 2, tok)
    ids = flip_if(c, flip_if(sb, ids, 1), 3).transpose(0, 3, 2, 1, 4).reshape(2, length)
    live.drop("inputs", "cotangent", "got", "my_ids", "ids_got", "gate_w", "up_w", "qkv_c")
    live.done(
        qkv_1=swap_fh(live.w_qkv),
        qkv_2=swap_sb(live.w_qkv),
        w_gu=of_rows(exchange(live.gu_c)),
        own_x=own_x,
        own_dy=own_dy,
        x_rep=rep(own_x),
        out_2=swap_sb(live.out_w) if natural else live.out_w,
        out_3=swap_sb(live.out_1) if natural else live.out_w,
        ids=ids,
        id_col=ids.reshape(N, 1),
    )

    cut = n_sr // 2
    gu_a, gu_b = live.w_gu[:cut], live.w_gu[cut:]
    live.done(
        qkv_3=swap_sb(live.qkv_1),
        x_mine=flat(over_quad(live.x_rep)),
        dy_rep=rep(live.own_dy),
        gu_1a=swap_fh(gu_a),
        gu_b=gu_b,
    )
    small = [v_[:, :, rows, :n_small] for v_ in (live.w_qkv, live.qkv_1, live.qkv_2, live.qkv_3)]
    small = in_order(small, sb, fh).transpose(0, 2, 1, 3, 4).reshape(n_dev, n_small).astype(F32)
    if natural:
        out_own = in_order((live.out_w, live.out_1, live.out_2, live.out_3), sb, fh)
        out_own = out_own.reshape(wide, D)
    else:
        out_all = lax.all_gather(out_weight, EVERY, axis=0, tiled=True)
        out_own = lax.dynamic_slice_in_dim(out_all, (sr * 2 + fl) * wide, wide, 0)
    gain1, bias1, gain2, bias2 = (
        small[:, n * rows : (n + 1) * rows].reshape(1, D) for n in range(4)
    )
    bias_all = small[:, 4 * rows :].reshape(H, 3, HD)
    if natural:
        my_bias = bias_all.reshape(2, n_sr, 2, 2, 3, HD)
        my_bias = lax.dynamic_index_in_dim(my_bias, sr, 1, keepdims=False)
        my_bias = lax.dynamic_index_in_dim(my_bias, fl, 2, keepdims=False).reshape(heads, 3, HD)
    else:
        my_bias = lax.dynamic_slice_in_dim(bias_all, (sr * 2 + fl) * heads, heads, 0)
    my_bias = my_bias.transpose(1, 0, 2).reshape(1, 3 * wide)

    live.done(
        x_other=swap_c(live.x_mine),
        gain1=gain1,
        bias1=bias1,
        gain2=gain2,
        bias2=bias2,
        my_bias=my_bias,
        out_own=out_own,
    )

    qkv = lambda: [(live.w_qkv, 0, 0), (live.qkv_1, 1, 0), (live.qkv_2, 2, 0), (live.qkv_3, 3, 0)]
    h1, q, k, v, o, lse, keep, send = attention(
        live.sc,
        Rows(live.x_mine, live.x_other),
        live.gain1,
        live.bias1,
        live.my_bias,
        live.tables,
        live.ids,
        live.id_col,
        live.out_own,
        qkv(),
        heads,
        rows,
    )
    live.drop("x_mine", "x_other", "x_rep", "out_w", "out_1", "out_2", "out_3", "gu_c", "bias1", "my_bias")
    live.done(
        h1=h1,
        q=q,
        k=k,
        v=v,
        o=o,
        lse=lse,
        keep=keep,
        send=send,
        gu_1b=swap_fh(live.gu_b),
        down_1a=swap_fh(live.down_a),
        gu_2=swap_sb(live.w_gu),
        down_2a=swap_sb(live.down_a),
        dy_mine=flat(over_quad(live.dy_rep)),
    )
    live.drop("dy_rep", "gu_b")

    def plus(a_, b_, kind=F32):
        return (a_.astype(F32) + b_.astype(F32)).astype(kind)

    live.done(got=swap_c(live.send))
    live.done(
        terms=over_quad(by_member_of_quad(plus(live.keep, live.got, BF16))),
        gu_3=[swap_sb(live.gu_1a), swap_sb(live.gu_1b)],
        dy_other=swap_c(live.dy_mine),
        down_1b=swap_fh(live.down_b),
    )
    x2_own, h2_rep = norm_step(live.terms, live.own_x, live.gain2, live.bias2)
    live.done(
        x2_own=x2_own,
        h2_mine=flat(over_quad(h2_rep)),
        down_2b=swap_sb(live.down_b),
        down_3=[swap_sb(live.down_1a), swap_sb(live.down_1b)],
    )
    live.done(h2_other=swap_c(live.h2_mine))

    down = [live.down_a, live.down_1a, live.down_2a, live.down_3[0], live.down_b, live.down_1b, live.down_2b, live.down_3[1]]
    down_places = [(n, 0) for n in range(4)] + [(n, half_rows) for n in range(4)]
    if ff_rows % 16 != 0:
        down = in_order([jnp.concatenate([down[n], down[n + 4]], 0) for n in range(4)], sb, fh)
        down, down_places = [down.reshape(ff, D)], [(0, 0)]
    gu = [(live.w_gu, 0, 0), (live.gu_1a, 1, 0), (live.gu_1b, 1, cut)]
    gu += [(live.gu_2, 2, 0), (live.gu_3[0], 3, 0), (live.gu_3[1], 3, cut)]
    h2, act, d_gu, keep, send = ffn(
        live.sc,
        Rows(live.h2_mine, live.h2_other),
        Rows(live.dy_mine, live.dy_other),
        gu,
        down,
        down_places,
        rows,
    )
    live.drop("w_gu", "gu_1a", "gu_1b", "gu_2", "gu_3", "down_a", "down_b")
    live.drop("down_1a", "down_1b", "down_2a", "down_2b", "down_3")
    live.drop("h2_mine", "h2_other", "bias2", "got", "terms")

    def give_back(v_):
        other = swap_sb(v_[tok:])
        first = jnp.where(sb == 0, v_[:tok], other)
        second = jnp.where(sb == 0, other, v_[:tok])
        return jnp.stack([first, second])[:, None]

    live.done(
        h2=h2,
        act=act,
        d_gu=d_gu,
        down=down,
        keep=keep,
        got=swap_c(send),
        gu_t=grad_rows(live.sc, h2, d_gu, 1, n_sr, rows),
    )
    live.done(
        terms=over_quad(by_member_of_quad(plus(live.keep, live.got, BF16))),
        gu_got1=[swap_sb(v_) for v_ in live.gu_t[:2]],
        down_t=grad_slices(live.sc, live.act, Rows(live.dy_mine, live.dy_other)),
        gu_m=grad_rows(live.sc, live.h2, live.d_gu, 0, n_sr, rows),
    )
    live.drop("dy_mine", "dy_other", "h2", "d_gu")
    d_x2, att_rep, sums2 = norm_step_back(live.terms, live.x2_own, live.own_dy, live.gain2, quad)
    y_keep, y_send = down_product(live.sc, live.act, live.down, down_places)
    live.drop("act", "down")
    live.done(
        d_x2=d_x2,
        sums2=sums2,
        att_mine=flat(over_quad(att_rep)),
        gu_over=[swap_fh(plus(live.gu_m[0], live.gu_got1[0], BF16))],
        gu_give=plus(live.gu_m[1], live.gu_got1[1], BF16),
        gu_got0=[swap_sb(v_) for v_ in live.gu_t[2:]],
        y_keep=y_keep,
        y_send=y_send,
    )
    live.drop("gu_t", "gu_got1")
    live.done(att_other=swap_c(live.att_mine), y_got=swap_c(live.y_send))
    d_lin, bias_term, keep, send = attention_back(
        live.sc,
        live.tables,
        live.ids,
        live.id_col,
        live.q,
        live.k,
        live.v,
        live.lse,
        live.out_own,
        Rows(live.att_mine, live.att_other),
        qkv(),
    )
    live.drop("q", "k", "v", "lse", "out_own", "w_qkv", "qkv_1", "qkv_2", "qkv_3", "tables", "ids", "id_col", "y_send")
    live.done(
        d_lin=d_lin,
        bias_term=bias_term,
        keep=keep,
        send=send,
        y_terms=over_quad(by_member_of_quad(plus(live.y_keep, live.y_got, BF16))),
        down_got=[swap_sb(v_) for v_ in live.down_t[2:]],
        gu_over=live.gu_over + [swap_fh(live.gu_give)],
    )
    live.drop("y_keep", "y_got", "gu_give")
    live.done(
        got=swap_c(live.send),
        qkv_t=grad_rows(live.sc, live.h1, live.d_lin, 1, n_sr, rows),
        down_give=plus(live.down_t[1], live.down_got[1], BF16),
    )
    live.drop("send")
    gu_sum = [
        (live.gu_m[2 + n].astype(F32) + live.gu_got0[n].astype(F32) + live.gu_over[n].astype(F32)).astype(BF16)
        for n in range(2)
    ]
    live.done(
        terms=over_quad(by_member_of_quad(plus(live.keep, live.got, BF16))),
        qkv_got=[swap_sb(v_) for v_ in live.qkv_t],
        down_over=swap_fh(live.down_give),
        qkv_m=grad_rows(live.sc, live.h1, live.d_lin, 0, n_sr, rows),
        out_t=grad_slices(live.sc, live.o, Rows(live.att_mine, live.att_other)) if natural else (),
        gu_sum=jnp.concatenate(gu_sum, 0),
    )
    live.drop("keep", "got", "h1", "d_lin", "qkv_t", "gu_m", "gu_got0", "gu_over", "down_give")
    _, input_low, sums1 = norm_step_back(live.terms, live.own_x, live.d_x2, live.gain1, 1)
    qkv_give = jnp.concatenate([plus(live.qkv_m[n], live.qkv_got[n], BF16) for n in range(2)], 0)
    y = live.x2_own + jnp.sum(live.y_terms.astype(F32), axis=0)
    live.done(
        input_low=input_low[0],
        sums1=sums1,
        gu_done=exchange(live.gu_sum.reshape(members, rows, -1)),
        qkv_over=swap_fh(qkv_give),
        out_got=[swap_sb(v_) for v_ in live.out_t[2:]],
        layer_out=give_back(y.astype(BF16)),
        down_grad=plus(live.down_t[0], live.down_got[0]) + live.down_over.astype(F32),
    )
    live.drop("down_t", "down_got", "down_over", "y_terms", "gu_sum")
    if natural:
        out_grad = swap_fh(plus(live.out_t[1], live.out_got[1], BF16)).astype(F32)
        out_grad = plus(live.out_t[0], live.out_got[0]) + out_grad
    else:
        d_att = jnp.stack([live.att_mine.reshape(2, N // 4, D), live.att_other.reshape(2, N // 4, D)], 1)
        t = lax.dot_general(live.o, d_att.reshape(N, D), TN, preferred_element_type=F32)
        t = jnp.where(jnp.arange(members)[:, None, None] == sr * 2 + fl, t[None], 0.0)
        out_grad = lax.psum_scatter(t.reshape(H * HD, D), EVERY, scatter_dimension=0, tiled=True)
    qkv_sum = jnp.concatenate([plus(live.qkv_m[2 + n], live.qkv_got[2 + n]) for n in range(2)], 0)
    qkv_sum = plus(qkv_sum, live.qkv_over, BF16)
    qkv_grad = uncolumns([exchange(qkv_sum.reshape(members, rows, -1))], qkv_back)
    input_grad, layer_out, down_grad = give_back(live.input_low), live.layer_out, live.down_grad
    gate_grad = uncolumns([live.gu_done], gate_back)
    up_grad = uncolumns([live.gu_done], up_back)
    sums1, sums2, bias_term = live.sums1, live.sums2, live.bias_term

    bias_term = bias_term.reshape(3, heads, HD).transpose(1, 0, 2)
    if natural:
        bias_term = bias_term.reshape(2, 1, 2, 1, -1)
        here = jnp.arange(n_sr)[None, :, None, None, None] == sr
        here = here & (jnp.arange(2)[None, None, None, :, None] == fl)
    else:
        bias_term = bias_term[None]
        here = jnp.arange(members)[:, None, None, None] == sr * 2 + fl
    bias_term = jnp.where(here, bias_term, 0.0).reshape(n_dev, -1)
    small = jnp.concatenate(
        [sums1[0].reshape(n_dev, -1), sums1[1].reshape(n_dev, -1)]
        + [sums2[0].reshape(n_dev, -1), sums2[1].reshape(n_dev, -1), bias_term],
        axis=1,
    )
    small = small.reshape(2, n_sr, 2, 2, -1).transpose(1, 3, 0, 2, 4).reshape(members, 4, -1)
    small = jnp.sum(exchange(small), axis=0).reshape(2, 2, -1)
    small = pick(small, sb) + swap_sb(pick(small, 1 - sb))
    small = pick(small, fh) + swap_fh(pick(small, 1 - fh))
    gain1_grad, bias1_grad, gain2_grad, bias2_grad = (
        small[n * rows : (n + 1) * rows] for n in range(4)
    )
    bias_grad = small[4 * rows :]
    return (
        layer_out,
        input_grad,
        gain1_grad,
        bias1_grad,
        qkv_grad,
        bias_grad,
        out_grad,
        gain2_grad,
        bias2_grad,
        gate_grad,
        up_grad,
        down_grad,
    )


def solution(mesh):
    names = dict(mesh.shape)
    n_seq, n_fsdp = names["seq"], names["fsdp"]
    fine = Mesh(mesh.devices.reshape(2, n_seq // 4, 2, 2, n_fsdp // 2), EVERY)
    tokens = P(None, ("fh", "fl"), ("sb", "sx", "c"), None)
    vector = P(EVERY)
    matrix = P(EVERY, None)
    in_specs = (tokens, tokens, P(None, ("fh", "fl"), None), vector, vector, matrix, vector, matrix)
    in_specs += (vector, vector, matrix, matrix, matrix)
    out_specs = (tokens, tokens, vector, vector, matrix, vector, matrix, vector, vector)
    out_specs += (matrix, matrix, matrix)
    return jax.shard_map(shards, mesh=fine, in_specs=in_specs, out_specs=out_specs, check_vma=False)
```

time: 828 us -> 622 us (0.75)
  local copies, waits for them, and re-layouts: 220 us -> 29.5 us
  Pallas kernels: 0 us -> 159 us
  matrix products: 100 us -> 0 us
  blocking collectives: 79.4 us -> 0 us
  other arithmetic: 76.5 us -> 51.6 us
  waiting for transfers between devices: 250 us -> 267 us
  starting transfers between devices: 89.5 us -> 104 us
    pallas_call x0 -> x18, Pallas kernels: none -> 159 us  [the longest x1 29.6 us: ffn(): pl.pallas_call(functools.partial(ffn_kernel, dims, h_rows, dy_rows), grid...]
    dot_general x28 -> x0, matrix products: 93 us -> none  [the longest x4 16.8 us: part(): lax.dot_general(side, d, (((0,), (0,)), ((), ())), preferred_element_type...]
    ppermute x8 -> x12, waiting for transfers between devices: 52.9 us -> 142 us  [swap_fh(): return lax.ppermute(v, 'fh', SWAP)]
    unnamed x2 -> x0, blocking collectives: 79.4 us -> none
    ppermute x17 -> x1, waiting for transfers between devices: 73.6 us -> 0.35 us  [swap_fl(): return lax.ppermute(v, 'fl', SWAP)]
    reshape x26 -> x11, local copies, waits for them, and re-layouts: 77.6 us -> 4.92 us  [the longest x4 2.7 us: shards(): small[:, n * rows:(n + 1) * rows].reshape(1, D)]
    unnamed x247 -> x105, local copies, waits for them, and re-layouts: 45.5 us -> 8.25 us
    all_to_all x0 -> x8, starting transfers between devices: none -> 33.8 us  [over_quad(): return lax.all_to_all(v, QUAD, split_axis=0, concat_axis=0, tiled=True)]
  transfers between devices with their start and end apart: 84 -> 61, of which waited for: 32 -> 30; matrix products, arithmetic and copies ran while one was open for 43% -> 8% of each run, Pallas kernels for 0% -> 18%
where the time goes in v2:
time: 622 us; the launch traced here: 613 us
  waiting for transfers between devices  267 us (43%)
  Pallas kernels  159 us (26%)
  starting transfers between devices  104 us (17%)
  other arithmetic  51.6 us (8%)
  local copies, waits for them, and re-layouts  29.5 us (5%)
    ppermute x12, waiting for transfers between devices, swap_fh(): return lax.ppermute(v, 'fh', SWAP)  142 us
    ppermute x27, waiting for transfers between devices, swap_sb(): return lax.ppermute(v, 'sb', SWAP)  94.4 us
    all_to_all x8, starting transfers between devices, over_quad(): return lax.all_to_all(v, QUAD, split_axis=0, concat_axis=0, tiled=True)  33.8 us
    ppermute x27, starting transfers between devices, swap_sb(): return lax.ppermute(v, 'sb', SWAP)  30.3 us
    pallas_call x1, Pallas kernels, ffn(): pl.pallas_call(functools.partial(ffn_kernel, dims, h_rows, dy_rows), grid...  29.6 us
    pallas_call x4, Pallas kernels, grad_rows(): pl.pallas_call(functools.partial(rows_kernel, (n, 2 * rows)), grid_spec=s...  28.8 us
    convert_element_type x11, other arithmetic, plus(): return (a_.astype(F32) + b_.astype(F32)).astype(kind)  26.9 us
    pallas_call x1, Pallas kernels, attention(): pl.pallas_call(functools.partial(attention_kernel, (heads, length, block,...  26.1 us
  transfers between devices with their start and end apart: 61, of which 30 were waited for; matrix products, arithmetic and copies ran while one was open for 8% of the time, Pallas kernels for 18%

profile of v2, /device:TPU:0, one launch (start us, length us, event | category | flops | bytes accessed | tf_op | source)
XLA Modules:
  0.0 613.2 jit_solution(222120265875720858)
XLA Ops:
  43.7 21.4 %collective-permute-done.4 = bf16[64,2048]{1,0:T(8,128)(2,1)} collective-permute-done((bf16[64,2048]{1,0:T(8,128)(2,1)}, bf16[64,2048]{1,0:T(8,128)(2,1)}, u32[]{:S(2)}, u32[]{:S(2)}) %collective-permute-start.4) | collective-permute-done | bytes 262176 | tf_op jit(solution)/shard_map/ppermute | solution.py:48
  70.3 9.9 %collective-permute-done.5.refs_1_ = bf16[4,2,72,768]{3,2,1,0:T(8,128)(2,1)} collective-permute-done((bf16[4,2,72,768]{3,2,1,0:T(8,128)(2,1)}, bf16[4,2,72,768]{3,2,1,0:T(8,128)(2,1)}, u32[]{:S(2)}, u32[]{:S(2)}) %collective-permute-start.5) | collective-permute-done | bytes 884768 | tf_op jit(solution)/shard_map/ppermute | solution.py:52
  88.1 36.4 %collective-permute-done.7.refs_1_ = bf16[2,2,64,1408]{3,2,1,0:T(8,128)(2,1)S(1)} collective-permute-done((bf16[2,2,64,1408]{3,2,1,0:T(8,128)(2,1)S(1)}, bf16[2,2,64,1408]{3,2,1,0:T(8,128)(2,1)S(1)}, u32[]{:S(2)}, u32[]{:S(2)}) %collective-permute-start.7) | collective-permute-done | bytes 720928 | tf_op jit(solution)/shard_map/ppermute | solution.py:52
  145.9 26.1 %shard_map.249 = (bf16[1024,2048]{1,0:T(8,128)(2,1)}, bf16[1024,256]{1,0:T(8,128)(2,1)}, bf16[1024,256]{1,0:T(8,128)(2,1)}, bf16[1024,256]{1,0:T(8,128)(2,1)}, b...) custom-call(s32[2]{0:T(128)} %pad_add_fusion.sc, ...), custom_call_target="tpu_custom_call" | custom-call | flops 24999999488 | bytes 1024 | tf_op jit(solution)/shard_map/pallas_call | solution.py:313
  172.0 17.5 %collective-permute-done.12.refs_2_ = bf16[2,2,64,1408]{3,2,1,0:T(8,128)(2,1)} collective-permute-done((bf16[2,2,64,1408]{3,2,1,0:T(8,128)(2,1)}, bf16[2,2,64,1408]{3,2,1,0:T(8,128)(2,1)}, u32[]{:S(2)}, u32[]{:S(2)}) %collective-permute-start.12) | collective-permute-done | bytes 720928 | tf_op jit(solution)/shard_map/ppermute | solution.py:52
  204.9 29.0 %collective-permute-done.15.refs_11_.refs_5_ = bf16[96,2048]{1,0:T(8,128)(2,1)S(1)} collective-permute-done((bf16[96,2048]{1,0:T(8,128)(2,1)S(1)}, bf16[96,2048]{1,0:T(8,128)(2,1)S(1)}, u32[]{:S(2)}, u32[]{:S(2)}) %collective-permute-start.15) | collective-permute-done | bytes 393248 | tf_op jit(solution)/shard_map/ppermute | solution.py:52
  249.1 22.3 %collective-permute-done.20.refs_9_.refs_3_ = bf16[80,2048]{1,0:T(8,128)(2,1)S(1)} collective-permute-done((bf16[80,2048]{1,0:T(8,128)(2,1)}, bf16[80,2048]{1,0:T(8,128)(2,1)S(1)}, u32[]{:S(2)}, u32[]{:S(2)}) %collective-permute-start.20) | collective-permute-done | bytes 327712 | tf_op jit(solution)/shard_map/ppermute | solution.py:48
  276.5 29.6 %shard_map.251 = (bf16[1024,2048]{1,0:T(8,128)(2,1)}, bf16[1024,704]{1,0:T(8,128)(2,1)}, bf16[1024,1408]{1,0:T(8,128)(2,1)}, bf16[512,2048]{1,0:T(8,128)(2,1)}, bf16[512,2048]{1,0:T(8,128)(2,1)}) custom-call(s32[2]{0:T(128)} %pad_add_fusion.sc, bf16[512,2048]{1,0:T(8,128)(2,1)} %bitcast.98, bf16[512,2048]{1,0:T(8,128)(2,1)} %collective-permute-done.22.h1, ...), custom_call_target="tpu_custom_call" | custom-call | flops 30000001024 | bytes 1024 | tf_op jit(solution)/shard_map/pallas_call | solution.py:396
  306.3 8.6 %shard_map.252 = (bf16[256,1408]{1,0:T(8,128)(2,1)}, bf16[256,1408]{1,0:T(8,128)(2,1)}, bf16[256,1408]{1,0:T(8,128)(2,1)}, bf16[256,1408]{1,0:T(8,128)(2,1)}) custom-call(s32[2]{0:T(128)} %pad_add_fusion.sc, bf16[1024,2048]{1,0:T(8,128)(2,1)} %get-tuple-element.854.h, bf16[1024,1408]{1,0:T(8,128)(2,1)} %get-tuple-element.833.d), custom_call_target="tpu_custom_call" | custom-call | flops 7000000000 | bytes 1024 | tf_op jit(solution)/shard_map/pallas_call | solution.py:579
  324.7 9.9 %shard_map.253 = (bf16[176,2048]{1,0:T(8,128)(2,1)}, bf16[176,2048]{1,0:T(8,128)(2,1)}, bf16[176,2048]{1,0:T(8,128)(2,1)}, bf16[176,2048]{1,0:T(8,128)(2,1)}) custom-call(s32[2]{0:T(128)} %pad_add_fusion.sc, bf16[1024,704]{1,0:T(8,128)(2,1)} %get-tuple-element.915.a.act, bf16[512,2048]{1,0:T(8,128)(2,1)} %bitcast.96, ...), custom_call_target="tpu_custom_call" | custom-call | flops 8999999488 | bytes 1024 | tf_op jit(solution)/shard_map/pallas_call | solution.py:618
  334.6 8.4 %shard_map.254 = (bf16[256,1408]{1,0:T(8,128)(2,1)}, bf16[256,1408]{1,0:T(8,128)(2,1)}, bf16[256,1408]{1,0:T(8,128)(2,1)}, bf16[256,1408]{1,0:T(8,128)(2,1)}) custom-call(s32[2]{0:T(128)} %pad_add_fusion.sc, bf16[1024,2048]{1,0:T(8,128)(2,1)} %get-tuple-element.854.h, bf16[1024,1408]{1,0:T(8,128)(2,1)} %get-tuple-element.833.d), custom_call_target="tpu_custom_call" | custom-call | flops 7000000000 | bytes 1024 | tf_op jit(solution)/shard_map/pallas_call | solution.py:579
  343.0 13.5 %collective-permute-done.25 = bf16[256,1408]{1,0:T(8,128)(2,1)S(1)} collective-permute-done((bf16[256,1408]{1,0:T(8,128)(2,1)}, bf16[256,1408]{1,0:T(8,128)(2,1)S(1)}, u32[]{:S(2)}, u32[]{:S(2)}) %collective-permute-start.25) | collective-permute-done | bytes 720928 | tf_op jit(solution)/shard_map/ppermute | solution.py:48
  373.7 9.5 %shard_map.256 = (bf16[512,2048]{1,0:T(8,128)(2,1)}, bf16[512,2048]{1,0:T(8,128)(2,1)}) custom-call(s32[2]{0:T(128)} %pad_add_fusion.sc, bf16[1024,704]{1,0:T(8,128)(2,1)} %get-tuple-element.915.a.act, bf16[80,2048]{1,0:T(8,128)(2,1)} %slice.86.refs_6_.refs_0_, bf16[80,2048]{1,0:T(8,128)(2,1)} %collective-permute-done.10.refs_7_.refs_1_, ...), custom_call_target="tpu_custom_call" | custom-call | flops 8999999488 | bytes 1024 | tf_op jit(solution)/shard_map/pallas_call | solution.py:450
  383.2 21.1 %collective-permute-done.28 = bf16[256,1408]{1,0:T(8,128)(2,1)} collective-permute-done((bf16[256,1408]{1,0:T(8,128)(2,1)}, bf16[256,1408]{1,0:T(8,128)(2,1)}, u32[]{:S(2)}, u32[]{:S(2)}) %collective-permute-start.28) | collective-permute-done | bytes 720928 | tf_op jit(solution)/shard_map/ppermute | solution.py:52
  406.9 6.6 %collective-permute-done.29.d1 = bf16[512,2048]{1,0:T(8,128)(2,1)S(1)} collective-permute-done((bf16[512,2048]{1,0:T(8,128)(2,1)S(1)}, bf16[512,2048]{1,0:T(8,128)(2,1)S(1)}, u32[]{:S(2)}, u32[]{:S(2)}) %collective-permute-start.29) | collective-permute-done | bytes 2097184 | tf_op jit(solution)/shard_map/ppermute | solution.py:60
  426.6 21.6 %shard_map.257 = (bf16[1024,768]{1,0:T(8,128)(2,1)}, f32[1,768]{1,0:T(1,128)}, bf16[512,2048]{1,0:T(8,128)(2,1)}, bf16[512,2048]{1,0:T(8,128)(2,1)}) custom-call(s32[2]{0:T(128)} %pad_add_fusion.sc, f32[3,512,512]{2,1,0:T(8,128)} %pad_maximum_fusion.tables, s32[2,512]{1,0:T(2,128)} %reshape.544.id_row, s32[1024,1]{1,0:T(8,128)} %copy.134.id_col, ...), custom_call_target="tpu_custom_call" | custom-call | flops 23000000512 | bytes 1024 | tf_op jit(solution)/shard_map/pallas_call | solution.py:528
  448.2 9.4 %collective-permute-done.32 = bf16[176,2048]{1,0:T(8,128)(2,1)} collective-permute-done((bf16[176,2048]{1,0:T(8,128)(2,1)}, bf16[176,2048]{1,0:T(8,128)(2,1)}, u32[]{:S(2)}, u32[]{:S(2)}) %collective-permute-start.32) | collective-permute-done | bytes 720928 | tf_op jit(solution)/shard_map/ppermute | solution.py:48
  465.3 5.9 shard_map.258
  487.5 5.9 shard_map.260
  493.4 7.3 %shard_map.259 = (bf16[64,2048]{1,0:T(8,128)(2,1)}, bf16[64,2048]{1,0:T(8,128)(2,1)}, bf16[64,2048]{1,0:T(8,128)(2,1)}, bf16[64,2048]{1,0:T(8,128)(2,1)}) custom-call(s32[2]{0:T(128)} %pad_add_fusion.sc, bf16[1024,256]{1,0:T(8,128)(2,1)} %get-tuple-element.1044.a, bf16[512,2048]{1,0:T(8,128)(2,1)} %bitcast.93, bf16[512,2048]{1,0:T(8,128)(2,1)} %copy-done.41), custom_call_target="tpu_custom_call" | custom-call | flops 8999999488 | bytes 1024 | tf_op jit(solution)/shard_map/pallas_call | solution.py:618
  503.7 5.6 collective-permute-done.38
  510.0 7.4 %collective-permute-done.39 = bf16[256,768]{1,0:T(8,128)(2,1)} collective-permute-done((bf16[256,768]{1,0:T(8,128)(2,1)}, bf16[256,768]{1,0:T(8,128)(2,1)}, u32[]{:S(2)}, u32[]{:S(2)}) %collective-permute-start.39) | collective-permute-done | bytes 393248 | tf_op jit(solution)/shard_map/ppermute | solution.py:48
  546.8 21.8 %collective-permute-done.43 = bf16[512,768]{1,0:T(8,128)(2,1)} collective-permute-done((bf16[512,768]{1,0:T(8,128)(2,1)}, bf16[512,768]{1,0:T(8,128)(2,1)}, u32[]{:S(2)}, u32[]{:S(2)}) %collective-permute-start.43) | collective-permute-done | bytes 786464 | tf_op jit(solution)/shard_map/ppermute | solution.py:52
  603.0 6.5 %all-to-all-done.12.refs_0_ = bf16[8,64,768]{2,1,0:T(8,128)(2,1)S(1)} async-done(((bf16[8,64,768]{2,1,0:T(8,128)(2,1)}), bf16[8,64,768]{2,1,0:T(8,128)(2,1)S(1)}, u32[]{:S(2)}, u32[]{:S(2)}) %all-to-all-start.12) | async-done | bytes 786464 | tf_op jit(solution)/shard_map/all_to_all | solution.py:743
  (334 shorter events, 250.5 us)
Async XLA Ops:
  32.7 47.6 %all-to-all-start.1 = ((bf16[8,64,1408]{2,1,0:T(8,128)(2,1)}), bf16[8,64,1408]{2,1,0:T(8,128)(2,1)S(1)}, u32[]{:S(2)}, u32[]{:S(2)}) async-start(bf16[8,64,1408]{2,1,0:T(8,128)(2,1)} %shard_map.248), calls=%async_computation.1 | async-start | bytes 2883584 | tf_op jit(solution)/shard_map/all_to_all | solution.py:743
  36.7 33.6 %collective-permute-start.6 = (bf16[4,2,72,768]{3,2,1,0:T(8,128)(2,1)}, bf16[4,2,72,768]{3,2,1,0:T(8,128)(2,1)}, u32[]{:S(2)}, u32[]{:S(2)}) collective-permute-start(bf16[4,2,72,768]{3,2,1,0:T(8,128)(2,1)} %bitcast.5.refs_0_), channel_id=1, source_target_pairs={{0,16},{16,0},{1,17},{17,1},{2,18},{18,2},{3,19},{19,3},{4,20},{20... | collective-permute-start | bytes 2654216 | tf_op jit(solution)/shard_map/ppermute | solution.py:48
  38.2 42.0 %collective-permute-start.5 = (bf16[4,2,72,768]{3,2,1,0:T(8,128)(2,1)}, bf16[4,2,72,768]{3,2,1,0:T(8,128)(2,1)}, u32[]{:S(2)}, u32[]{:S(2)}) collective-permute-start(bf16[4,2,72,768]{3,2,1,0:T(8,128)(2,1)} %bitcast.5.refs_0_), channel_id=1, source_target_pairs={{0,2},{2,0},{1,3},{3,1},{4,6},{6,4},{5,7},{7,5},{8,10},{10,8},{9,1... | collective-permute-start | bytes 2654216 | tf_op jit(solution)/shard_map/ppermute | solution.py:52
  82.1 44.7 %all-to-all-start.2 = ((bf16[4,128,2048]{2,1,0:T(8,128)(2,1)}), bf16[4,128,2048]{2,1,0:T(8,128)(2,1)}, u32[]{:S(2)}, u32[]{:S(2)}) async-start(bf16[4,128,2048]{2,1,0:T(8,128)(2,1)} %broadcast_in_dim.26), calls=%async_computation.2 | async-start | bytes 4194304 | tf_op jit(solution)/shard_map/all_to_all | solution.py:64
  86.6 38.0 %collective-permute-start.8 = (bf16[4,2,72,768]{3,2,1,0:T(8,128)(2,1)}, bf16[4,2,72,768]{3,2,1,0:T(8,128)(2,1)}, u32[]{:S(2)}, u32[]{:S(2)}) collective-permute-start(bf16[4,2,72,768]{3,2,1,0:T(8,128)(2,1)} %collective-permute-done.5.refs_1_), channel_id=1, source_target_pairs={{0,16},{16,0},{1,17},{17,1},{2,18},{18,2},{3,19},{19,3},{4,20},{20... | collective-permute-start | bytes 2654216 | tf_op jit(solution)/shard_map/ppermute | solution.py:48
  88.1 36.4 %collective-permute-start.7 = (bf16[2,2,64,1408]{3,2,1,0:T(8,128)(2,1)S(1)}, bf16[2,2,64,1408]{3,2,1,0:T(8,128)(2,1)S(1)}, u32[]{:S(2)}, u32[]{:S(2)}) collective-permute-start(bf16[2,2,64,1408]{3,2,1,0:T(8,128)(2,1)S(1)} %get-tuple-element.1187), channel_id=1, source_target_pairs={{0,2},{2,0},{1,3},{3,1},{4,6},{6,4},{5,7},{7,5},{8,10},{10,8},{9,1... | collective-permute-start | bytes 2162696 | tf_op jit(solution)/shard_map/ppermute | solution.py:52
  135.8 53.7 %all-to-all-start.3 = ((bf16[4,128,2048]{2,1,0:T(8,128)(2,1)}), bf16[4,128,2048]{2,1,0:T(8,128)(2,1)S(1)}, u32[]{:S(2)}, u32[]{:S(2)}) async-start(bf16[4,128,2048]{2,1,0:T(8,128)(2,1)} %broadcast_in_dim.27), calls=%async_computation.3 | async-start | bytes 4194304 | tf_op jit(solution)/shard_map/all_to_all | solution.py:64
  142.6 46.9 %collective-permute-start.12 = (bf16[2,2,64,1408]{3,2,1,0:T(8,128)(2,1)}, bf16[2,2,64,1408]{3,2,1,0:T(8,128)(2,1)}, u32[]{:S(2)}, u32[]{:S(2)}) collective-permute-start(bf16[2,2,64,1408]{3,2,1,0:T(8,128)(2,1)} %get-tuple-element.625), channel_id=1, source_target_pairs={{0,2},{2,0},{1,3},{3,1},{4,6},{6,4},{5,7},{7,5},{8,10},{10,8},{9,1... | collective-permute-start | bytes 2162696 | tf_op jit(solution)/shard_map/ppermute | solution.py:52
  144.4 45.1 %collective-permute-start.13 = (bf16[4,2,64,1408]{3,2,1,0:T(8,128)(2,1)S(1)}, bf16[4,2,64,1408]{3,2,1,0:T(8,128)(2,1)}, u32[]{:S(2)}, u32[]{:S(2)}) collective-permute-start(bf16[4,2,64,1408]{3,2,1,0:T(8,128)(2,1)S(1)} %bitcast.89), channel_id=1, source_target_pairs={{0,16},{16,0},{1,17},{17,1},{2,18},{18,2},{3,19},{19,3},{4,20},{20... | collective-permute-start | bytes 4325384 | tf_op jit(solution)/shard_map/ppermute | solution.py:48
  197.7 39.5 %all-to-all-start.4 = ((bf16[4,128,2048]{2,1,0:T(8,128)(2,1)}), bf16[4,128,2048]{2,1,0:T(8,128)(2,1)}, u32[]{:S(2)}, u32[]{:S(2)}) async-start(bf16[4,128,2048]{2,1,0:T(8,128)(2,1)} %bitcast.24), calls=%async_computation.4 | async-start | bytes 4194304 | tf_op jit(solution)/shard_map/all_to_all | solution.py:64
  202.3 34.9 %collective-permute-start.16 = (bf16[512,2048]{1,0:T(8,128)(2,1)S(1)}, bf16[512,2048]{1,0:T(8,128)(2,1)}, u32[]{:S(2)}, u32[]{:S(2)}) collective-permute-start(bf16[512,2048]{1,0:T(8,128)(2,1)S(1)} %bitcast.94), channel_id=1, source_target_pairs={{0,4},{4,0},{1,5},{5,1},{2,6},{6,2},{3,7},{7,3},{8,12},{12,8},{9,1... | collective-permute-start | bytes 6291464 | tf_op jit(solution)/shard_map/ppermute | solution.py:60
  204.0 32.3 %collective-permute-start.18 = (bf16[2,2,64,1408]{3,2,1,0:T(8,128)(2,1)}, bf16[2,2,64,1408]{3,2,1,0:T(8,128)(2,1)S(1)}, u32[]{:S(2)}, u32[]{:S(2)}) collective-permute-start(bf16[2,2,64,1408]{3,2,1,0:T(8,128)(2,1)} %collective-permute-done.12.refs_2_), channel_id=1, source_target_pairs={{0,16},{16,0},{1,17},{17,1},{2,18},{18,2},{3,19},{19,3},{4,20},{20... | collective-permute-start | bytes 2162696 | tf_op jit(solution)/shard_map/ppermute | solution.py:48
  318.7 37.8 %all-to-all-start.6 = ((bf16[4,128,2048]{2,1,0:T(8,128)(2,1)}), bf16[4,128,2048]{2,1,0:T(8,128)(2,1)S(1)}, u32[]{:S(2)}, u32[]{:S(2)}) async-start(bf16[4,128,2048]{2,1,0:T(8,128)(2,1)} %bitcast.26), calls=%async_computation.6 | async-start | bytes 4194304 | tf_op jit(solution)/shard_map/all_to_all | solution.py:64
  362.7 43.6 %all-to-all-start.7 = ((bf16[4,128,2048]{2,1,0:T(8,128)(2,1)}), bf16[4,128,2048]{2,1,0:T(8,128)(2,1)S(1)}, u32[]{:S(2)}, u32[]{:S(2)}) async-start(bf16[4,128,2048]{2,1,0:T(8,128)(2,1)} %get-tuple-element.883), calls=%async_computation.7 | async-start | bytes 4194304 | tf_op jit(solution)/shard_map/all_to_all | solution.py:64
  368.9 35.4 %collective-permute-start.28 = (bf16[256,1408]{1,0:T(8,128)(2,1)}, bf16[256,1408]{1,0:T(8,128)(2,1)}, u32[]{:S(2)}, u32[]{:S(2)}) collective-permute-start(bf16[256,1408]{1,0:T(8,128)(2,1)} %add_convert_fusion.7), channel_id=1, source_target_pairs={{0,2},{2,0},{1,3},{3,1},{4,6},{6,4},{5,7},{7,5},{8,10},{10,8},{9,1... | collective-permute-start | bytes 2162696 | tf_op jit(solution)/shard_map/ppermute | solution.py:52
  370.6 33.7 %collective-permute-start.26 = (bf16[256,1408]{1,0:T(8,128)(2,1)}, bf16[256,1408]{1,0:T(8,128)(2,1)}, u32[]{:S(2)}, u32[]{:S(2)}) collective-permute-start(bf16[256,1408]{1,0:T(8,128)(2,1)} %get-tuple-element.892), channel_id=1, source_target_pairs={{0,16},{16,0},{1,17},{17,1},{2,18},{18,2},{3,19},{19,3},{4,20},{20... | collective-permute-start | bytes 2162696 | tf_op jit(solution)/shard_map/ppermute | solution.py:48
  418.6 44.5 %all-to-all-start.8 = ((bf16[4,128,2048]{2,1,0:T(8,128)(2,1)}), bf16[4,128,2048]{2,1,0:T(8,128)(2,1)S(1)}, u32[]{:S(2)}, u32[]{:S(2)}) async-start(bf16[4,128,2048]{2,1,0:T(8,128)(2,1)} %bitcast.28), calls=%async_computation.8 | async-start | bytes 4194304 | tf_op jit(solution)/shard_map/all_to_all | solution.py:64
  425.2 32.4 %collective-permute-start.32 = (bf16[176,2048]{1,0:T(8,128)(2,1)}, bf16[176,2048]{1,0:T(8,128)(2,1)}, u32[]{:S(2)}, u32[]{:S(2)}) collective-permute-start(bf16[176,2048]{1,0:T(8,128)(2,1)} %get-tuple-element.978), channel_id=1, source_target_pairs={{0,16},{16,0},{1,17},{17,1},{2,18},{18,2},{3,19},{19,3},{4,20},{20... | collective-permute-start | bytes 2162696 | tf_op jit(solution)/shard_map/ppermute | solution.py:48
  425.7 35.3 %collective-permute-start.33 = (bf16[256,1408]{1,0:T(8,128)(2,1)}, bf16[256,1408]{1,0:T(8,128)(2,1)}, u32[]{:S(2)}, u32[]{:S(2)}) collective-permute-start(bf16[256,1408]{1,0:T(8,128)(2,1)} %add_convert_fusion.8), channel_id=1, source_target_pairs={{0,2},{2,0},{1,3},{3,1},{4,6},{6,4},{5,7},{7,5},{8,10},{10,8},{9,1... | collective-permute-start | bytes 2162696 | tf_op jit(solution)/shard_map/ppermute | solution.py:52
  475.7 45.8 %all-to-all-start.9 = ((bf16[4,128,2048]{2,1,0:T(8,128)(2,1)}), bf16[4,128,2048]{2,1,0:T(8,128)(2,1)}, u32[]{:S(2)}, u32[]{:S(2)}) async-start(bf16[4,128,2048]{2,1,0:T(8,128)(2,1)} %bitcast.29), calls=%async_computation.9 | async-start | bytes 4194304 | tf_op jit(solution)/shard_map/all_to_all | solution.py:64
  483.8 33.6 %collective-permute-start.39 = (bf16[256,768]{1,0:T(8,128)(2,1)}, bf16[256,768]{1,0:T(8,128)(2,1)}, u32[]{:S(2)}, u32[]{:S(2)}) collective-permute-start(bf16[256,768]{1,0:T(8,128)(2,1)} %get-tuple-element.1054), channel_id=1, source_target_pairs={{0,16},{16,0},{1,17},{17,1},{2,18},{18,2},{3,19},{19,3},{4,20},{20... | collective-permute-start | bytes 1179656 | tf_op jit(solution)/shard_map/ppermute | solution.py:48
  484.4 35.0 %collective-permute-start.35 = (bf16[176,2048]{1,0:T(8,128)(2,1)}, bf16[176,2048]{1,0:T(8,128)(2,1)S(1)}, u32[]{:S(2)}, u32[]{:S(2)}) collective-permute-start(bf16[176,2048]{1,0:T(8,128)(2,1)} %add_convert_fusion.6), channel_id=1, source_target_pairs={{0,2},{2,0},{1,3},{3,1},{4,6},{6,4},{5,7},{7,5},{8,10},{10,8},{9,1... | collective-permute-start | bytes 2162696 | tf_op jit(solution)/shard_map/ppermute | solution.py:52
  521.5 47.1 %all-to-all-start.10 = ((bf16[8,64,1408]{2,1,0:T(8,128)(2,1)}), bf16[8,64,1408]{2,1,0:T(8,128)(2,1)S(1)}, u32[]{:S(2)}, u32[]{:S(2)}) async-start(bf16[8,64,1408]{2,1,0:T(8,128)(2,1)} %bitcast.30), calls=%async_computation.10 | async-start | bytes 2883584 | tf_op jit(solution)/shard_map/all_to_all | solution.py:743
  531.2 37.5 %collective-permute-start.43 = (bf16[512,768]{1,0:T(8,128)(2,1)}, bf16[512,768]{1,0:T(8,128)(2,1)}, u32[]{:S(2)}, u32[]{:S(2)}) collective-permute-start(bf16[512,768]{1,0:T(8,128)(2,1)} %pad_maximum_fusion.3), channel_id=1, source_target_pairs={{0,2},{2,0},{1,3},{3,1},{4,6},{6,4},{5,7},{7,5},{8,10},{10,8},{9,1... | collective-permute-start | bytes 2359304 | tf_op jit(solution)/shard_map/ppermute | solution.py:52
  (87 other events, 1231.9 us)

commit v3 on v2

v3 whole, which is shorter than its diff:
```python
import functools

import jax
import jax.numpy as jnp
import numpy as np
from jax import lax
from jax.experimental import pallas as pl
from jax.experimental.pallas import tpu as pltpu
from jax.sharding import Mesh
from jax.sharding import PartitionSpec as P

H = 32
HD = 64
ROT = 16

eps_norm = 1e-05
rope_base = 10000.0
masked_score = -1e30

F32 = jnp.float32
BF16 = jnp.bfloat16

SWAP = [(0, 1), (1, 0)]
EVERY = ("sb", "sx", "c", "fh", "fl")
MEMBERS = ("sx", "c", "fl")
QUAD = ("fl", "sx")
ANY = pl.BlockSpec(memory_space=pl.ANY)
SMEM = pl.BlockSpec(memory_space=pltpu.SMEM)
VMEM = pl.BlockSpec(memory_space=pltpu.VMEM)
NT = (((1,), (1,)), ((), ()))
TN = (((0,), (0,)), ((), ()))
LIMIT = 60 * 1024 * 1024


def params():
    return pltpu.CompilerParams(vmem_limit_bytes=LIMIT)


def cost(microseconds):
    return pl.CostEstimate(flops=int(microseconds * 1e9), bytes_accessed=1024, transcendentals=0)


def dot(a, b, dims=(((1,), (0,)), ((), ()))):
    return lax.dot_general(a, b, dims, preferred_element_type=F32)


def swap_sb(v):
    return lax.ppermute(v, "sb", SWAP)


def swap_fh(v):
    return lax.ppermute(v, "fh", SWAP)


def swap_fl(v):
    return lax.ppermute(v, "fl", SWAP)


def swap_c(v):
    return lax.ppermute(v, "c", SWAP)


def swap_sx(v, bit=1):
    n = lax.axis_size("sx")
    return lax.ppermute(v, "sx", [(i, i ^ bit) for i in range(n)])


def over_quad(v):
    return lax.all_to_all(v, QUAD, split_axis=0, concat_axis=0, tiled=True)


class Live(dict):
    def __getattr__(self, name):
        return self[name]

    def done(self, **new):
        self.update(new)
        self.update(lax.optimization_barrier(dict(self)))

    def drop(self, *names):
        for name in names:
            del self[name]


def normalize(values):
    average = jnp.mean(values, axis=-1, keepdims=True)
    centered = values - average
    inv_std = lax.rsqrt(jnp.mean(centered * centered, axis=-1, keepdims=True) + eps_norm)
    return centered * inv_std, inv_std


def normalize_back(grad_normed, normed, inv_std):
    first_mean = jnp.mean(grad_normed, axis=-1, keepdims=True)
    second_mean = jnp.mean(grad_normed * normed, axis=-1, keepdims=True)
    return inv_std * (grad_normed - first_mean - normed * second_mean)


def gather_first(x):
    return (x, swap_sx(x), swap_fl(x), swap_c(x))


def gather_second(first):
    n_sx = lax.axis_size("sx")
    x, a, b, xo = first
    h = x.shape[0] // 2
    d1 = swap_fl(a[:h])
    d2 = swap_sx(b[h:])
    ao = swap_c(a)
    bo = swap_c(b)
    got = [x, a, b, d1, d2, xo, ao, bo, swap_c(d1), swap_c(d2)]
    bit = 2
    while bit < n_sx:
        got = got + [swap_sx(v, bit) for v in got]
        bit *= 2
    return got


def gather_rows(n_sx, m):
    h = m // 2
    got = []
    for c in range(2):
        at = c * n_sx * m
        over = 2 * n_sx * m + at
        got += [at, at + m, over, over + m, over + m + h]
    bit = 2
    while bit < n_sx:
        got = got + [r + bit * m for r in got]
        bit *= 2
    return got


def add_first_kernel(keep, got, send_x, send_l, keep_x, keep_l):
    h = keep.shape[2] // 2
    for f in range(2):
        for x in range(2):
            q = keep[f, x].astype(F32) + got[f, x].astype(F32)
            if x == 1:
                send_x[f] = q[:h].astype(BF16)
            else:
                keep_x[f] = q[:h]
            if f == 1:
                send_l[x] = q[h:].astype(BF16)
            else:
                keep_l[x] = q[h:]


def add_second_kernel(keep_x, got_x, keep_l, got_l, send_x, send_l, own_x, own_l):
    own_x[...] = keep_x[0] + got_x[0].astype(F32)
    own_l[...] = keep_l[0] + got_l[0].astype(F32)
    send_x[...] = (keep_x[1] + got_x[1].astype(F32)).astype(BF16)
    send_l[...] = (keep_l[1] + got_l[1].astype(F32)).astype(BF16)


def add_first(keep, got):
    bit = keep.shape[1] // 2
    while bit >= 2:
        q = keep.astype(F32) + got.astype(F32)
        keep = q[:, :bit].astype(BF16)
        got = swap_sx(q[:, bit:].astype(BF16), bit)
        bit //= 2
    m, D = keep.shape[2:]
    h = m // 2
    low = jax.ShapeDtypeStruct((2, h, D), BF16)
    high = jax.ShapeDtypeStruct((2, h, D), F32)
    return pl.pallas_call(
        add_first_kernel,
        out_shape=[low, low, high, high],
        in_specs=[VMEM] * 2,
        out_specs=[VMEM] * 4,
        compiler_params=params(),
        cost_estimate=cost(4),
    )(keep, got)


def add_second(keep_x, got_x, keep_l, got_l):
    _, h, D = keep_x.shape
    return pl.pallas_call(
        add_second_kernel,
        out_shape=[jax.ShapeDtypeStruct((h, D), BF16)] * 2 + [jax.ShapeDtypeStruct((h, D), F32)] * 2,
        in_specs=[VMEM] * 4,
        out_specs=[VMEM] * 4,
        compiler_params=params(),
        cost_estimate=cost(3),
    )(keep_x, got_x, keep_l, got_l)


def in_order(pieces, sb, fh):
    w, z, y, yz = pieces
    a, b = jnp.where(fh == 1, z, w), jnp.where(fh == 1, w, z)
    c, d = jnp.where(fh == 1, yz, y), jnp.where(fh == 1, y, yz)
    first = jnp.stack([jnp.where(sb == 1, c, a), jnp.where(sb == 1, d, b)])
    second = jnp.stack([jnp.where(sb == 1, a, c), jnp.where(sb == 1, b, d)])
    return jnp.stack([first, second])


def flip_if(bit, v, axis):
    return jnp.where(bit == 1, lax.rev(v, (axis,)), v)


def xor_order(v, axis, index, n):
    shape = v.shape
    bit = 1
    while bit < n:
        r = v.reshape(shape[:axis] + (n // (2 * bit), 2, bit) + shape[axis + 1 :])
        v = flip_if((index // bit) % 2, r, axis + 1).reshape(shape)
        bit *= 2
    return v


def load_groups(sc, pieces, places, buf, sems, first=0, start=True):
    copies = []
    rows = buf.shape[4]
    for n, (piece, (k, r)) in enumerate(zip(pieces, places)):
        where = buf.at[sc[0] ^ (k // 2), pl.ds(r, piece.shape[0]), sc[1] ^ (k % 2)]
        copies.append(pltpu.make_async_copy(piece.at[:, :, pl.ds(first, rows)], where, sems.at[n]))
    for c in copies if start else ():
        c.start()
    return copies


def load_down(sc, pieces, places, buf, sems, start=True):
    copies = []
    for n, (piece, (k, r)) in enumerate(zip(pieces, places)):
        where = buf
        if len(places) > 1:
            where = buf.at[sc[0] ^ (k // 2), sc[1] ^ (k % 2), pl.ds(r, piece.shape[0])]
        copies.append(pltpu.make_async_copy(piece, where, sems.at[n]))
    for c in copies if start else ():
        c.start()
    return copies


class Rows:
    def __init__(self, arrays, firsts):
        self.arrays, self.firsts = list(arrays), firsts
        self.N, self.D = sum(v.shape[0] for v in arrays), arrays[0].shape[1]

    def scratch(self):
        return [pltpu.VMEM((self.N, self.D), BF16), pltpu.SemaphoreType.DMA((len(self.arrays),))]

    def load(self, sc, refs, buf, sems, start=True):
        copies = [
            pltpu.make_async_copy(ref, buf.at[pl.ds(r, ref.shape[0])], sems.at[n])
            for n, (ref, r) in enumerate(zip(refs, self.firsts))
        ]
        for c in copies if start else ():
            c.start()
        return copies


class Quads:
    def __init__(self, mine, other, m):
        self.arrays, self.m = [mine, other], m
        self.N, self.D = 2 * mine.shape[0], mine.shape[1]
        self.n_sx = mine.shape[0] // (2 * m)

    def scratch(self):
        return [pltpu.VMEM((self.N, self.D), BF16), pltpu.SemaphoreType.DMA((4 * self.n_sx,))]

    def load(self, sc, refs, buf, sems, start=True):
        copies = []
        for k in range(2):
            for f in range(2):
                for x in range(self.n_sx):
                    to = ((2 * (f ^ sc[2]) + k) * self.n_sx + (x ^ sc[3])) * self.m
                    copies.append(
                        pltpu.make_async_copy(
                            refs[k].at[pl.ds((f * self.n_sx + x) * self.m, self.m)],
                            buf.at[pl.ds(pl.multiple_of(to, self.m), self.m)],
                            sems.at[len(copies)],
                        )
                    )
        for c in copies if start else ():
            c.start()
        return copies


def sides(nb, by_index=False):
    def place(f, b, sc):
        if by_index:
            f, b = f ^ sc[2], b ^ (sc[3] // 2)
        return f * nb + b

    def keep(i, sc=None):
        f, k, b = i // (2 * nb), lax.rem(i // nb, 2), lax.rem(i, nb)
        return place(f, jnp.where(k == 0, b, nb - 1), sc)

    def send(i, sc=None):
        f, k, b = i // (2 * nb), lax.rem(i // nb, 2), lax.rem(i, nb)
        return place(f, jnp.where(k == 0, 0, b), sc)

    return keep, send


def columns_kernel(plan, n_in, *refs):
    ins, vectors, out = refs[:n_in], refs[n_in:-1], refs[-1]
    rows = ins[0].shape[0]
    if vectors:
        row = jnp.concatenate([v[...] for v in vectors], axis=-1)
    for t, ranges in enumerate(plan):
        out[t, :rows] = jnp.concatenate([ins[i][:, a : a + n] for i, a, n in ranges], axis=-1)
        if vectors:
            out[t, rows : rows + 1, : row.shape[1]] = row


def columns(arrays, plan, vectors=()):
    width = sum(n for _, _, n in plan[0])
    rows = arrays[0].shape[0] + (8 if vectors else 0)
    return pl.pallas_call(
        functools.partial(columns_kernel, plan, len(arrays)),
        out_shape=jax.ShapeDtypeStruct((len(plan), rows, width), arrays[0].dtype),
        in_specs=[VMEM] * (len(arrays) + len(vectors)),
        out_specs=VMEM,
        compiler_params=params(),
        cost_estimate=cost(3),
    )(*arrays, *vectors)


def uncolumns_kernel(plan, *refs):
    ins, out = refs[:-1], refs[-1]
    width = ins[0].shape[2]
    if True:
        at, group, size = 0, [], 0
        for t, b, n in plan:
            group.append(ins[b // width][t, :, b % width : b % width + n].astype(F32))
            size += n
            if size % 128 == 0:
                out[:, at : at + size] = jnp.concatenate(group, axis=-1)
                at, group, size = at + size, [], 0
        if group:
            out[:, at : at + size] = jnp.concatenate(group, axis=-1)


def uncolumns(arrays, plan):
    rows = arrays[0].shape[1]
    return pl.pallas_call(
        functools.partial(uncolumns_kernel, plan),
        out_shape=jax.ShapeDtypeStruct((rows, sum(n for _, _, n in plan)), F32),
        in_specs=[VMEM] * len(arrays),
        out_specs=VMEM,
        compiler_params=params(),
        cost_estimate=cost(3),
    )(*arrays)


def turn(v, c_ref_value, sa, sb_, direction):
    width = v.shape[1]
    back = pltpu.roll(v, ROT // 2, 1)
    front = pltpu.roll(v, width - ROT // 2, 1)
    return v * c_ref_value + direction * (back * sa + front * sb_)


def attention_kernel(dims, places, x_rows, sc, tables, id_row, id_col, w_out, *refs):
    heads, length, block, D = dims
    x_refs, refs = refs[: len(x_rows.arrays)], refs[len(x_rows.arrays) :]
    w_refs, refs = refs[: len(places)], refs[len(places) :]
    h1, q, k, v, o, lse, keep, send, vectors, w, sems, small, small_sems, bias_q, x_buf, x_sems = refs
    wide = heads * HD
    per = length // block
    i = pl.program_id(0)

    @pl.when(i == 0)
    def _():
        n_sr, rows_ = w.shape[1], w.shape[4]
        copies = x_rows.load(sc, x_refs, x_buf, x_sems)
        copies += load_groups(sc, w_refs, places, small, small_sems, rows_)
        for c in load_groups(sc, w_refs, places, w, sems) + copies:
            c.wait()
        every = [(s, j, f, l) for s in range(2) for j in range(n_sr) for f in range(2) for l in range(2)]
        for n in range(4):
            row = [small[s, j, f, l, 0:1, n * rows_ : (n + 1) * rows_] for s, j, f, l in every]
            vectors[n : n + 1, :] = jnp.concatenate(row, axis=-1).astype(F32)
        first = 4 * rows_
        if 3 * rows_ == 3 * HD:
            row = [
                small[a // 2, sc[4], a % 2, sc[2], 0:1, first + p * HD : first + (p + 1) * HD]
                for p in range(3)
                for a in range(heads)
            ]
        else:
            count = 3 * HD // (3 * rows_)
            row = []
            for a in range(heads):
                for n in range(count):
                    d = ((sc[4] * 2 + sc[2]) * heads + a) * count + n
                    at = (d // (4 * n_sr), lax.rem(d // 4, n_sr), lax.rem(d // 2, 2), lax.rem(d, 2))
                    row.append(small[at[0], at[1], at[2], at[3], 0:1, first : first + 3 * rows_])
        bias_q[...] = jnp.concatenate(row, axis=-1).astype(F32)

    rows = pl.ds(pl.multiple_of(i * block, block), block)
    normed, _ = normalize(x_buf[rows, :].astype(F32))
    h = (normed * vectors[0:1, :] + vectors[1:2, :]).astype(BF16)
    h1[...] = h
    lin = dot(h, w[...].reshape(D, 3 * wide)) + bias_q[...]
    qk = turn(lin[:, : 2 * wide], tables[0], tables[1], tables[2], 1.0)
    q[rows, :] = qk[:, :wide].astype(BF16)
    k[rows, :] = qk[:, wide:].astype(BF16)
    v[rows, :] = lin[:, 2 * wide :].astype(BF16)

    @pl.when(lax.rem(i, per) == per - 1)
    def _():
        s = i // per
        start = pl.multiple_of(s * length, length)
        step = min(length, (1 << 18) // length)
        for r in range(length // step):
            part = pl.ds(pl.multiple_of(start + r * step, step), step)
            allowed = id_col[part, 0:1] >= id_row[pl.ds(s, 1), :]
            for hd in range(heads):
                lanes = slice(hd * HD, (hd + 1) * HD)
                kh = k[pl.ds(start, length), lanes]
                vh = v[pl.ds(start, length), lanes]
                score = dot(q[part, lanes], kh, NT) * (HD**-0.5)
                score = jnp.where(allowed, score, masked_score)
                peak = jnp.max(score, axis=-1, keepdims=True)
                e = jnp.exp(score - peak)
                total = jnp.sum(e, axis=-1, keepdims=True)
                p = (e * (1.0 / total)).astype(BF16)
                o[part, lanes] = dot(p, vh).astype(BF16)
                lse[part, hd : hd + 1] = peak + jnp.log(total)
        for side, out in enumerate((keep, send)):
            for b in range(per // 2):
                part = pl.ds(pl.multiple_of(start + (side * (per // 2) + b) * block, block), block)
                out[0, b * block : (b + 1) * block] = dot(o[part, :], w_out[...]).astype(BF16)


def attention(sc, x_rows, tables, id_row, id_col, w_out, weight, heads, rows):
    N, D = x_rows.N, x_rows.D
    length = N // 2
    block = 256
    per = length // block
    wide = heads * HD
    n_sr, _, _, f = weight[0][0].shape
    places = [p[1:] for p in weight]
    whole = lambda shape: pl.BlockSpec(shape, lambda i, sc: (0,) * len(shape))
    side = pl.BlockSpec((1, length // 2, D), lambda i, sc: (i // per, 0, 0))
    spec = pltpu.PrefetchScalarGridSpec(
        num_scalar_prefetch=1,
        grid=(N // block,),
        in_specs=[
            pl.BlockSpec((3, block, 2 * wide), lambda i, sc: (0, lax.rem(i, per), 0)),
            whole((2, length)),
            whole((N, 1)),
            whole((wide, D)),
        ]
        + [ANY] * (len(x_rows.arrays) + len(places)),
        out_specs=[pl.BlockSpec((block, D), lambda i, sc: (i, 0))]
        + [whole((N, wide))] * 4
        + [whole((N, heads)), side, side, whole((4, D))],
        scratch_shapes=[
            pltpu.VMEM((2, n_sr, 2, 2, rows, f), BF16),
            pltpu.SemaphoreType.DMA((len(places),)),
            pltpu.VMEM((2, n_sr, 2, 2, 8, f), BF16),
            pltpu.SemaphoreType.DMA((len(places),)),
            pltpu.VMEM((1, 3 * wide), F32),
        ]
        + x_rows.scratch(),
    )
    return pl.pallas_call(
        functools.partial(attention_kernel, (heads, length, block, D), places, x_rows),
        grid_spec=spec,
        out_shape=[jax.ShapeDtypeStruct((N, D), BF16)]
        + [jax.ShapeDtypeStruct((N, wide), BF16)] * 4
        + [jax.ShapeDtypeStruct((N, heads), F32)]
        + [jax.ShapeDtypeStruct((2, length // 2, D), BF16)] * 2
        + [jax.ShapeDtypeStruct((4, D), F32)],
        compiler_params=params(),
        cost_estimate=cost(25),
    )(sc, tables, id_row, id_col, w_out, *x_rows.arrays, *[p[0] for p in weight])


def ffn_kernel(dims, h_rows, dy_rows, sc, *refs):
    g_list, d_list, block, nb, D, ff = dims
    h_refs, refs = refs[: len(h_rows.arrays)], refs[len(h_rows.arrays) :]
    dy_refs, refs = refs[: len(dy_rows.arrays)], refs[len(dy_rows.arrays) :]
    g_refs, refs = refs[: len(g_list)], refs[len(g_list) :]
    d_refs, refs = refs[: len(d_list)], refs[len(d_list) :]
    h2, act, d_gu, keep, send, g_buf, d_buf, sem_g, sem_d, h_buf, h_sems, dy_buf, dy_sems = refs
    i = pl.program_id(0)
    rows = pl.ds(pl.multiple_of(i * block, block), block)

    @pl.when(i == 0)
    def _():
        first = h_rows.load(sc, h_refs, h_buf, h_sems) + load_groups(sc, g_refs, g_list, g_buf, sem_g)
        dy_rows.load(sc, dy_refs, dy_buf, dy_sems)
        load_down(sc, d_refs, d_list, d_buf, sem_d)
        for c in first:
            c.wait()

    h = h_buf[rows, :]
    h2[...] = h
    w_gu = g_buf[...].reshape(D, 2 * ff)
    gu = dot(h, w_gu)
    g, u = gu[:, :ff], gu[:, ff:]
    s = jax.nn.sigmoid(g)
    silu = g * s
    act[...] = (silu * u).astype(BF16)

    @pl.when(i == 0)
    def _():
        second = dy_rows.load(sc, dy_refs, dy_buf, dy_sems, False)
        for c in second + load_down(sc, d_refs, d_list, d_buf, sem_d, False):
            c.wait()

    d_act = dot(dy_buf[rows, :], d_buf[...].reshape(ff, D), NT)
    d_g = (d_act * u * s * (1.0 + g * (1.0 - s))).astype(BF16)
    d_u = (d_act * silu).astype(BF16)
    d = jnp.concatenate([d_g, d_u], axis=-1)
    d_gu[...] = d
    d_h = dot(d, w_gu, NT).astype(BF16)
    side = lax.rem(i // nb, 2)

    @pl.when(side == 0)
    def _():
        keep[...] = d_h

    @pl.when(side == 1)
    def _():
        send[...] = d_h


def ffn(sc, h_rows, dy_rows, gu, down, down_places, rows_):
    N, D = h_rows.N, h_rows.D
    block = 256
    nb = N // 4 // block
    n_sr, _, _, two_ff = gu[0][0].shape
    ff = two_ff // 2
    rows = lambda width: pl.BlockSpec((block, width), lambda i, sc: (i, 0))
    d_shape = (2, 2, ff // 4, D) if len(down) > 1 else (ff, D)
    keep, send = sides(nb)
    spec = pltpu.PrefetchScalarGridSpec(
        num_scalar_prefetch=1,
        grid=(N // block,),
        in_specs=[ANY] * (len(h_rows.arrays) + len(dy_rows.arrays) + len(gu) + len(down)),
        out_specs=[
            rows(D),
            rows(ff),
            rows(2 * ff),
            pl.BlockSpec((block, D), lambda i, sc: (keep(i), 0)),
            pl.BlockSpec((block, D), lambda i, sc: (send(i), 0)),
        ],
        scratch_shapes=[
            pltpu.VMEM((2, n_sr, 2, 2, rows_, two_ff), BF16),
            pltpu.VMEM(d_shape, BF16),
            pltpu.SemaphoreType.DMA((len(gu),)),
            pltpu.SemaphoreType.DMA((len(down),)),
        ]
        + h_rows.scratch()
        + dy_rows.scratch(),
    )
    dims = ([p[1:] for p in gu], down_places, block, nb, D, ff)
    return pl.pallas_call(
        functools.partial(ffn_kernel, dims, h_rows, dy_rows),
        grid_spec=spec,
        out_shape=[
            jax.ShapeDtypeStruct((N, D), BF16),
            jax.ShapeDtypeStruct((N, ff), BF16),
            jax.ShapeDtypeStruct((N, 2 * ff), BF16),
            jax.ShapeDtypeStruct((N // 2, D), BF16),
            jax.ShapeDtypeStruct((N // 2, D), BF16),
        ],
        compiler_params=params(),
        cost_estimate=cost(30),
    )(sc, *h_rows.arrays, *dy_rows.arrays, *[p[0] for p in gu], *down)


def down_kernel(d_list, nb, ff, D, sc, act, *refs):
    n_d = len(d_list)
    d_refs, (keep, send, d_buf, sem) = refs[:n_d], refs[n_d:]
    i = pl.program_id(0)

    @pl.when(i == 0)
    def _():
        for c in load_down(sc, d_refs, d_list, d_buf, sem):
            c.wait()

    y = dot(act[...], d_buf[...].reshape(ff, D)).astype(BF16)
    side = lax.rem(i // nb, 2)
    m = y.shape[0] // 2
    for k, out in enumerate((keep, send)):
        for t in range(2):

            @pl.when((side == k) & (lax.rem(sc[3], 2) == t))
            def _():
                out[t * m : (t + 1) * m, :] = y[:m]
                out[(1 - t) * m : (2 - t) * m, :] = y[m:]


def down_product(sc, act, down, places):
    N, ff = act.shape
    D = down[0].shape[-1]
    block = 256
    nb = N // 4 // block
    d_shape = (2, 2, ff // 4, D) if len(down) > 1 else (ff, D)
    keep, send = sides(nb, by_index=True)
    spec = pltpu.PrefetchScalarGridSpec(
        num_scalar_prefetch=1,
        grid=(N // block,),
        in_specs=[pl.BlockSpec((block, ff), lambda i, sc: (i, 0))] + [ANY] * len(down),
        out_specs=[
            pl.BlockSpec((block, D), lambda i, sc: (keep(i, sc), 0)),
            pl.BlockSpec((block, D), lambda i, sc: (send(i, sc), 0)),
        ],
        scratch_shapes=[pltpu.VMEM(d_shape, BF16), pltpu.SemaphoreType.DMA((len(down),))],
    )
    return pl.pallas_call(
        functools.partial(down_kernel, places, nb, ff, D),
        grid_spec=spec,
        out_shape=[jax.ShapeDtypeStruct((N // 2, D), BF16)] * 2,
        compiler_params=params(),
        cost_estimate=cost(9),
    )(sc, act, *down)


def h_buf_rows(length):
    return 256 if length <= 1024 else 128


def attention_back_kernel(dims, d_rows, sc, tables, id_row, id_col, q, k, v, lse, w_out, h1, vectors, *refs):
    heads, length, N, D, w_list = dims
    block = h_buf_rows(length)
    d_refs, refs = refs[: len(d_rows.arrays)], refs[len(d_rows.arrays) :]
    w_refs, refs = refs[: len(w_list)], refs[len(w_list) :]
    d_lin, bias_grad, sums, keep, send, w, d_o, d_qk, sem_w, h_buf, sem_h, d_att, sem_d = refs
    wide = heads * HD
    copies = d_rows.load(sc, d_refs, d_att, sem_d)
    loads = load_groups(sc, w_refs, w_list, w, sem_w)
    h_loads = [
        pltpu.make_async_copy(h1.at[pl.ds(n * block, block)], h_buf.at[n % 2], sem_h.at[n % 2])
        for n in range(N // block)
    ]
    h_loads[0].start()
    for c in copies:
        c.wait()
    sums[...] = jnp.zeros_like(sums)
    step = min(length, (1 << 18) // length)
    scale = HD**-0.5
    bias_grad[...] = jnp.zeros_like(bias_grad)
    for s in range(2):
        start = s * length
        for r in range(length // step):
            at = pl.ds(start + r * step, step)
            d_o[pl.ds(r * step, step), :] = dot(d_att[at, :], w_out[...], NT).astype(BF16)
        d_qk[:, wide:] = jnp.zeros_like(d_qk[:, wide:])
        for hd in range(heads):
            lanes = slice(hd * HD, (hd + 1) * HD)
            k_lanes = slice(wide + hd * HD, wide + (hd + 1) * HD)
            v_lanes = slice(2 * wide + hd * HD, 2 * wide + (hd + 1) * HD)
            kh = k[pl.ds(start, length), lanes]
            vh = v[pl.ds(start, length), lanes]
            for r in range(length // step):
                part = pl.ds(start + r * step, step)
                local = pl.ds(r * step, step)
                allowed = id_col[part, 0:1] >= id_row[s : s + 1, :]
                qh = q[part, lanes]
                score = dot(qh, kh, NT) * scale
                p = jnp.where(allowed, jnp.exp(score - lse[part, hd : hd + 1]), 0.0)
                doh = d_o[local, lanes]
                dp = dot(doh, vh, NT)
                inner = jnp.sum(p * dp, axis=-1, keepdims=True)
                ds = (p * (dp - inner)).astype(BF16)
                d_qk[local, lanes] = dot(ds, kh) * scale
                dk = dot(ds, qh, TN) * scale
                dv = dot(p.astype(BF16), doh, TN)
                if length == step:
                    d_qk[:, k_lanes] = dk
                    d_qk[:, v_lanes] = dv
                else:
                    d_qk[:, k_lanes] += dk
                    d_qk[:, v_lanes] += dv
        if s == 0:
            for c in loads:
                c.wait()
        half = length // 2
        for b in range(length // block):
            local = pl.ds(b * block, block)
            at = pl.ds(start + b * block, block)
            qk = turn(d_qk[local, : 2 * wide], tables[0, local], tables[1, local], tables[2, local], -1.0)
            lin = jnp.concatenate([qk, d_qk[local, 2 * wide :]], axis=-1).astype(BF16)
            d_lin[at, :] = lin
            bias_grad[...] += jnp.sum(lin.astype(F32), axis=0, keepdims=True)
            d_h = dot(lin, w[...].reshape(D, 3 * wide), NT)
            n = (start + b * block) // block
            h_loads[n].wait()
            if n + 1 < N // block:
                h_loads[n + 1].start()
            sums[0:1, :] += jnp.sum(d_h * h_buf[n % 2].astype(F32), axis=0, keepdims=True)
            sums[1:2, :] += jnp.sum(d_h, axis=0, keepdims=True)
            d_h = d_h.astype(BF16)
            out = keep if b * block < half else send
            out[pl.ds(s * half + (b * block) % half, block), :] = d_h
    sums[0:1, :] = (sums[0:1, :] - vectors[1:2, :] * sums[1:2, :]) / vectors[0:1, :]


def attention_back(sc, tables, id_row, id_col, q, k, v, lse, w_out, h1, vectors, d_rows, weight):
    N, wide = q.shape
    D = w_out.shape[1]
    heads = wide // HD
    length = N // 2
    n_sr, _, _, f = weight[0][0].shape
    rows = D // (8 * n_sr)
    dims = (heads, length, N, D, [p[1:] for p in weight])
    return pl.pallas_call(
        functools.partial(attention_back_kernel, dims, d_rows),
        out_shape=[
            jax.ShapeDtypeStruct((N, 3 * wide), BF16),
            jax.ShapeDtypeStruct((1, 3 * wide), F32),
            jax.ShapeDtypeStruct((2, D), F32),
            jax.ShapeDtypeStruct((N // 2, D), BF16),
            jax.ShapeDtypeStruct((N // 2, D), BF16),
        ],
        in_specs=[SMEM] + [VMEM] * 8 + [ANY, VMEM] + [ANY] * (len(d_rows.arrays) + len(weight)),
        out_specs=[VMEM] * 5,
        scratch_shapes=[
            pltpu.VMEM((2, n_sr, 2, 2, rows, f), BF16),
            pltpu.VMEM((length, wide), BF16),
            pltpu.VMEM((length, 3 * wide), F32),
            pltpu.SemaphoreType.DMA((len(weight),)),
            pltpu.VMEM((2, h_buf_rows(length), D), BF16),
            pltpu.SemaphoreType.DMA((2,)),
        ]
        + d_rows.scratch(),
        compiler_params=params(),
        cost_estimate=cost(23),
    )(sc, tables, id_row, id_col, q, k, v, lse, w_out, h1, vectors, *d_rows.arrays, *[p[0] for p in weight])


def rows_kernel(dims, sc, h, d, *outs):
    n, two_rows = dims
    t = dot(h[...], d[...], TN).astype(BF16)
    i = pl.program_id(0)
    others, same = outs[:-1], outs[-1]
    for f in range(2):
        places = [(same, sc[1] == f)]
        for k, other in enumerate(others):
            places.append((other, (sc[1] != f) if len(others) == 1 else (sc[1] != f) & (i == k)))
        for out, here in places:

            @pl.when(here)
            def _():
                for j in range(n):
                    r = (2 * j + f) * two_rows
                    out[j * two_rows : (j + 1) * two_rows, :] = t[r : r + two_rows]


def grad_rows(sc, h, d, side, n_sr, rows, parts=2):
    N, D = h.shape
    f = d.shape[1]
    cut = D // 4
    n = n_sr // 2
    half, whole = pl.BlockSpec((cut // 2, f), lambda i, sc: (0, 0)), pl.BlockSpec((cut // 2, f), lambda i, sc: (i, 0))
    shape = lambda r: jax.ShapeDtypeStruct((r, f), BF16)
    spec = pltpu.PrefetchScalarGridSpec(
        num_scalar_prefetch=1,
        grid=(2,),
        in_specs=[
            pl.BlockSpec((N, cut), lambda i, sc: (0, (sc[0] ^ side) * 2 + i)),
            pl.BlockSpec((N, f), lambda i, sc: (0, 0)),
        ],
        out_specs=([half] * 2 if parts == 2 else [whole]) + [whole],
    )
    return pl.pallas_call(
        functools.partial(rows_kernel, (n, 2 * rows)),
        grid_spec=spec,
        out_shape=([shape(cut // 2)] * 2 if parts == 2 else [shape(cut)]) + [shape(cut)],
        compiler_params=params(),
        cost_estimate=cost(7),
    )(sc, h, d)


def slices_kernel(rows, cut, d_rows, sc, a, *refs):
    d_refs, refs = refs[: len(d_rows.arrays)], refs[len(d_rows.arrays) :]
    outs, (buf, sems) = refs[:4], refs[4:]
    i = pl.program_id(0)

    @pl.when(i == 0)
    def _():
        for c in d_rows.load(sc, d_refs, buf, sems):
            c.wait()

    d = buf[:, pl.ds(pl.multiple_of(i * cut, cut), cut)]
    t = dot(a[...], d, TN).astype(BF16)
    for n in range(4):
        for k in range(4):

            @pl.when((sc[0] == (n // 2) ^ (k // 2)) & (sc[1] == (n % 2) ^ (k % 2)))
            def _():
                outs[k][...] = t[n * rows : (n + 1) * rows]


def grad_slices(sc, a, d_rows):
    N, f = a.shape
    D = d_rows.D
    cut = D // 4
    spec = pltpu.PrefetchScalarGridSpec(
        num_scalar_prefetch=1,
        grid=(D // cut,),
        in_specs=[pl.BlockSpec((N, f), lambda i, sc: (0, 0))] + [ANY] * len(d_rows.arrays),
        out_specs=[pl.BlockSpec((f // 4, cut), lambda i, sc: (0, i))] * 4,
        scratch_shapes=d_rows.scratch(),
    )
    return pl.pallas_call(
        functools.partial(slices_kernel, f // 4, cut, d_rows),
        grid_spec=spec,
        out_shape=[jax.ShapeDtypeStruct((f // 4, D), BF16)] * 4,
        compiler_params=params(),
        cost_estimate=cost(9),
    )(sc, a, *d_rows.arrays)


def total_of(u0, u1, w0, w1):
    return jnp.concatenate([u0[...] + u1[...].astype(F32), w0[...] + w1[...].astype(F32)], axis=0)


def forward_kernel(u0, u1, w0, w1, x, vectors, x2, low):
    v = x[...].astype(F32) + total_of(u0, u1, w0, w1)
    x2[...] = v
    normed, _ = normalize(v)
    low[...] = (normed * vectors[2:3, :] + vectors[3:4, :]).astype(BF16)


def norm_step(terms, x, vectors):
    m, D = x.shape
    return pl.pallas_call(
        forward_kernel,
        out_shape=[jax.ShapeDtypeStruct((m, D), F32), jax.ShapeDtypeStruct((m, D), BF16)],
        in_specs=[VMEM] * 6,
        out_specs=[VMEM] * 2,
        compiler_params=params(),
        cost_estimate=cost(4),
    )(*terms, x, vectors)


def back_kernel(which, u0, u1, w0, w1, x, dy, vectors, grad, low, sums):
    d_h = total_of(u0, u1, w0, w1)
    normed, inv_std = normalize(x[...].astype(F32))
    total = dy[...].astype(F32) + normalize_back(d_h * vectors[which : which + 1, :], normed, inv_std)
    grad[...] = total
    low[...] = total.astype(BF16)
    sums[0:1, :] = jnp.sum(d_h * normed, axis=0, keepdims=True)
    sums[1:2, :] = jnp.sum(d_h, axis=0, keepdims=True)


def norm_step_back(terms, x, dy, vectors, which):
    m, D = x.shape
    return pl.pallas_call(
        functools.partial(back_kernel, which),
        out_shape=[
            jax.ShapeDtypeStruct((m, D), F32),
            jax.ShapeDtypeStruct((m, D), BF16),
            jax.ShapeDtypeStruct((2, D), F32),
        ],
        in_specs=[VMEM] * 7,
        out_specs=[VMEM] * 3,
        compiler_params=params(),
        cost_estimate=cost(4),
    )(*terms, x, dy, vectors)


def shards(
    inputs,
    cotangent,
    block_ids,
    ln1_gain,
    ln1_bias,
    qkv_weight,
    qkv_bias,
    out_weight,
    ln2_gain,
    ln2_bias,
    gate_weight,
    up_weight,
    down_weight,
):
    sb, sx, c, fh, fl = (lax.axis_index(a).astype(jnp.int32) for a in EVERY)
    n_sx = lax.axis_size("sx")
    sr, n_sr = sx * 2 + c, 2 * n_sx
    quad = 2 * n_sx
    n_dev = 8 * n_sr
    members = 2 * n_sr
    tok = inputs.shape[2]
    m = 2 * tok
    D = inputs.shape[3]
    length = block_ids.shape[2]
    N = 2 * length
    rows = qkv_weight.shape[0]
    ff_rows = down_weight.shape[0]
    ff = 4 * ff_rows
    heads = H // members
    wide = heads * HD
    natural = H % n_dev == 0
    sc = jnp.stack([sb, fh, fl, sx, sr])

    def pick(v, i):
        return lax.dynamic_index_in_dim(v, i, 0, keepdims=False)

    def device_of(t, a):
        return (((a // 2) * n_sr + t // 2) * 2 + a % 2) * 2 + t % 2

    def head_of(t, i):
        return device_of(t, i) if natural else t * heads + i

    qkv_plan = [
        [(0, (head_of(t, i) * 3 + part) * HD, HD) for part in range(3) for i in range(heads)]
        for t in range(members)
    ]
    gu_plan = [
        [(w, device_of(t, a) * ff_rows, ff_rows) for w in range(2) for a in range(4)]
        for t in range(members)
    ]
    head_place = {head_of(t, i): (t, i) for t in range(members) for i in range(heads)}
    qkv_back = [
        (head_place[h][0], part * wide + head_place[h][1] * HD, HD) for h in range(H) for part in range(3)
    ]
    ff_place = {device_of(t, a): (t, a) for t in range(members) for a in range(4)}
    gate_back = [(ff_place[d][0], ff_place[d][1] * ff_rows, ff_rows) for d in range(n_dev)]
    up_back = [(t, ff + b, n) for t, b, n in gate_back]

    def exchange(v):
        return lax.all_to_all(v, MEMBERS, split_axis=0, concat_axis=0, tiled=True)

    def of_rows(v):
        return v.reshape((n_sr, 2) + v.shape[1:])

    def both(bit, own, other):
        return jnp.stack([jnp.where(bit == 0, own, other), jnp.where(bit == 0, other, own)])

    my_ids = pick(block_ids, sb)
    c_of = (jnp.arange(2, dtype=jnp.int32) ^ c)[:, None, None, None]
    sx_of = (jnp.arange(n_sx, dtype=jnp.int32) ^ sx)[None, :, None, None]
    sb_of = (jnp.arange(2, dtype=jnp.int32) ^ sb)[None, None, :, None]
    pos = ((sb_of * n_sx + sx_of) * 2 + c_of) * tok + jnp.arange(tok, dtype=jnp.int32)[None, None, None, :]
    pos = pos.reshape(-1)
    half = ROT // 2
    lane = np.arange(2 * wide) % HD
    turned = lane < ROT
    frequency = np.where(turned, rope_base ** (-2.0 * (lane % half).astype(np.float32) / ROT), 0.0)
    angles = pos.astype(F32)[:, None] * jnp.asarray(frequency, F32)[None, :]
    sine = jnp.sin(angles)
    to_back = jnp.asarray(np.where(turned & (lane >= half), 1.0, 0.0), F32)
    to_front = jnp.asarray(np.where(lane < half, -1.0, 0.0), F32)
    tables = jnp.stack([jnp.cos(angles), sine * to_back, sine * to_front])

    rep = lambda v_: jnp.broadcast_to(v_[None], (quad,) + v_.shape)
    flat = lambda v_: v_.reshape(-1, v_.shape[-1])
    blocks = lambda v_: v_.reshape(2, n_sx, m, D)
    firsts = gather_rows(n_sx, m)

    def plus(a_, b_, kind=F32):
        return (a_.astype(F32) + b_.astype(F32)).astype(kind)

    vectors = [v_[None] for v_ in (ln1_gain, ln1_bias, ln2_gain, ln2_bias, qkv_bias)]
    live = Live(
        sc=sc,
        inputs=inputs,
        cotangent=cotangent,
        my_ids=my_ids,
        out_w=out_weight,
        gate_w=gate_weight,
        up_w=up_weight,
        down_w=down_weight,
    )
    half_rows = ff_rows // 32 * 16 if ff_rows % 16 == 0 else ff_rows // 2
    live.done(qkv_c=columns([qkv_weight], qkv_plan, vectors))
    give = jnp.concatenate([pick(live.inputs, 1 - sb)[0], pick(live.cotangent, 1 - sb)[0]], 0)
    live.done(
        w_qkv=of_rows(exchange(live.qkv_c)),
        got=swap_sb(give),
        out_1=swap_fh(live.out_w) if natural else live.out_w,
        out_2=swap_sb(live.out_w) if natural else live.out_w,
        ids_got=swap_fl(live.my_ids),
        gu_c=columns([live.gate_w, live.up_w], gu_plan),
        down_a=live.down_w[:half_rows],
        down_b=live.down_w[half_rows:],
        tables=tables,
    )

    own_x = jnp.concatenate([pick(live.inputs, sb)[0], live.got[:tok]], 0)
    own_dy = jnp.concatenate([pick(live.cotangent, sb)[0], live.got[tok:]], 0)
    ids = both(fl, live.my_ids, live.ids_got).reshape(2, 2, n_sx, 2, tok)
    ids = flip_if(fl, flip_if(c, flip_if(sb, ids, 1), 3), 0)
    ids = xor_order(ids, 2, sx, n_sx).transpose(0, 3, 2, 1, 4).reshape(2, length)
    live.drop("inputs", "cotangent", "got", "my_ids", "ids_got", "gate_w", "up_w", "qkv_c")
    live.done(
        qkv_1=swap_fh(live.w_qkv),
        qkv_2=swap_sb(live.w_qkv),
        w_gu=of_rows(exchange(live.gu_c)),
        own_x=own_x,
        own_dy=own_dy,
        x_first=gather_first(own_x),
        out_3=swap_sb(live.out_1) if natural else live.out_w,
        ids=ids,
        id_col=ids.reshape(N, 1),
        dy_rep=rep(own_dy),
    )

    cuts = [n_sr * n // 4 for n in (0, 1, 3, 4)]
    part = [live.w_gu[a_:b_] for a_, b_ in zip(cuts, cuts[1:])]
    if natural:
        out_own = in_order((live.out_w, live.out_1, live.out_2, live.out_3), sb, fh)
        out_own = out_own.reshape(wide, D)
    else:
        out_all = lax.all_gather(out_weight, EVERY, axis=0, tiled=True)
        out_own = lax.dynamic_slice_in_dim(out_all, (sr * 2 + fl) * wide, wide, 0)
    live.done(
        qkv_3=swap_sb(live.qkv_1),
        x_all=gather_second(live.x_first),
        gu_1=[swap_fh(part[0])],
        gu_part=part,
        out_own=out_own,
    )

    qkv = lambda: [(live.w_qkv, 0, 0), (live.qkv_1, 1, 0), (live.qkv_2, 2, 0), (live.qkv_3, 3, 0)]
    h1, q, k, v, o, lse, keep, send, vectors = attention(
        live.sc,
        Rows(live.x_all, firsts),
        live.tables,
        live.ids,
        live.id_col,
        live.out_own,
        qkv(),
        heads,
        rows,
    )
    live.drop("x_first", "x_all", "out_w", "out_1", "out_2", "out_3", "gu_c")
    live.done(
        h1=h1,
        q=q,
        k=k,
        v=v,
        o=o,
        lse=lse,
        keep=keep,
        send=send,
        vectors=vectors,
        gu_1=live.gu_1 + [swap_fh(live.gu_part[1])],
        gu_2=swap_sb(live.w_gu),
        dy_mine=flat(over_quad(live.dy_rep)),
    )
    live.drop("dy_rep")

    live.done(got=swap_c(live.send), dy_other=swap_c(live.dy_mine))
    send_x, send_l, keep_x, keep_l = add_first(blocks(live.keep), blocks(live.got))
    live.done(
        keep=(keep_x, keep_l),
        got=(swap_sx(send_x), swap_fl(send_l)),
        gu_1=live.gu_1 + [swap_fh(live.gu_part[2])],
        gu_3=[swap_sb(v_) for v_ in live.gu_1],
    )
    send_x, send_l, keep_x, keep_l = add_second(live.keep[0], live.got[0], live.keep[1], live.got[1])
    live.done(
        keep=(keep_x, keep_l),
        got=(swap_fl(send_x), swap_sx(send_l)),
        down_1b=swap_fh(live.down_b),
        down_2=swap_sb(live.down_w),
        gu_3=live.gu_3 + [swap_sb(live.gu_1[2])],
    )
    terms = (live.keep[0], live.got[0], live.keep[1], live.got[1])
    x2_own, h2_own = norm_step(terms, live.own_x, live.vectors)
    live.done(
        x2_own=x2_own,
        h2_first=gather_first(h2_own),
        down_3b=swap_sb(live.down_1b),
        down_1a=swap_fh(live.down_a),
    )
    live.done(h2_all=gather_second(live.h2_first), down_3a=swap_sb(live.down_1a))

    down = [live.down_w, live.down_1a, live.down_1b, live.down_2, live.down_3a, live.down_3b]
    down_places = [(0, 0), (1, 0), (1, half_rows), (2, 0), (3, 0), (3, half_rows)]
    if ff_rows % 16 != 0:
        down = [live.down_w, jnp.concatenate(down[1:3], 0), live.down_2, jnp.concatenate(down[4:6], 0)]
        down, down_places = [in_order(down, sb, fh).reshape(ff, D)], [(0, 0)]
    gu = [(live.w_gu, 0, 0), (live.gu_2, 2, 0)]
    gu += [(v_, 1, n) for n, v_ in zip(cuts, live.gu_1)] + [(v_, 3, n) for n, v_ in zip(cuts, live.gu_3)]
    h2, act, d_gu, keep, send = ffn(
        live.sc,
        Rows(live.h2_all, firsts),
        Quads(live.dy_mine, live.dy_other, m),
        gu,
        down,
        down_places,
        rows,
    )
    live.drop("w_gu", "gu_1", "gu_2", "gu_3", "gu_part", "down_a", "down_b", "down_w")
    live.drop("down_1a", "down_1b", "down_2", "down_3a", "down_3b")
    live.drop("h2_first", "h2_all")

    def give_back(v_):
        other = swap_sb(v_[tok:])
        first = jnp.where(sb == 0, v_[:tok], other)
        second = jnp.where(sb == 0, other, v_[:tok])
        return jnp.stack([first, second])[:, None]

    live.done(
        h2=h2,
        act=act,
        d_gu=d_gu,
        down=down,
        keep=keep,
        got=swap_c(send),
        gu_t=grad_rows(live.sc, h2, d_gu, 1, n_sr, rows),
    )
    send_x, send_l, keep_x, keep_l = add_first(blocks(live.keep), blocks(live.got))
    y_keep, y_send = down_product(live.sc, live.act, live.down, down_places)
    live.drop("down")
    live.done(
        keep=(keep_x, keep_l),
        got=(swap_sx(send_x), swap_fl(send_l)),
        gu_got1=swap_sb(live.gu_t[0]),
        gu_m=grad_rows(live.sc, live.h2, live.d_gu, 0, n_sr, rows),
        y_keep=y_keep,
        y_send=y_send,
    )
    live.drop("h2", "d_gu")
    send_x, send_l, keep_x, keep_l = add_second(live.keep[0], live.got[0], live.keep[1], live.got[1])
    halves = lambda v_: (v_[: v_.shape[0] // 2], v_[v_.shape[0] // 2 :])
    gu_give = [plus(a_, b_, BF16) for a_, b_ in zip(halves(live.gu_m[0]), halves(live.gu_got1))]
    live.done(
        keep=(keep_x, keep_l),
        got=(swap_fl(send_x), swap_sx(send_l)),
        gu_got1=swap_sb(live.gu_t[1]),
        gu_over=[swap_fh(gu_give[0])],
        gu_give=gu_give[1],
        down_t=grad_slices(live.sc, live.act, Quads(live.dy_mine, live.dy_other, m)),
        y_got=swap_c(live.y_send),
    )
    live.drop("dy_mine", "dy_other", "act", "y_send")
    terms = (live.keep[0], live.got[0], live.keep[1], live.got[1])
    d_x2, d_att, sums2 = norm_step_back(terms, live.x2_own, live.own_dy, live.vectors, 2)
    gu_give = [plus(a_, b_, BF16) for a_, b_ in zip(halves(live.gu_m[1]), halves(live.gu_got1))]
    live.done(
        d_x2=d_x2,
        sums2=sums2,
        att_first=gather_first(d_att),
        gu_over=live.gu_over + [swap_fh(live.gu_give)],
        gu_give=gu_give,
        down_got1=swap_sb(live.down_t[3]),
        y_sum=plus(live.y_keep, live.y_got, BF16),
    )
    live.drop("gu_got1", "y_keep", "y_got")
    down_cut = live.down_t[1].shape[0] // 32 * 16
    down_give = plus(live.down_t[1], live.down_got1, BF16)
    live.done(
        att_all=gather_second(live.att_first),
        gu_over=live.gu_over + [swap_fh(live.gu_give[0])],
        down_got0=swap_sb(live.down_t[2]),
        down_give=(down_give[:down_cut], down_give[down_cut:]),
    )
    live.drop("att_first")
    d_lin, bias_term, sums1, keep, send = attention_back(
        live.sc,
        live.tables,
        live.ids,
        live.id_col,
        live.q,
        live.k,
        live.v,
        live.lse,
        live.out_own,
        live.h1,
        live.vectors,
        Rows(live.att_all, firsts),
        qkv(),
    )
    live.drop("q", "k", "v", "lse", "out_own", "w_qkv", "qkv_1", "qkv_2", "qkv_3", "tables", "ids", "id_col")
    live.done(
        d_lin=d_lin,
        bias_term=bias_term,
        sums1=sums1,
        keep=keep,
        send=send,
        y_terms=over_quad(live.y_sum.reshape(quad, m, D)),
        gu_got0=swap_sb(live.gu_t[2]),
        gu_over=live.gu_over + [swap_fh(live.gu_give[1])],
    )
    live.drop("gu_give", "y_sum", "down_got1", "gu_t")
    live.done(
        got=swap_c(live.send),
        qkv_t=grad_rows(live.sc, live.h1, live.d_lin, 1, n_sr, rows, 1),
    )
    live.drop("send")

    def half_sum(v_, bit, swap):
        n = v_.shape[1] // 2
        take = lambda k: lax.dynamic_slice_in_dim(v_, k * n, n, 1)
        return take(bit) + swap(take(1 - bit))

    bias_term = live.bias_term.reshape(3, heads, HD).transpose(1, 0, 2)
    if natural:
        bias_term = bias_term.reshape(2, 1, 2, 1, -1)
        here = jnp.arange(n_sr)[None, :, None, None, None] == sr
        here = here & (jnp.arange(2)[None, None, None, :, None] == fl)
    else:
        bias_term = bias_term[None]
        here = jnp.arange(members)[:, None, None, None] == sr * 2 + fl
    bias_term = jnp.where(here, bias_term, 0.0).reshape(n_dev, 3, rows).transpose(1, 0, 2).reshape(3, D)
    gu_sum = plus(live.gu_m[2], live.gu_got0) + jnp.concatenate(live.gu_over, 0).astype(F32)
    send_x, send_l, keep_x, keep_l = add_first(blocks(live.keep), blocks(live.got))
    live.done(
        keep=(keep_x, keep_l),
        got=(swap_sx(send_x), swap_fl(send_l)),
        qkv_got1=swap_sb(live.qkv_t[0]),
        down_over=[swap_fh(live.down_give[1])],
        down_give=live.down_give[0],
        qkv_m=grad_rows(live.sc, live.h1, live.d_lin, 0, n_sr, rows, 1),
        gu_sum=gu_sum.astype(BF16),
        small=jnp.concatenate([live.sums1, live.sums2, bias_term], axis=0),
        out_t=grad_slices(live.sc, live.o, Rows(live.att_all, firsts)) if natural else (),
    )
    live.drop("h1", "d_lin", "gu_m", "gu_got0", "gu_over")
    send_x, send_l, keep_x, keep_l = add_second(live.keep[0], live.got[0], live.keep[1], live.got[1])
    qkv_give = [plus(a_, b_, BF16) for a_, b_ in zip(halves(live.qkv_m[0]), halves(live.qkv_got1))]
    live.done(
        keep=(keep_x, keep_l),
        got=(swap_fl(send_x), swap_sx(send_l)),
        qkv_got0=swap_sb(live.qkv_t[1]),
        qkv_over=[swap_fh(qkv_give[0])],
        qkv_give=qkv_give[1],
        small=half_sum(live.small, sb, swap_sb),
    )
    live.drop("qkv_t", "qkv_got1")
    terms = (live.keep[0], live.got[0], live.keep[1], live.got[1])
    _, input_low, _ = norm_step_back(terms, live.own_x, live.d_x2, live.vectors, 0)
    y = live.x2_own + jnp.sum(live.y_terms.astype(F32), axis=0)
    small = live.small
    bit = n_sx // 2
    while bit >= 1:
        small = half_sum(small, (sx // bit) % 2, functools.partial(swap_sx, bit=bit))
        bit //= 2
    live.done(
        input_low=input_low,
        small=half_sum(small, c, swap_c),
        qkv_over=live.qkv_over + [swap_fh(live.qkv_give)],
        out_got=[swap_sb(v_) for v_ in live.out_t[2:]],
        qkv_sum=plus(live.qkv_m[1], live.qkv_got0),
        layer_out=give_back(y.astype(BF16)),
        gu_done=exchange(live.gu_sum.reshape(members, rows, -1)),
    )
    live.drop("y_terms", "gu_sum")
    qkv_sum = live.qkv_sum + jnp.concatenate(live.qkv_over, 0).astype(F32)
    if natural:
        out_over = swap_fh(plus(live.out_t[1], live.out_got[1], BF16))
    else:
        d_att = jnp.zeros((N, D), BF16)
        for v_, r in zip(live.att_all, firsts):
            d_att = lax.dynamic_update_slice_in_dim(d_att, v_, r, 0)
        t = lax.dot_general(live.o, d_att, TN, preferred_element_type=F32)
        t = jnp.where(jnp.arange(members)[:, None, None] == sr * 2 + fl, t[None], 0.0)
        out_over = lax.psum_scatter(t.reshape(H * HD, D), EVERY, scatter_dimension=0, tiled=True)
    live.done(
        qkv_done=exchange(qkv_sum.astype(BF16).reshape(members, rows, -1)),
        out_over=out_over,
        small=half_sum(live.small, fh, swap_fh),
        down_over=[swap_fh(live.down_give)] + live.down_over,
        input_grad=give_back(live.input_low),
        gate_grad=uncolumns([live.gu_done], gate_back),
        up_grad=uncolumns([live.gu_done], up_back),
    )
    small = half_sum(live.small, fl, swap_fl)
    qkv_grad = uncolumns([live.qkv_done], qkv_back)
    out_grad = live.out_over
    if natural:
        out_grad = plus(live.out_t[0], live.out_got[0]) + out_grad.astype(F32)
    input_grad, layer_out = live.input_grad, live.layer_out
    down_grad = plus(live.down_t[0], live.down_got0) + jnp.concatenate(live.down_over, 0).astype(F32)
    gate_grad, up_grad = live.gate_grad, live.up_grad
    gain1_grad, bias1_grad, gain2_grad, bias2_grad = (small[n] for n in range(4))
    bias_grad = small[4:].reshape(-1)
    return (
        layer_out,
        input_grad,
        gain1_grad,
        bias1_grad,
        qkv_grad,
        bias_grad,
        out_grad,
        gain2_grad,
        bias2_grad,
        gate_grad,
        up_grad,
        down_grad,
    )


def solution(mesh):
    names = dict(mesh.shape)
    n_seq, n_fsdp = names["seq"], names["fsdp"]
    fine = Mesh(mesh.devices.reshape(2, n_seq // 4, 2, 2, n_fsdp // 2), EVERY)
    tokens = P(None, ("fh", "fl"), ("sb", "sx", "c"), None)
    vector = P(EVERY)
    matrix = P(EVERY, None)
    in_specs = (tokens, tokens, P(None, ("fh", "fl"), None), vector, vector, matrix, vector, matrix)
    in_specs += (vector, vector, matrix, matrix, matrix)
    out_specs = (tokens, tokens, vector, vector, matrix, vector, matrix, vector, vector)
    out_specs += (matrix, matrix, matrix)
    return jax.shard_map(shards, mesh=fine, in_specs=in_specs, out_specs=out_specs, check_vma=False)
```

time: 622 us -> 582 us (0.936)
  waiting for transfers between devices: 267 us -> 209 us
  Pallas kernels: 159 us -> 184 us
  other arithmetic: 51.6 us -> 38.1 us
    ppermute x1 -> x14, waiting for transfers between devices: 0.35 us -> 61.5 us  [swap_fl(): return lax.ppermute(v, 'fl', SWAP)]
    ppermute x27 -> x24, waiting for transfers between devices: 94.4 us -> 36.8 us  [swap_sb(): return lax.ppermute(v, 'sb', SWAP)]
    ppermute x12 -> x17, waiting for transfers between devices: 142 us -> 84.6 us  [swap_fh(): return lax.ppermute(v, 'fh', SWAP)]
    all_to_all x8 -> x2, starting transfers between devices: 33.8 us -> 8.28 us  [over_quad(): return lax.all_to_all(v, QUAD, split_axis=0, concat_axis=0, tiled=True)]
    pallas_call x2 -> x8, Pallas kernels: 9.09 us -> 29.5 us  [the longest x3 12.3 us: add_first(): pl.pallas_call(add_first_kernel, out_shape=[low, low, high, high], in_spe...]
    ppermute x1 -> x14, starting transfers between devices: 2.04 us -> 18.8 us  [swap_fl(): return lax.ppermute(v, 'fl', SWAP)]
    convert_element_type x11 -> x6, other arithmetic: 26.9 us -> 10.5 us  [plus(): return (a_.astype(F32) + b_.astype(F32)).astype(kind)]
    ppermute x0 -> x13, starting transfers between devices: none -> 16.4 us  [swap_sx(): return lax.ppermute(v, 'sx', [(i, i ^ bit) for i in range(n)])]
  transfers between devices with their start and end apart: 61 -> 95, of which waited for: 30 -> 39; matrix products, arithmetic and copies ran while one was open for 8% -> 9% of each run, Pallas kernels for 18% -> 23%
where the time goes in v3:
time: 582 us; the launch traced here: 574 us
  waiting for transfers between devices  209 us (36%)
  Pallas kernels  184 us (32%)
  starting transfers between devices  110 us (19%)
  other arithmetic  38.1 us (7%)
  local copies, waits for them, and re-layouts  30.6 us (5%)
    ppermute x17, waiting for transfers between devices, swap_fh(): return lax.ppermute(v, 'fh', SWAP)  84.6 us
    ppermute x14, waiting for transfers between devices, swap_fl(): return lax.ppermute(v, 'fl', SWAP)  61.5 us
    ppermute x24, waiting for transfers between devices, swap_sb(): return lax.ppermute(v, 'sb', SWAP)  36.8 us
    pallas_call x1, Pallas kernels, ffn(): pl.pallas_call(functools.partial(ffn_kernel, dims, h_rows, dy_rows), grid...  31.2 us
    ppermute x17, starting transfers between devices, swap_fh(): return lax.ppermute(v, 'fh', SWAP)  27.7 us
    pallas_call x4, Pallas kernels, grad_rows(): pl.pallas_call(functools.partial(rows_kernel, (n, 2 * rows)), grid_spec=s...  27.5 us
    pallas_call x1, Pallas kernels, attention(): pl.pallas_call(functools.partial(attention_kernel, (heads, length, block,...  26.4 us
    pallas_call x1, Pallas kernels, attention_back(): pl.pallas_call(functools.partial(attention_back_kernel, dims, d_rows), ou...  25.3 us
  transfers between devices with their start and end apart: 95, of which 39 were waited for; matrix products, arithmetic and copies ran while one was open for 9% of the time, Pallas kernels for 23%

profile of v3, /device:TPU:0, one launch (start us, length us, event | category | flops | bytes accessed | tf_op | source)
XLA Modules:
  0.0 574.2 jit_solution(3681011133472789456)
XLA Ops:
  44.8 14.6 %collective-permute-done.4 = bf16[64,2048]{1,0:T(8,128)(2,1)S(1)} collective-permute-done((bf16[64,2048]{1,0:T(8,128)(2,1)}, bf16[64,2048]{1,0:T(8,128)(2,1)S(1)}, u32[]{:S(2)}, u32[]{:S(2)}) %collective-permute-start.4) | collective-permute-done | bytes 262176 | tf_op jit(solution)/shard_map/ppermute | solution.py:48
  61.3 6.1 %collective-permute-done.7.refs_1_ = bf16[128,2048]{1,0:T(8,128)(2,1)} collective-permute-done((bf16[128,2048]{1,0:T(8,128)(2,1)}, bf16[128,2048]{1,0:T(8,128)(2,1)}, u32[]{:S(2)}, u32[]{:S(2)}) %collective-permute-start.7) | collective-permute-done | bytes 524320 | tf_op jit(solution)/shard_map/ppermute | solution.py:65
  67.4 19.3 %collective-permute-done.8.refs_2_ = bf16[128,2048]{1,0:T(8,128)(2,1)} collective-permute-done((bf16[128,2048]{1,0:T(8,128)(2,1)}, bf16[128,2048]{1,0:T(8,128)(2,1)}, u32[]{:S(2)}, u32[]{:S(2)}) %collective-permute-start.8) | collective-permute-done | bytes 524320 | tf_op jit(solution)/shard_map/ppermute | solution.py:56
  97.0 7.6 %collective-permute-done.12.refs_3_ = bf16[64,2048]{1,0:T(8,128)(2,1)S(1)} collective-permute-done((bf16[64,2048]{1,0:T(8,128)(2,1)S(1)}, bf16[64,2048]{1,0:T(8,128)(2,1)S(1)}, u32[]{:S(2)}, u32[]{:S(2)}) %collective-permute-start.12) | collective-permute-done | bytes 262176 | tf_op jit(solution)/shard_map/ppermute | solution.py:56
  120.8 26.4 %shard_map.249 = (bf16[1024,2048]{1,0:T(8,128)(2,1)}, bf16[1024,256]{1,0:T(8,128)(2,1)}, bf16[1024,256]{1,0:T(8,128)(2,1)}, bf16[1024,256]{1,0:T(8,128)(2,1)}, b...) custom-call(s32[5]{0:T(128)} %stack.83.sc, ...), custom_call_target="tpu_custom_call" | custom-call | flops 24999999488 | bytes 1024 | tf_op jit(solution)/shard_map/pallas_call | solution.py:458
  147.2 8.1 %collective-permute-done.18.refs_15_ = bf16[2,2,64,1408]{3,2,1,0:T(8,128)(2,1)} collective-permute-done((bf16[2,2,64,1408]{3,2,1,0:T(8,128)(2,1)}, bf16[2,2,64,1408]{3,2,1,0:T(8,128)(2,1)}, u32[]{:S(2)}, u32[]{:S(2)}) %collective-permute-start.18) | collective-permute-done | bytes 720928 | tf_op jit(solution)/shard_map/ppermute | solution.py:52
  157.8 6.6 %collective-permute-done.20.refs_11_.refs_1_ = bf16[512,2048]{1,0:T(8,128)(2,1)S(1)} collective-permute-done((bf16[512,2048]{1,0:T(8,128)(2,1)S(1)}, bf16[512,2048]{1,0:T(8,128)(2,1)S(1)}, u32[]{:S(2)}, u32[]{:S(2)}) %collective-permute-start.20) | collective-permute-done | bytes 2097184 | tf_op jit(solution)/shard_map/ppermute | solution.py:60
  175.2 17.8 %collective-permute-done.24.refs_16_ = bf16[1,2,64,1408]{3,2,1,0:T(8,128)(2,1)S(1)} collective-permute-done((bf16[1,2,64,1408]{3,2,1,0:T(8,128)(2,1)S(1)}, bf16[1,2,64,1408]{3,2,1,0:T(8,128)(2,1)S(1)}, u32[]{:S(2)}, u32[]{:S(2)}) %collective-permute-start.24) | collective-permute-done | bytes 360480 | tf_op jit(solution)/shard_map/ppermute | solution.py:52
  202.9 13.7 %collective-permute-done.29.u1 = bf16[64,2048]{1,0:T(8,128)(2,1)S(1)} collective-permute-done((bf16[64,2048]{1,0:T(8,128)(2,1)}, bf16[64,2048]{1,0:T(8,128)(2,1)S(1)}, u32[]{:S(2)}, u32[]{:S(2)}) %collective-permute-start.29) | collective-permute-done | bytes 262176 | tf_op jit(solution)/shard_map/ppermute | solution.py:56
  226.5 14.3 %collective-permute-done.32.refs_21_.refs_1_ = bf16[80,2048]{1,0:T(8,128)(2,1)S(1)} collective-permute-done((bf16[80,2048]{1,0:T(8,128)(2,1)S(1)}, bf16[80,2048]{1,0:T(8,128)(2,1)S(1)}, u32[]{:S(2)}, u32[]{:S(2)}) %collective-permute-start.32) | collective-permute-done | bytes 327712 | tf_op jit(solution)/shard_map/ppermute | solution.py:52
  257.6 31.2 %shard_map.253 = (bf16[1024,2048]{1,0:T(8,128)(2,1)}, bf16[1024,704]{1,0:T(8,128)(2,1)}, bf16[1024,1408]{1,0:T(8,128)(2,1)}, bf16[512,2048]{1,0:T(8,128)(2,1)}, bf16[512,2048]{1,0:T(8,128)(2,1)}) custom-call(s32[5]{0:T(128)} %stack.83.sc, bf16[128,2048]{1,0:T(8,128)(2,1)} %get-tuple-element.954.refs_0_, bf16[128,2048]{1,0:T(8,128)(2,1)} %copy-done.40, ...), custom_call_target="tpu_custom_call" | custom-call | flops 30000001024 | bytes 1024 | tf_op jit(solution)/shard_map/pallas_call | solution.py:551
  288.9 8.2 %shard_map.254 = (bf16[256,1408]{1,0:T(8,128)(2,1)}, bf16[256,1408]{1,0:T(8,128)(2,1)}, bf16[512,1408]{1,0:T(8,128)(2,1)}) custom-call(s32[5]{0:T(128)} %stack.83.sc, bf16[1024,2048]{1,0:T(8,128)(2,1)} %get-tuple-element.1016.h, bf16[1024,1408]{1,0:T(8,128)(2,1)} %get-tuple-element.1007.d), custom_call_target="tpu_custom_call" | custom-call | flops 7000000000 | bytes 1024 | tf_op jit(solution)/shard_map/pallas_call | solution.py:761
  303.6 9.6 %shard_map.257 = (bf16[512,2048]{1,0:T(8,128)(2,1)}, bf16[512,2048]{1,0:T(8,128)(2,1)}) custom-call(s32[5]{0:T(128)} %stack.83.sc, bf16[1024,704]{1,0:T(8,128)(2,1)} %get-tuple-element.1050.act.a, bf16[176,2048]{1,0:T(8,128)(2,1)} %refs_0_.3, bf16[80,2048]{1,0:T(8,128)(2,1)} %copy-done.68, bf16[96,2048]{1,0:T(8,128)(2,1)} %copy-done.62, ...), custom_call_target="tpu_custom_call" | custom-call | flops 8999999488 | bytes 1024 | tf_op jit(solution)/shard_map/pallas_call | solution.py:605
  313.2 8.1 %shard_map.256 = (bf16[256,1408]{1,0:T(8,128)(2,1)}, bf16[256,1408]{1,0:T(8,128)(2,1)}, bf16[512,1408]{1,0:T(8,128)(2,1)}) custom-call(s32[5]{0:T(128)} %stack.83.sc, bf16[1024,2048]{1,0:T(8,128)(2,1)} %get-tuple-element.1016.h, bf16[1024,1408]{1,0:T(8,128)(2,1)} %get-tuple-element.1007.d), custom_call_target="tpu_custom_call" | custom-call | flops 7000000000 | bytes 1024 | tf_op jit(solution)/shard_map/pallas_call | solution.py:761
  334.0 10.0 %shard_map.258 = (bf16[176,2048]{1,0:T(8,128)(2,1)}, bf16[176,2048]{1,0:T(8,128)(2,1)}, bf16[176,2048]{1,0:T(8,128)(2,1)}, bf16[176,2048]{1,0:T(8,128)(2,1)}) custom-call(s32[5]{0:T(128)} %stack.83.sc, bf16[1024,704]{1,0:T(8,128)(2,1)} %get-tuple-element.1050.act.a, bf16[512,2048]{1,0:T(8,128)(2,1)} %bitcast.79, bf16[512,2048]{1,0:T(8,128)(2,1)} %copy-done.46), custom_call_target="tpu_custom_call" | custom-call | flops 8999999488 | bytes 1024 | tf_op jit(solution)/shard_map/pallas_call | solution.py:801
  344.0 7.1 %collective-permute-done.51 = bf16[128,1408]{1,0:T(8,128)(2,1)S(1)} collective-permute-done((bf16[128,1408]{1,0:T(8,128)(2,1)}, bf16[128,1408]{1,0:T(8,128)(2,1)S(1)}, u32[]{:S(2)}, u32[]{:S(2)}) %collective-permute-start.51) | collective-permute-done | bytes 360480 | tf_op jit(solution)/shard_map/ppermute | solution.py:52
  365.4 10.1 %collective-permute-done.57 = bf16[128,1408]{1,0:T(8,128)(2,1)S(1)} collective-permute-done((bf16[128,1408]{1,0:T(8,128)(2,1)S(1)}, bf16[128,1408]{1,0:T(8,128)(2,1)S(1)}, u32[]{:S(2)}, u32[]{:S(2)}) %collective-permute-start.57) | collective-permute-done | bytes 360480 | tf_op jit(solution)/shard_map/ppermute | solution.py:52
  382.8 8.3 %collective-permute-done.58.refs_3_ = bf16[64,2048]{1,0:T(8,128)(2,1)S(1)} collective-permute-done((bf16[64,2048]{1,0:T(8,128)(2,1)S(1)}, bf16[64,2048]{1,0:T(8,128)(2,1)S(1)}, u32[]{:S(2)}, u32[]{:S(2)}) %collective-permute-start.58) | collective-permute-done | bytes 262176 | tf_op jit(solution)/shard_map/ppermute | solution.py:56
  405.2 25.3 %shard_map.261 = (bf16[1024,768]{1,0:T(8,128)(2,1)}, f32[1,768]{1,0:T(1,128)}, f32[2,2048]{1,0:T(2,128)}, bf16[512,2048]{1,0:T(8,128)(2,1)}, bf16[512,2048]{1,0:T(8,128)(2,1)}) custom-call(s32[5]{0:T(128)} %stack.83.sc, f32[3,512,512]{2,1,0:T(8,128)} %pad_maximum_fusion.tables, s32[2,512]{1,0:T(2,128)} %reshape.395.id_row, s32[1024,1]{1,0:T(8,128)} %copy.40.id_col, ...), custom_call_target="tpu_custom_call" | custom-call | flops 23000000512 | bytes 1024 | tf_op jit(solution)/shard_map/pallas_call | solution.py:702
  437.6 5.6 shard_map.262
  457.8 7.5 %shard_map.264 = (bf16[64,2048]{1,0:T(8,128)(2,1)}, bf16[64,2048]{1,0:T(8,128)(2,1)}, bf16[64,2048]{1,0:T(8,128)(2,1)}, bf16[64,2048]{1,0:T(8,128)(2,1)}) custom-call(s32[5]{0:T(128)} %stack.83.sc, bf16[1024,256]{1,0:T(8,128)(2,1)} %get-tuple-element.1277.a, bf16[128,2048]{1,0:T(8,128)(2,1)} %get-tuple-element.1247.refs_0_, bf16[128,2048]{1,0:T(8,128)(2,1)} %copy-done.38, ...), custom_call_target="tpu_custom_call" | custom-call | flops 8999999488 | bytes 1024 | tf_op jit(solution)/shard_map/pallas_call | solution.py:801
  483.9 6.5 %collective-permute-done.77 = f32[7,1024]{1,0:T(8,128)S(1)} collective-permute-done((f32[7,1024]{1,0:T(8,128)S(1)}, f32[7,1024]{1,0:T(8,128)S(1)}, u32[]{:S(2)}, u32[]{:S(2)}) %collective-permute-start.77) | collective-permute-done | bytes 28704 | tf_op jit(solution)/shard_map/ppermute | solution.py:48
  545.2 5.8 %collective-permute-done.87 = f32[7,128]{1,0:T(8,128)S(1)} collective-permute-done((f32[7,128]{1,0:T(8,128)S(1)}, f32[7,128]{1,0:T(8,128)S(1)}, u32[]{:S(2)}, u32[]{:S(2)}) %collective-permute-start.87) | collective-permute-done | bytes 3616 | tf_op jit(solution)/shard_map/ppermute | solution.py:52
  552.8 9.3 %collective-permute-done.86 = bf16[64,2048]{1,0:T(8,128)(2,1)S(1)} collective-permute-done((bf16[64,2048]{1,0:T(8,128)(2,1)S(1)}, bf16[64,2048]{1,0:T(8,128)(2,1)S(1)}, u32[]{:S(2)}, u32[]{:S(2)}) %collective-permute-start.86) | collective-permute-done | bytes 262176 | tf_op jit(solution)/shard_map/ppermute | solution.py:52
  (453 shorter events, 285.2 us)
Async XLA Ops:
  5.0 22.9 %collective-permute-start.2 = (bf16[64,2048]{1,0:T(8,128)(2,1)}, bf16[64,2048]{1,0:T(8,128)(2,1)}, u32[]{:S(2)}, u32[]{:S(2)}) collective-permute-start(bf16[64,2048]{1,0:T(8,128)(2,1)} %param.23), channel_id=1, source_target_pairs={{0,2},{2,0},{1,3},{3,1},{4,6},{6,4},{5,7},{7,5},{8,10},{10,8},{9,1... | collective-permute-start | bytes 786440 | tf_op jit(solution)/shard_map/ppermute | solution.py:52
  31.7 55.0 %collective-permute-start.5 = (bf16[4,2,72,768]{3,2,1,0:T(8,128)(2,1)S(1)}, bf16[4,2,72,768]{3,2,1,0:T(8,128)(2,1)}, u32[]{:S(2)}, u32[]{:S(2)}) collective-permute-start(bf16[4,2,72,768]{3,2,1,0:T(8,128)(2,1)S(1)} %bitcast.82), channel_id=1, source_target_pairs={{0,2},{2,0},{1,3},{3,1},{4,6},{6,4},{5,7},{7,5},{8,10},{10,8},{9,1... | collective-permute-start | bytes 2654216 | tf_op jit(solution)/shard_map/ppermute | solution.py:52
  32.5 54.2 %collective-permute-start.6 = (bf16[4,2,72,768]{3,2,1,0:T(8,128)(2,1)S(1)}, bf16[4,2,72,768]{3,2,1,0:T(8,128)(2,1)}, u32[]{:S(2)}, u32[]{:S(2)}) collective-permute-start(bf16[4,2,72,768]{3,2,1,0:T(8,128)(2,1)S(1)} %bitcast.83), channel_id=1, source_target_pairs={{0,16},{16,0},{1,17},{17,1},{2,18},{18,2},{3,19},{19,3},{4,20},{20... | collective-permute-start | bytes 2654216 | tf_op jit(solution)/shard_map/ppermute | solution.py:48
  34.0 52.7 %all-to-all-start.1 = ((bf16[8,64,1408]{2,1,0:T(8,128)(2,1)}), bf16[8,64,1408]{2,1,0:T(8,128)(2,1)S(1)}, u32[]{:S(2)}, u32[]{:S(2)}) async-start(bf16[8,64,1408]{2,1,0:T(8,128)(2,1)} %shard_map.248), calls=%async_computation.1 | async-start | bytes 2883584 | tf_op jit(solution)/shard_map/all_to_all | solution.py:919
  40.5 26.9 %collective-permute-start.7 = (bf16[128,2048]{1,0:T(8,128)(2,1)}, bf16[128,2048]{1,0:T(8,128)(2,1)}, u32[]{:S(2)}, u32[]{:S(2)}) collective-permute-start(bf16[128,2048]{1,0:T(8,128)(2,1)} %pad_maximum_fusion.4.refs_0_.x), channel_id=1, source_target_pairs={{0,8},{8,0},{1,9},{9,1},{2,10},{10,2},{3,11},{11,3},{4,12},{12,4},... | collective-permute-start | bytes 1572872 | tf_op jit(solution)/shard_map/ppermute | solution.py:65
  42.5 44.1 %collective-permute-start.8 = (bf16[128,2048]{1,0:T(8,128)(2,1)}, bf16[128,2048]{1,0:T(8,128)(2,1)}, u32[]{:S(2)}, u32[]{:S(2)}) collective-permute-start(bf16[128,2048]{1,0:T(8,128)(2,1)} %pad_maximum_fusion.4.refs_0_.x), channel_id=1, source_target_pairs={{0,1},{1,0},{2,3},{3,2},{4,5},{5,4},{6,7},{7,6},{8,9},{9,8},{10,11... | collective-permute-start | bytes 1572872 | tf_op jit(solution)/shard_map/ppermute | solution.py:56
  59.4 27.2 %collective-permute-start.9 = (bf16[128,2048]{1,0:T(8,128)(2,1)}, bf16[128,2048]{1,0:T(8,128)(2,1)}, u32[]{:S(2)}, u32[]{:S(2)}) collective-permute-start(bf16[128,2048]{1,0:T(8,128)(2,1)} %pad_maximum_fusion.4.refs_0_.x), channel_id=1, source_target_pairs={{0,4},{4,0},{1,5},{5,1},{2,6},{6,2},{3,7},{7,3},{8,12},{12,8},{9,1... | collective-permute-start | bytes 1572872 | tf_op jit(solution)/shard_map/ppermute | solution.py:60
  90.3 22.4 %collective-permute-start.11 = (bf16[4,2,72,768]{3,2,1,0:T(8,128)(2,1)}, bf16[4,2,72,768]{3,2,1,0:T(8,128)(2,1)}, u32[]{:S(2)}, u32[]{:S(2)}) collective-permute-start(bf16[4,2,72,768]{3,2,1,0:T(8,128)(2,1)} %collective-permute-done.5.refs_11_), channel_id=1, source_target_pairs={{0,16},{16,0},{1,17},{17,1},{2,18},{18,2},{3,19},{19,3},{4,20},{20... | collective-permute-start | bytes 2654216 | tf_op jit(solution)/shard_map/ppermute | solution.py:48
  112.7 44.6 %all-to-all-start.2 = ((bf16[4,128,2048]{2,1,0:T(8,128)(2,1)}), bf16[4,128,2048]{2,1,0:T(8,128)(2,1)S(1)}, u32[]{:S(2)}, u32[]{:S(2)}) async-start(bf16[4,128,2048]{2,1,0:T(8,128)(2,1)} %broadcast_in_dim.70), calls=%async_computation.2 | async-start | bytes 4194304 | tf_op jit(solution)/shard_map/all_to_all | solution.py:69
  117.2 38.0 %collective-permute-start.18 = (bf16[2,2,64,1408]{3,2,1,0:T(8,128)(2,1)}, bf16[2,2,64,1408]{3,2,1,0:T(8,128)(2,1)}, u32[]{:S(2)}, u32[]{:S(2)}) collective-permute-start(bf16[2,2,64,1408]{3,2,1,0:T(8,128)(2,1)} %slice.115), channel_id=1, source_target_pairs={{0,2},{2,0},{1,3},{3,1},{4,6},{6,4},{5,7},{7,5},{8,10},{10,8},{9,1... | collective-permute-start | bytes 2162696 | tf_op jit(solution)/shard_map/ppermute | solution.py:52
  119.2 36.0 %collective-permute-start.19 = (bf16[4,2,64,1408]{3,2,1,0:T(8,128)(2,1)S(1)}, bf16[4,2,64,1408]{3,2,1,0:T(8,128)(2,1)}, u32[]{:S(2)}, u32[]{:S(2)}) collective-permute-start(bf16[4,2,64,1408]{3,2,1,0:T(8,128)(2,1)S(1)} %bitcast.75), channel_id=1, source_target_pairs={{0,16},{16,0},{1,17},{17,1},{2,18},{18,2},{3,19},{19,3},{4,20},{20... | collective-permute-start | bytes 4325384 | tf_op jit(solution)/shard_map/ppermute | solution.py:48
  164.7 29.1 %collective-permute-start.26 = (bf16[2,2,64,1408]{3,2,1,0:T(8,128)(2,1)}, bf16[2,2,64,1408]{3,2,1,0:T(8,128)(2,1)}, u32[]{:S(2)}, u32[]{:S(2)}) collective-permute-start(bf16[2,2,64,1408]{3,2,1,0:T(8,128)(2,1)} %collective-permute-done.18.refs_15_), channel_id=1, source_target_pairs={{0,16},{16,0},{1,17},{17,1},{2,18},{18,2},{3,19},{19,3},{4,20},{20... | collective-permute-start | bytes 2162696 | tf_op jit(solution)/shard_map/ppermute | solution.py:48
  170.7 22.3 %collective-permute-start.22 = (bf16[2,64,2048]{2,1,0:T(8,128)(2,1)}, bf16[2,64,2048]{2,1,0:T(8,128)(2,1)S(1)}, u32[]{:S(2)}, u32[]{:S(2)}) collective-permute-start(bf16[2,64,2048]{2,1,0:T(8,128)(2,1)} %get-tuple-element.812), channel_id=1, source_target_pairs={{0,8},{8,0},{1,9},{9,1},{2,10},{10,2},{3,11},{11,3},{4,12},{12,4},... | collective-permute-start | bytes 1572872 | tf_op jit(solution)/shard_map/ppermute | solution.py:65
  193.8 24.8 %collective-permute-start.28 = (bf16[176,2048]{1,0:T(8,128)(2,1)S(1)}, bf16[176,2048]{1,0:T(8,128)(2,1)S(1)}, u32[]{:S(2)}, u32[]{:S(2)}) collective-permute-start(bf16[176,2048]{1,0:T(8,128)(2,1)S(1)} %copy-done.16), channel_id=1, source_target_pairs={{0,16},{16,0},{1,17},{17,1},{2,18},{18,2},{3,19},{19,3},{4,20},{20... | collective-permute-start | bytes 2162696 | tf_op jit(solution)/shard_map/ppermute | solution.py:48
  194.4 24.2 %collective-permute-start.27 = (bf16[96,2048]{1,0:T(8,128)(2,1)S(1)}, bf16[96,2048]{1,0:T(8,128)(2,1)S(1)}, u32[]{:S(2)}, u32[]{:S(2)}) collective-permute-start(bf16[96,2048]{1,0:T(8,128)(2,1)S(1)} %copy-done.26), channel_id=1, source_target_pairs={{0,2},{2,0},{1,3},{3,1},{4,6},{6,4},{5,7},{7,5},{8,10},{10,8},{9,1... | collective-permute-start | bytes 1179656 | tf_op jit(solution)/shard_map/ppermute | solution.py:52
  322.1 29.0 %collective-permute-start.52 = (bf16[512,2048]{1,0:T(8,128)(2,1)}, bf16[512,2048]{1,0:T(8,128)(2,1)S(1)}, u32[]{:S(2)}, u32[]{:S(2)}) collective-permute-start(bf16[512,2048]{1,0:T(8,128)(2,1)} %get-tuple-element.1090), channel_id=1, source_target_pairs={{0,4},{4,0},{1,5},{5,1},{2,6},{6,2},{3,7},{7,3},{8,12},{12,8},{9,1... | collective-permute-start | bytes 6291464 | tf_op jit(solution)/shard_map/ppermute | solution.py:60
  398.4 39.0 %all-to-all-start.3 = ((bf16[4,128,2048]{2,1,0:T(8,128)(2,1)}), bf16[4,128,2048]{2,1,0:T(8,128)(2,1)S(1)}, u32[]{:S(2)}, u32[]{:S(2)}) async-start(bf16[4,128,2048]{2,1,0:T(8,128)(2,1)} %bitcast.29), calls=%async_computation.3 | async-start | bytes 4194304 | tf_op jit(solution)/shard_map/all_to_all | solution.py:69
  403.2 34.2 %collective-permute-start.66 = (bf16[512,1408]{1,0:T(8,128)(2,1)}, bf16[512,1408]{1,0:T(8,128)(2,1)S(1)}, u32[]{:S(2)}, u32[]{:S(2)}) collective-permute-start(bf16[512,1408]{1,0:T(8,128)(2,1)} %get-tuple-element.1198), channel_id=1, source_target_pairs={{0,16},{16,0},{1,17},{17,1},{2,18},{18,2},{3,19},{19,3},{4,20},{20... | collective-permute-start | bytes 4325384 | tf_op jit(solution)/shard_map/ppermute | solution.py:48
  404.0 29.5 %collective-permute-start.67 = (bf16[128,1408]{1,0:T(8,128)(2,1)}, bf16[128,1408]{1,0:T(8,128)(2,1)S(1)}, u32[]{:S(2)}, u32[]{:S(2)}) collective-permute-start(bf16[128,1408]{1,0:T(8,128)(2,1)} %get-tuple-element.1197), channel_id=1, source_target_pairs={{0,2},{2,0},{1,3},{3,1},{4,6},{6,4},{5,7},{7,5},{8,10},{10,8},{9,1... | collective-permute-start | bytes 1081352 | tf_op jit(solution)/shard_map/ppermute | solution.py:52
  443.2 26.7 %collective-permute-start.69 = (bf16[96,2048]{1,0:T(8,128)(2,1)}, bf16[96,2048]{1,0:T(8,128)(2,1)}, u32[]{:S(2)}, u32[]{:S(2)}) collective-permute-start(bf16[96,2048]{1,0:T(8,128)(2,1)} %slice.147), channel_id=1, source_target_pairs={{0,2},{2,0},{1,3},{3,1},{4,6},{6,4},{5,7},{7,5},{8,10},{10,8},{9,1... | collective-permute-start | bytes 1179656 | tf_op jit(solution)/shard_map/ppermute | solution.py:52
  470.9 23.4 %collective-permute-start.75 = (bf16[512,768]{1,0:T(8,128)(2,1)}, bf16[512,768]{1,0:T(8,128)(2,1)S(1)}, u32[]{:S(2)}, u32[]{:S(2)}) collective-permute-start(bf16[512,768]{1,0:T(8,128)(2,1)} %get-tuple-element.1314), channel_id=1, source_target_pairs={{0,16},{16,0},{1,17},{17,1},{2,18},{18,2},{3,19},{19,3},{4,20},{20... | collective-permute-start | bytes 2359304 | tf_op jit(solution)/shard_map/ppermute | solution.py:48
  495.3 31.3 %all-to-all-start.4 = ((bf16[8,64,1408]{2,1,0:T(8,128)(2,1)}), bf16[8,64,1408]{2,1,0:T(8,128)(2,1)S(1)}, u32[]{:S(2)}, u32[]{:S(2)}) async-start(bf16[8,64,1408]{2,1,0:T(8,128)(2,1)} %bitcast.34), calls=%async_computation.4 | async-start | bytes 2883584 | tf_op jit(solution)/shard_map/all_to_all | solution.py:919
  533.4 28.8 %collective-permute-start.84 = (bf16[80,2048]{1,0:T(8,128)(2,1)S(1)}, bf16[80,2048]{1,0:T(8,128)(2,1)S(1)}, u32[]{:S(2)}, u32[]{:S(2)}) collective-permute-start(bf16[80,2048]{1,0:T(8,128)(2,1)S(1)} %copy-done.33), channel_id=1, source_target_pairs={{0,2},{2,0},{1,3},{3,1},{4,6},{6,4},{5,7},{7,5},{8,10},{10,8},{9,1... | collective-permute-start | bytes 983048 | tf_op jit(solution)/shard_map/ppermute | solution.py:52
  537.4 27.9 %all-to-all-start.5 = ((bf16[8,64,768]{2,1,0:T(8,128)(2,1)}), bf16[8,64,768]{2,1,0:T(8,128)(2,1)S(1)}, u32[]{:S(2)}, u32[]{:S(2)}) async-start(bf16[8,64,768]{2,1,0:T(8,128)(2,1)} %bitcast.41), calls=%async_computation.5 | async-start | bytes 1572864 | tf_op jit(solution)/shard_map/all_to_all | solution.py:919
  (154 other events, 1697.3 us)

commit v4 on v3

--- a/solution.py
+++ b/solution.py
@@ -37,7 +37,7 @@
 
 
 def cost(microseconds):
-    return pl.CostEstimate(flops=int(microseconds * 1e9), bytes_accessed=1024, transcendentals=0)
+    return pl.CostEstimate(flops=int(microseconds * 1e8), bytes_accessed=1024, transcendentals=0)
 
 
 def dot(a, b, dims=(((1,), (0,)), ((), ()))):
@@ -1236,7 +1236,7 @@
         gu_done=exchange(live.gu_sum.reshape(members, rows, -1)),
     )
     live.drop("y_terms", "gu_sum")
-    qkv_sum = live.qkv_sum + jnp.concatenate(live.qkv_over, 0).astype(F32)
+    live.done(qkv_sum=(live.qkv_sum + jnp.concatenate(live.qkv_over, 0).astype(F32)).astype(BF16))
     if natural:
         out_over = swap_fh(plus(live.out_t[1], live.out_got[1], BF16))
     else:
@@ -1247,7 +1247,7 @@
         t = jnp.where(jnp.arange(members)[:, None, None] == sr * 2 + fl, t[None], 0.0)
         out_over = lax.psum_scatter(t.reshape(H * HD, D), EVERY, scatter_dimension=0, tiled=True)
     live.done(
-        qkv_done=exchange(qkv_sum.astype(BF16).reshape(members, rows, -1)),
+        qkv_done=exchange(live.qkv_sum.reshape(members, rows, -1)),
         out_over=out_over,
         small=half_sum(live.small, fh, swap_fh),
         down_over=[swap_fh(live.down_give)] + live.down_over,

time: 582 us -> 576 us (0.990)
    ppermute x14, waiting for transfers between devices: 61.5 us -> 68 us  [swap_fl(): return lax.ppermute(v, 'fl', SWAP)]
    unnamed x167 -> x183, local copies, waits for them, and re-layouts: 12.4 us -> 13.9 us
  transfers between devices with their start and end apart: 95 -> 95, of which waited for: 39 -> 35; matrix products, arithmetic and copies ran while one was open for 9% -> 8% of each run, Pallas kernels for 23% -> 24%
where the time goes in v4:
time: 576 us; the launch traced here: 568 us
  waiting for transfers between devices  205 us (36%)
  Pallas kernels  184 us (32%)
  starting transfers between devices  109 us (19%)
  other arithmetic  36.3 us (6%)
  local copies, waits for them, and re-layouts  32.6 us (6%)
    ppermute x17, waiting for transfers between devices, swap_fh(): return lax.ppermute(v, 'fh', SWAP)  80.6 us
    ppermute x14, waiting for transfers between devices, swap_fl(): return lax.ppermute(v, 'fl', SWAP)  68 us
    ppermute x24, waiting for transfers between devices, swap_sb(): return lax.ppermute(v, 'sb', SWAP)  34.7 us
    pallas_call x1, Pallas kernels, ffn(): pl.pallas_call(functools.partial(ffn_kernel, dims, h_rows, dy_rows), grid...  31.3 us
    pallas_call x4, Pallas kernels, grad_rows(): pl.pallas_call(functools.partial(rows_kernel, (n, 2 * rows)), grid_spec=s...  27.4 us
    ppermute x24, starting transfers between devices, swap_sb(): return lax.ppermute(v, 'sb', SWAP)  26.5 us
    pallas_call x1, Pallas kernels, attention(): pl.pallas_call(functools.partial(attention_kernel, (heads, length, block,...  26.3 us
    pallas_call x1, Pallas kernels, attention_back(): pl.pallas_call(functools.partial(attention_back_kernel, dims, d_rows), ou...  25.3 us
  transfers between devices with their start and end apart: 95, of which 35 were waited for; matrix products, arithmetic and copies ran while one was open for 8% of the time, Pallas kernels for 24%

profile of v4, /device:TPU:0, one launch (start us, length us, event | category | flops | bytes accessed | tf_op | source)
XLA Modules:
  0.0 568.1 jit_solution(5355928295720969588)
XLA Ops:
  43.6 14.7 %collective-permute-done.4 = bf16[64,2048]{1,0:T(8,128)(2,1)} collective-permute-done((bf16[64,2048]{1,0:T(8,128)(2,1)}, bf16[64,2048]{1,0:T(8,128)(2,1)}, u32[]{:S(2)}, u32[]{:S(2)}) %collective-permute-start.4) | collective-permute-done | bytes 262176 | tf_op jit(solution)/shard_map/ppermute | solution.py:48
  60.1 5.3 collective-permute-done.7.refs_1_
  65.4 19.8 %collective-permute-done.8.refs_2_ = bf16[128,2048]{1,0:T(8,128)(2,1)} collective-permute-done((bf16[128,2048]{1,0:T(8,128)(2,1)S(1)}, bf16[128,2048]{1,0:T(8,128)(2,1)}, u32[]{:S(2)}, u32[]{:S(2)}) %collective-permute-start.8) | collective-permute-done | bytes 524320 | tf_op jit(solution)/shard_map/ppermute | solution.py:56
  97.0 6.4 %collective-permute-done.12.refs_3_ = bf16[64,2048]{1,0:T(8,128)(2,1)S(1)} collective-permute-done((bf16[64,2048]{1,0:T(8,128)(2,1)S(1)}, bf16[64,2048]{1,0:T(8,128)(2,1)S(1)}, u32[]{:S(2)}, u32[]{:S(2)}) %collective-permute-start.12) | collective-permute-done | bytes 262176 | tf_op jit(solution)/shard_map/ppermute | solution.py:56
  120.4 26.3 %shard_map.249 = (bf16[1024,2048]{1,0:T(8,128)(2,1)}, bf16[1024,256]{1,0:T(8,128)(2,1)}, bf16[1024,256]{1,0:T(8,128)(2,1)}, bf16[1024,256]{1,0:T(8,128)(2,1)}, b...) custom-call(s32[5]{0:T(128)} %stack.83.sc, ...), custom_call_target="tpu_custom_call" | custom-call | flops 2500000000 | bytes 1024 | tf_op jit(solution)/shard_map/pallas_call | solution.py:458
  146.7 8.3 %collective-permute-done.18.refs_15_ = bf16[2,2,64,1408]{3,2,1,0:T(8,128)(2,1)} collective-permute-done((bf16[2,2,64,1408]{3,2,1,0:T(8,128)(2,1)}, bf16[2,2,64,1408]{3,2,1,0:T(8,128)(2,1)}, u32[]{:S(2)}, u32[]{:S(2)}) %collective-permute-start.18) | collective-permute-done | bytes 720928 | tf_op jit(solution)/shard_map/ppermute | solution.py:52
  157.6 6.6 %collective-permute-done.20.refs_11_.refs_1_ = bf16[512,2048]{1,0:T(8,128)(2,1)S(1)} collective-permute-done((bf16[512,2048]{1,0:T(8,128)(2,1)S(1)}, bf16[512,2048]{1,0:T(8,128)(2,1)S(1)}, u32[]{:S(2)}, u32[]{:S(2)}) %collective-permute-start.20) | collective-permute-done | bytes 2097184 | tf_op jit(solution)/shard_map/ppermute | solution.py:60
  175.4 16.6 %collective-permute-done.24.refs_16_ = bf16[1,2,64,1408]{3,2,1,0:T(8,128)(2,1)S(1)} collective-permute-done((bf16[1,2,64,1408]{3,2,1,0:T(8,128)(2,1)}, bf16[1,2,64,1408]{3,2,1,0:T(8,128)(2,1)S(1)}, u32[]{:S(2)}, u32[]{:S(2)}) %collective-permute-start.24) | collective-permute-done | bytes 360480 | tf_op jit(solution)/shard_map/ppermute | solution.py:52
  202.0 13.8 %collective-permute-done.29.u1 = bf16[64,2048]{1,0:T(8,128)(2,1)S(1)} collective-permute-done((bf16[64,2048]{1,0:T(8,128)(2,1)}, bf16[64,2048]{1,0:T(8,128)(2,1)S(1)}, u32[]{:S(2)}, u32[]{:S(2)}) %collective-permute-start.29) | collective-permute-done | bytes 262176 | tf_op jit(solution)/shard_map/ppermute | solution.py:56
  226.6 17.0 %collective-permute-done.32.refs_21_.refs_1_ = bf16[80,2048]{1,0:T(8,128)(2,1)S(1)} collective-permute-done((bf16[80,2048]{1,0:T(8,128)(2,1)}, bf16[80,2048]{1,0:T(8,128)(2,1)S(1)}, u32[]{:S(2)}, u32[]{:S(2)}) %collective-permute-start.32) | collective-permute-done | bytes 327712 | tf_op jit(solution)/shard_map/ppermute | solution.py:52
  257.8 31.3 %shard_map.253 = (bf16[1024,2048]{1,0:T(8,128)(2,1)}, bf16[1024,704]{1,0:T(8,128)(2,1)}, bf16[1024,1408]{1,0:T(8,128)(2,1)}, bf16[512,2048]{1,0:T(8,128)(2,1)}, bf16[512,2048]{1,0:T(8,128)(2,1)}) custom-call(s32[5]{0:T(128)} %stack.83.sc, bf16[128,2048]{1,0:T(8,128)(2,1)} %get-tuple-element.967.refs_0_, bf16[128,2048]{1,0:T(8,128)(2,1)} %copy-done.28, ...), custom_call_target="tpu_custom_call" | custom-call | flops 3000000000 | bytes 1024 | tf_op jit(solution)/shard_map/pallas_call | solution.py:551
  289.1 8.2 %shard_map.254 = (bf16[256,1408]{1,0:T(8,128)(2,1)}, bf16[256,1408]{1,0:T(8,128)(2,1)}, bf16[512,1408]{1,0:T(8,128)(2,1)}) custom-call(s32[5]{0:T(128)} %stack.83.sc, bf16[1024,2048]{1,0:T(8,128)(2,1)} %get-tuple-element.1029.h, bf16[1024,1408]{1,0:T(8,128)(2,1)} %get-tuple-element.1020.d), custom_call_target="tpu_custom_call" | custom-call | flops 700000000 | bytes 1024 | tf_op jit(solution)/shard_map/pallas_call | solution.py:761
  305.1 8.1 %shard_map.256 = (bf16[256,1408]{1,0:T(8,128)(2,1)}, bf16[256,1408]{1,0:T(8,128)(2,1)}, bf16[512,1408]{1,0:T(8,128)(2,1)}) custom-call(s32[5]{0:T(128)} %stack.83.sc, bf16[1024,2048]{1,0:T(8,128)(2,1)} %get-tuple-element.1029.h, bf16[1024,1408]{1,0:T(8,128)(2,1)} %get-tuple-element.1020.d), custom_call_target="tpu_custom_call" | custom-call | flops 700000000 | bytes 1024 | tf_op jit(solution)/shard_map/pallas_call | solution.py:761
  313.3 9.8 %shard_map.257 = (bf16[512,2048]{1,0:T(8,128)(2,1)}, bf16[512,2048]{1,0:T(8,128)(2,1)}) custom-call(s32[5]{0:T(128)} %stack.83.sc, bf16[1024,704]{1,0:T(8,128)(2,1)} %get-tuple-element.1063.act.a, bf16[176,2048]{1,0:T(8,128)(2,1)} %refs_0_.3, bf16[80,2048]{1,0:T(8,128)(2,1)} %copy-done.26, bf16[96,2048]{1,0:T(8,128)(2,1)} %copy-done.22, ...), custom_call_target="tpu_custom_call" | custom-call | flops 900000000 | bytes 1024 | tf_op jit(solution)/shard_map/pallas_call | solution.py:605
  332.4 9.9 %shard_map.258 = (bf16[176,2048]{1,0:T(8,128)(2,1)}, bf16[176,2048]{1,0:T(8,128)(2,1)}, bf16[176,2048]{1,0:T(8,128)(2,1)}, bf16[176,2048]{1,0:T(8,128)(2,1)}) custom-call(s32[5]{0:T(128)} %stack.83.sc, bf16[1024,704]{1,0:T(8,128)(2,1)} %get-tuple-element.1063.act.a, bf16[512,2048]{1,0:T(8,128)(2,1)} %bitcast.75, bf16[512,2048]{1,0:T(8,128)(2,1)} %copy-done.5), custom_call_target="tpu_custom_call" | custom-call | flops 900000000 | bytes 1024 | tf_op jit(solution)/shard_map/pallas_call | solution.py:801
  359.5 9.8 %collective-permute-done.57 = bf16[128,1408]{1,0:T(8,128)(2,1)S(1)} collective-permute-done((bf16[128,1408]{1,0:T(8,128)(2,1)S(1)}, bf16[128,1408]{1,0:T(8,128)(2,1)S(1)}, u32[]{:S(2)}, u32[]{:S(2)}) %collective-permute-start.57) | collective-permute-done | bytes 360480 | tf_op jit(solution)/shard_map/ppermute | solution.py:52
  376.3 9.9 %collective-permute-done.58.refs_3_ = bf16[64,2048]{1,0:T(8,128)(2,1)S(1)} collective-permute-done((bf16[64,2048]{1,0:T(8,128)(2,1)S(1)}, bf16[64,2048]{1,0:T(8,128)(2,1)S(1)}, u32[]{:S(2)}, u32[]{:S(2)}) %collective-permute-start.58) | collective-permute-done | bytes 262176 | tf_op jit(solution)/shard_map/ppermute | solution.py:56
  400.8 25.3 %shard_map.261 = (bf16[1024,768]{1,0:T(8,128)(2,1)}, f32[1,768]{1,0:T(1,128)}, f32[2,2048]{1,0:T(2,128)}, bf16[512,2048]{1,0:T(8,128)(2,1)}, bf16[512,2048]{1,0:T(8,128)(2,1)}) custom-call(s32[5]{0:T(128)} %stack.83.sc, f32[3,512,512]{2,1,0:T(8,128)} %pad_maximum_fusion.tables, s32[2,512]{1,0:T(2,128)} %reshape.395.id_row, s32[1024,1]{1,0:T(8,128)} %copy.40.id_col, ...), custom_call_target="tpu_custom_call" | custom-call | flops 2300000000 | bytes 1024 | tf_op jit(solution)/shard_map/pallas_call | solution.py:702
  432.4 5.6 shard_map.262
  451.0 5.5 shard_map.265
  456.6 7.4 %shard_map.264 = (bf16[64,2048]{1,0:T(8,128)(2,1)}, bf16[64,2048]{1,0:T(8,128)(2,1)}, bf16[64,2048]{1,0:T(8,128)(2,1)}, bf16[64,2048]{1,0:T(8,128)(2,1)}) custom-call(s32[5]{0:T(128)} %stack.83.sc, bf16[1024,256]{1,0:T(8,128)(2,1)} %get-tuple-element.1290.a, bf16[128,2048]{1,0:T(8,128)(2,1)} %get-tuple-element.1260.refs_0_, bf16[128,2048]{1,0:T(8,128)(2,1)} %copy-done.12, ...), custom_call_target="tpu_custom_call" | custom-call | flops 900000000 | bytes 1024 | tf_op jit(solution)/shard_map/pallas_call | solution.py:801
  478.5 6.5 %collective-permute-done.77 = f32[7,1024]{1,0:T(8,128)S(1)} collective-permute-done((f32[7,1024]{1,0:T(8,128)S(1)}, f32[7,1024]{1,0:T(8,128)S(1)}, u32[]{:S(2)}, u32[]{:S(2)}) %collective-permute-start.77) | collective-permute-done | bytes 28704 | tf_op jit(solution)/shard_map/ppermute | solution.py:48
  540.0 7.9 %collective-permute-done.87 = f32[7,128]{1,0:T(8,128)S(1)} collective-permute-done((f32[7,128]{1,0:T(8,128)S(1)}, f32[7,128]{1,0:T(8,128)S(1)}, u32[]{:S(2)}, u32[]{:S(2)}) %collective-permute-start.87) | collective-permute-done | bytes 3616 | tf_op jit(solution)/shard_map/ppermute | solution.py:52
  549.7 8.8 %collective-permute-done.86 = bf16[64,2048]{1,0:T(8,128)(2,1)S(1)} collective-permute-done((bf16[64,2048]{1,0:T(8,128)(2,1)S(1)}, bf16[64,2048]{1,0:T(8,128)(2,1)S(1)}, u32[]{:S(2)}, u32[]{:S(2)}) %collective-permute-start.86) | collective-permute-done | bytes 262176 | tf_op jit(solution)/shard_map/ppermute | solution.py:52
  (469 shorter events, 277.1 us)
Async XLA Ops:
  5.0 25.8 %collective-permute-start.2 = (bf16[64,2048]{1,0:T(8,128)(2,1)}, bf16[64,2048]{1,0:T(8,128)(2,1)}, u32[]{:S(2)}, u32[]{:S(2)}) collective-permute-start(bf16[64,2048]{1,0:T(8,128)(2,1)} %param.23), channel_id=1, source_target_pairs={{0,2},{2,0},{1,3},{3,1},{4,6},{6,4},{5,7},{7,5},{8,10},{10,8},{9,1... | collective-permute-start | bytes 786440 | tf_op jit(solution)/shard_map/ppermute | solution.py:52
  31.6 53.6 %collective-permute-start.5 = (bf16[4,2,72,768]{3,2,1,0:T(8,128)(2,1)S(1)}, bf16[4,2,72,768]{3,2,1,0:T(8,128)(2,1)}, u32[]{:S(2)}, u32[]{:S(2)}) collective-permute-start(bf16[4,2,72,768]{3,2,1,0:T(8,128)(2,1)S(1)} %bitcast.82), channel_id=1, source_target_pairs={{0,2},{2,0},{1,3},{3,1},{4,6},{6,4},{5,7},{7,5},{8,10},{10,8},{9,1... | collective-permute-start | bytes 2654216 | tf_op jit(solution)/shard_map/ppermute | solution.py:52
  31.6 53.6 %collective-permute-start.6 = (bf16[4,2,72,768]{3,2,1,0:T(8,128)(2,1)S(1)}, bf16[4,2,72,768]{3,2,1,0:T(8,128)(2,1)}, u32[]{:S(2)}, u32[]{:S(2)}) collective-permute-start(bf16[4,2,72,768]{3,2,1,0:T(8,128)(2,1)S(1)} %bitcast.83), channel_id=1, source_target_pairs={{0,16},{16,0},{1,17},{17,1},{2,18},{18,2},{3,19},{19,3},{4,20},{20... | collective-permute-start | bytes 2654216 | tf_op jit(solution)/shard_map/ppermute | solution.py:48
  32.7 52.6 %all-to-all-start.1 = ((bf16[8,64,1408]{2,1,0:T(8,128)(2,1)}), bf16[8,64,1408]{2,1,0:T(8,128)(2,1)S(1)}, u32[]{:S(2)}, u32[]{:S(2)}) async-start(bf16[8,64,1408]{2,1,0:T(8,128)(2,1)} %shard_map.248), calls=%async_computation.1 | async-start | bytes 2883584 | tf_op jit(solution)/shard_map/all_to_all | solution.py:919
  38.2 27.2 %collective-permute-start.7 = (bf16[128,2048]{1,0:T(8,128)(2,1)S(1)}, bf16[128,2048]{1,0:T(8,128)(2,1)}, u32[]{:S(2)}, u32[]{:S(2)}) collective-permute-start(bf16[128,2048]{1,0:T(8,128)(2,1)S(1)} %pad_maximum_fusion.4.refs_0_.x), channel_id=1, source_target_pairs={{0,8},{8,0},{1,9},{9,1},{2,10},{10,2},{3,11},{11,3},{4,12},{12,4},... | collective-permute-start | bytes 1572872 | tf_op jit(solution)/shard_map/ppermute | solution.py:65
  40.3 45.0 %collective-permute-start.8 = (bf16[128,2048]{1,0:T(8,128)(2,1)S(1)}, bf16[128,2048]{1,0:T(8,128)(2,1)}, u32[]{:S(2)}, u32[]{:S(2)}) collective-permute-start(bf16[128,2048]{1,0:T(8,128)(2,1)S(1)} %pad_maximum_fusion.4.refs_0_.x), channel_id=1, source_target_pairs={{0,1},{1,0},{2,3},{3,2},{4,5},{5,4},{6,7},{7,6},{8,9},{9,8},{10,11... | collective-permute-start | bytes 1572872 | tf_op jit(solution)/shard_map/ppermute | solution.py:56
  58.3 27.0 %collective-permute-start.9 = (bf16[128,2048]{1,0:T(8,128)(2,1)S(1)}, bf16[128,2048]{1,0:T(8,128)(2,1)}, u32[]{:S(2)}, u32[]{:S(2)}) collective-permute-start(bf16[128,2048]{1,0:T(8,128)(2,1)S(1)} %pad_maximum_fusion.4.refs_0_.x), channel_id=1, source_target_pairs={{0,4},{4,0},{1,5},{5,1},{2,6},{6,2},{3,7},{7,3},{8,12},{12,8},{9,1... | collective-permute-start | bytes 1572872 | tf_op jit(solution)/shard_map/ppermute | solution.py:60
  88.1 22.9 %collective-permute-start.14 = (bf16[128,2048]{1,0:T(8,128)(2,1)}, bf16[128,2048]{1,0:T(8,128)(2,1)S(1)}, u32[]{:S(2)}, u32[]{:S(2)}) collective-permute-start(bf16[128,2048]{1,0:T(8,128)(2,1)} %collective-permute-done.7.refs_1_), channel_id=1, source_target_pairs={{0,4},{4,0},{1,5},{5,1},{2,6},{6,2},{3,7},{7,3},{8,12},{12,8},{9,1... | collective-permute-start | bytes 1572872 | tf_op jit(solution)/shard_map/ppermute | solution.py:60
  89.4 22.4 %collective-permute-start.11 = (bf16[4,2,72,768]{3,2,1,0:T(8,128)(2,1)}, bf16[4,2,72,768]{3,2,1,0:T(8,128)(2,1)}, u32[]{:S(2)}, u32[]{:S(2)}) collective-permute-start(bf16[4,2,72,768]{3,2,1,0:T(8,128)(2,1)} %collective-permute-done.5.refs_11_), channel_id=1, source_target_pairs={{0,16},{16,0},{1,17},{17,1},{2,18},{18,2},{3,19},{19,3},{4,20},{20... | collective-permute-start | bytes 2654216 | tf_op jit(solution)/shard_map/ppermute | solution.py:48
  112.5 44.6 %all-to-all-start.2 = ((bf16[4,128,2048]{2,1,0:T(8,128)(2,1)}), bf16[4,128,2048]{2,1,0:T(8,128)(2,1)S(1)}, u32[]{:S(2)}, u32[]{:S(2)}) async-start(bf16[4,128,2048]{2,1,0:T(8,128)(2,1)} %broadcast_in_dim.70), calls=%async_computation.2 | async-start | bytes 4194304 | tf_op jit(solution)/shard_map/all_to_all | solution.py:69
  116.7 38.3 %collective-permute-start.19 = (bf16[4,2,64,1408]{3,2,1,0:T(8,128)(2,1)S(1)}, bf16[4,2,64,1408]{3,2,1,0:T(8,128)(2,1)}, u32[]{:S(2)}, u32[]{:S(2)}) collective-permute-start(bf16[4,2,64,1408]{3,2,1,0:T(8,128)(2,1)S(1)} %bitcast.78), channel_id=1, source_target_pairs={{0,16},{16,0},{1,17},{17,1},{2,18},{18,2},{3,19},{19,3},{4,20},{20... | collective-permute-start | bytes 4325384 | tf_op jit(solution)/shard_map/ppermute | solution.py:48
  117.7 37.3 %collective-permute-start.18 = (bf16[2,2,64,1408]{3,2,1,0:T(8,128)(2,1)}, bf16[2,2,64,1408]{3,2,1,0:T(8,128)(2,1)}, u32[]{:S(2)}, u32[]{:S(2)}) collective-permute-start(bf16[2,2,64,1408]{3,2,1,0:T(8,128)(2,1)} %slice.115), channel_id=1, source_target_pairs={{0,2},{2,0},{1,3},{3,1},{4,6},{6,4},{5,7},{7,5},{8,10},{10,8},{9,1... | collective-permute-start | bytes 2162696 | tf_op jit(solution)/shard_map/ppermute | solution.py:52
  165.6 28.6 %collective-permute-start.26 = (bf16[2,2,64,1408]{3,2,1,0:T(8,128)(2,1)}, bf16[2,2,64,1408]{3,2,1,0:T(8,128)(2,1)S(1)}, u32[]{:S(2)}, u32[]{:S(2)}) collective-permute-start(bf16[2,2,64,1408]{3,2,1,0:T(8,128)(2,1)} %collective-permute-done.18.refs_15_), channel_id=1, source_target_pairs={{0,16},{16,0},{1,17},{17,1},{2,18},{18,2},{3,19},{19,3},{4,20},{20... | collective-permute-start | bytes 2162696 | tf_op jit(solution)/shard_map/ppermute | solution.py:48
  195.0 24.9 %collective-permute-start.28 = (bf16[176,2048]{1,0:T(8,128)(2,1)S(1)}, bf16[176,2048]{1,0:T(8,128)(2,1)S(1)}, u32[]{:S(2)}, u32[]{:S(2)}) collective-permute-start(bf16[176,2048]{1,0:T(8,128)(2,1)S(1)} %copy-done.9), channel_id=1, source_target_pairs={{0,16},{16,0},{1,17},{17,1},{2,18},{18,2},{3,19},{19,3},{4,20},{20... | collective-permute-start | bytes 2162696 | tf_op jit(solution)/shard_map/ppermute | solution.py:48
  196.0 23.9 %collective-permute-start.27 = (bf16[96,2048]{1,0:T(8,128)(2,1)}, bf16[96,2048]{1,0:T(8,128)(2,1)S(1)}, u32[]{:S(2)}, u32[]{:S(2)}) collective-permute-start(bf16[96,2048]{1,0:T(8,128)(2,1)} %slice.111), channel_id=1, source_target_pairs={{0,2},{2,0},{1,3},{3,1},{4,6},{6,4},{5,7},{7,5},{8,10},{10,8},{9,1... | collective-permute-start | bytes 1179656 | tf_op jit(solution)/shard_map/ppermute | solution.py:52
  297.3 25.8 %collective-permute-start.47 = (bf16[256,1408]{1,0:T(8,128)(2,1)}, bf16[256,1408]{1,0:T(8,128)(2,1)S(1)}, u32[]{:S(2)}, u32[]{:S(2)}) collective-permute-start(bf16[256,1408]{1,0:T(8,128)(2,1)} %get-tuple-element.1027), channel_id=1, source_target_pairs={{0,16},{16,0},{1,17},{17,1},{2,18},{18,2},{3,19},{19,3},{4,20},{20... | collective-permute-start | bytes 2162696 | tf_op jit(solution)/shard_map/ppermute | solution.py:48
  394.1 38.1 %all-to-all-start.3 = ((bf16[4,128,2048]{2,1,0:T(8,128)(2,1)}), bf16[4,128,2048]{2,1,0:T(8,128)(2,1)S(1)}, u32[]{:S(2)}, u32[]{:S(2)}) async-start(bf16[4,128,2048]{2,1,0:T(8,128)(2,1)} %bitcast.29), calls=%async_computation.3 | async-start | bytes 4194304 | tf_op jit(solution)/shard_map/all_to_all | solution.py:69
  397.9 34.3 %collective-permute-start.66 = (bf16[512,1408]{1,0:T(8,128)(2,1)}, bf16[512,1408]{1,0:T(8,128)(2,1)S(1)}, u32[]{:S(2)}, u32[]{:S(2)}) collective-permute-start(bf16[512,1408]{1,0:T(8,128)(2,1)} %get-tuple-element.1211), channel_id=1, source_target_pairs={{0,16},{16,0},{1,17},{17,1},{2,18},{18,2},{3,19},{19,3},{4,20},{20... | collective-permute-start | bytes 4325384 | tf_op jit(solution)/shard_map/ppermute | solution.py:48
  399.2 30.0 %collective-permute-start.67 = (bf16[128,1408]{1,0:T(8,128)(2,1)}, bf16[128,1408]{1,0:T(8,128)(2,1)}, u32[]{:S(2)}, u32[]{:S(2)}) collective-permute-start(bf16[128,1408]{1,0:T(8,128)(2,1)} %get-tuple-element.1210), channel_id=1, source_target_pairs={{0,2},{2,0},{1,3},{3,1},{4,6},{6,4},{5,7},{7,5},{8,10},{10,8},{9,1... | collective-permute-start | bytes 1081352 | tf_op jit(solution)/shard_map/ppermute | solution.py:52
  438.0 26.7 %collective-permute-start.69 = (bf16[96,2048]{1,0:T(8,128)(2,1)}, bf16[96,2048]{1,0:T(8,128)(2,1)}, u32[]{:S(2)}, u32[]{:S(2)}) collective-permute-start(bf16[96,2048]{1,0:T(8,128)(2,1)} %slice.147), channel_id=1, source_target_pairs={{0,2},{2,0},{1,3},{3,1},{4,6},{6,4},{5,7},{7,5},{8,10},{10,8},{9,1... | collective-permute-start | bytes 1179656 | tf_op jit(solution)/shard_map/ppermute | solution.py:52
  465.6 23.4 %collective-permute-start.75 = (bf16[512,768]{1,0:T(8,128)(2,1)}, bf16[512,768]{1,0:T(8,128)(2,1)S(1)}, u32[]{:S(2)}, u32[]{:S(2)}) collective-permute-start(bf16[512,768]{1,0:T(8,128)(2,1)} %get-tuple-element.1327), channel_id=1, source_target_pairs={{0,16},{16,0},{1,17},{17,1},{2,18},{18,2},{3,19},{19,3},{4,20},{20... | collective-permute-start | bytes 2359304 | tf_op jit(solution)/shard_map/ppermute | solution.py:48
  490.1 31.3 %all-to-all-start.4 = ((bf16[8,64,1408]{2,1,0:T(8,128)(2,1)}), bf16[8,64,1408]{2,1,0:T(8,128)(2,1)S(1)}, u32[]{:S(2)}, u32[]{:S(2)}) async-start(bf16[8,64,1408]{2,1,0:T(8,128)(2,1)} %bitcast.86), calls=%async_computation.4 | async-start | bytes 2883584 | tf_op jit(solution)/shard_map/all_to_all | solution.py:919
  529.8 29.5 %collective-permute-start.84 = (bf16[80,2048]{1,0:T(8,128)(2,1)S(1)}, bf16[80,2048]{1,0:T(8,128)(2,1)S(1)}, u32[]{:S(2)}, u32[]{:S(2)}) collective-permute-start(bf16[80,2048]{1,0:T(8,128)(2,1)S(1)} %copy-done.67), channel_id=1, source_target_pairs={{0,2},{2,0},{1,3},{3,1},{4,6},{6,4},{5,7},{7,5},{8,10},{10,8},{9,1... | collective-permute-start | bytes 983048 | tf_op jit(solution)/shard_map/ppermute | solution.py:52
  532.2 27.1 %all-to-all-start.5 = ((bf16[8,64,768]{2,1,0:T(8,128)(2,1)}), bf16[8,64,768]{2,1,0:T(8,128)(2,1)S(1)}, u32[]{:S(2)}, u32[]{:S(2)}) async-start(bf16[8,64,768]{2,1,0:T(8,128)(2,1)} %bitcast.41), calls=%async_computation.5 | async-start | bytes 1572864 | tf_op jit(solution)/shard_map/all_to_all | solution.py:919
  (162 other events, 1859.6 us)

commit v5 on v4

--- a/solution.py
+++ b/solution.py
@@ -37,7 +37,7 @@
 
 
 def cost(microseconds):
-    return pl.CostEstimate(flops=int(microseconds * 1e8), bytes_accessed=1024, transcendentals=0)
+    return pl.CostEstimate(flops=int(microseconds * 2e8), bytes_accessed=1024, transcendentals=0)
 
 
 def dot(a, b, dims=(((1,), (0,)), ((), ()))):
@@ -393,7 +393,7 @@
     h1[...] = h
     lin = dot(h, w[...].reshape(D, 3 * wide)) + bias_q[...]
     qk = turn(lin[:, : 2 * wide], tables[0], tables[1], tables[2], 1.0)
-    q[rows, :] = qk[:, :wide].astype(BF16)
+    q[rows, :] = (qk[:, :wide] * (HD**-0.5)).astype(BF16)
     k[rows, :] = qk[:, wide:].astype(BF16)
     v[rows, :] = lin[:, 2 * wide :].astype(BF16)
 
@@ -409,7 +409,7 @@
                 lanes = slice(hd * HD, (hd + 1) * HD)
                 kh = k[pl.ds(start, length), lanes]
                 vh = v[pl.ds(start, length), lanes]
-                score = dot(q[part, lanes], kh, NT) * (HD**-0.5)
+                score = dot(q[part, lanes], kh, NT)
                 score = jnp.where(allowed, score, masked_score)
                 peak = jnp.max(score, axis=-1, keepdims=True)
                 e = jnp.exp(score - peak)
@@ -652,14 +652,14 @@
                 local = pl.ds(r * step, step)
                 allowed = id_col[part, 0:1] >= id_row[s : s + 1, :]
                 qh = q[part, lanes]
-                score = dot(qh, kh, NT) * scale
+                score = dot(qh, kh, NT)
                 p = jnp.where(allowed, jnp.exp(score - lse[part, hd : hd + 1]), 0.0)
                 doh = d_o[local, lanes]
                 dp = dot(doh, vh, NT)
                 inner = jnp.sum(p * dp, axis=-1, keepdims=True)
                 ds = (p * (dp - inner)).astype(BF16)
                 d_qk[local, lanes] = dot(ds, kh) * scale
-                dk = dot(ds, qh, TN) * scale
+                dk = dot(ds, qh, TN)
                 dv = dot(p.astype(BF16), doh, TN)
                 if length == step:
                     d_qk[:, k_lanes] = dk

time: 576 us -> 575 us (level)
    unnamed x183 -> x181, local copies, waits for them, and re-layouts: 13.9 us -> 11.4 us
  transfers between devices with their start and end apart: 95 -> 95, of which waited for: 35 -> 37; matrix products, arithmetic and copies ran while one was open for 8% -> 8% of each run, Pallas kernels for 24% -> 24%
where the time goes in v5:
time: 575 us; the launch traced here: 567 us
  waiting for transfers between devices  207 us (36%)
  Pallas kernels  183 us (32%)
  starting transfers between devices  107 us (19%)
  other arithmetic  36.3 us (6%)
  local copies, waits for them, and re-layouts  31 us (5%)
    ppermute x17, waiting for transfers between devices, swap_fh(): return lax.ppermute(v, 'fh', SWAP)  80.5 us
    ppermute x14, waiting for transfers between devices, swap_fl(): return lax.ppermute(v, 'fl', SWAP)  67.6 us
    ppermute x24, waiting for transfers between devices, swap_sb(): return lax.ppermute(v, 'sb', SWAP)  34 us
    pallas_call x1, Pallas kernels, ffn(): pl.pallas_call(functools.partial(ffn_kernel, dims, h_rows, dy_rows), grid...  31.2 us
    pallas_call x4, Pallas kernels, grad_rows(): pl.pallas_call(functools.partial(rows_kernel, (n, 2 * rows)), grid_spec=s...  27.4 us
    pallas_call x1, Pallas kernels, attention(): pl.pallas_call(functools.partial(attention_kernel, (heads, length, block,...  25.5 us
    pallas_call x1, Pallas kernels, attention_back(): pl.pallas_call(functools.partial(attention_back_kernel, dims, d_rows), ou...  25.2 us
    ppermute x17, starting transfers between devices, swap_fh(): return lax.ppermute(v, 'fh', SWAP)  24.2 us
  transfers between devices with their start and end apart: 95, of which 37 were waited for; matrix products, arithmetic and copies ran while one was open for 8% of the time, Pallas kernels for 24%

profile of v5, /device:TPU:0, one launch (start us, length us, event | category | flops | bytes accessed | tf_op | source)
XLA Modules:
  0.0 566.7 jit_solution(18177850549928148121)
XLA Ops:
  43.7 14.4 %collective-permute-done.4 = bf16[64,2048]{1,0:T(8,128)(2,1)S(1)} collective-permute-done((bf16[64,2048]{1,0:T(8,128)(2,1)}, bf16[64,2048]{1,0:T(8,128)(2,1)S(1)}, u32[]{:S(2)}, u32[]{:S(2)}) %collective-permute-start.4) | collective-permute-done | bytes 262176 | tf_op jit(solution)/shard_map/ppermute | solution.py:48
  60.9 4.7 collective-permute-done.7.refs_1_
  65.6 19.8 %collective-permute-done.8.refs_2_ = bf16[128,2048]{1,0:T(8,128)(2,1)} collective-permute-done((bf16[128,2048]{1,0:T(8,128)(2,1)S(1)}, bf16[128,2048]{1,0:T(8,128)(2,1)}, u32[]{:S(2)}, u32[]{:S(2)}) %collective-permute-start.8) | collective-permute-done | bytes 524320 | tf_op jit(solution)/shard_map/ppermute | solution.py:56
  96.7 7.0 %collective-permute-done.12.refs_3_ = bf16[64,2048]{1,0:T(8,128)(2,1)S(1)} collective-permute-done((bf16[64,2048]{1,0:T(8,128)(2,1)S(1)}, bf16[64,2048]{1,0:T(8,128)(2,1)S(1)}, u32[]{:S(2)}, u32[]{:S(2)}) %collective-permute-start.12) | collective-permute-done | bytes 262176 | tf_op jit(solution)/shard_map/ppermute | solution.py:56
  120.5 25.5 %shard_map.249 = (bf16[1024,2048]{1,0:T(8,128)(2,1)}, bf16[1024,256]{1,0:T(8,128)(2,1)}, bf16[1024,256]{1,0:T(8,128)(2,1)}, bf16[1024,256]{1,0:T(8,128)(2,1)}, b...) custom-call(s32[5]{0:T(128)} %stack.83.sc, ...), custom_call_target="tpu_custom_call" | custom-call | flops 5000000000 | bytes 1024 | tf_op jit(solution)/shard_map/pallas_call | solution.py:458
  145.9 9.2 %collective-permute-done.18.refs_15_ = bf16[2,2,64,1408]{3,2,1,0:T(8,128)(2,1)} collective-permute-done((bf16[2,2,64,1408]{3,2,1,0:T(8,128)(2,1)}, bf16[2,2,64,1408]{3,2,1,0:T(8,128)(2,1)}, u32[]{:S(2)}, u32[]{:S(2)}) %collective-permute-start.18) | collective-permute-done | bytes 720928 | tf_op jit(solution)/shard_map/ppermute | solution.py:52
  157.7 6.6 %collective-permute-done.20.refs_11_.refs_1_ = bf16[512,2048]{1,0:T(8,128)(2,1)S(1)} collective-permute-done((bf16[512,2048]{1,0:T(8,128)(2,1)S(1)}, bf16[512,2048]{1,0:T(8,128)(2,1)S(1)}, u32[]{:S(2)}, u32[]{:S(2)}) %collective-permute-start.20) | collective-permute-done | bytes 2097184 | tf_op jit(solution)/shard_map/ppermute | solution.py:60
  174.1 17.6 %collective-permute-done.24.refs_16_ = bf16[1,2,64,1408]{3,2,1,0:T(8,128)(2,1)S(1)} collective-permute-done((bf16[1,2,64,1408]{3,2,1,0:T(8,128)(2,1)}, bf16[1,2,64,1408]{3,2,1,0:T(8,128)(2,1)S(1)}, u32[]{:S(2)}, u32[]{:S(2)}) %collective-permute-start.24) | collective-permute-done | bytes 360480 | tf_op jit(solution)/shard_map/ppermute | solution.py:52
  201.5 12.2 %collective-permute-done.29.u1 = bf16[64,2048]{1,0:T(8,128)(2,1)S(1)} collective-permute-done((bf16[64,2048]{1,0:T(8,128)(2,1)}, bf16[64,2048]{1,0:T(8,128)(2,1)S(1)}, u32[]{:S(2)}, u32[]{:S(2)}) %collective-permute-start.29) | collective-permute-done | bytes 262176 | tf_op jit(solution)/shard_map/ppermute | solution.py:56
  224.8 14.1 %collective-permute-done.32.refs_21_.refs_1_ = bf16[80,2048]{1,0:T(8,128)(2,1)S(1)} collective-permute-done((bf16[80,2048]{1,0:T(8,128)(2,1)S(1)}, bf16[80,2048]{1,0:T(8,128)(2,1)S(1)}, u32[]{:S(2)}, u32[]{:S(2)}) %collective-permute-start.32) | collective-permute-done | bytes 327712 | tf_op jit(solution)/shard_map/ppermute | solution.py:52
  255.9 31.2 %shard_map.253 = (bf16[1024,2048]{1,0:T(8,128)(2,1)}, bf16[1024,704]{1,0:T(8,128)(2,1)}, bf16[1024,1408]{1,0:T(8,128)(2,1)}, bf16[512,2048]{1,0:T(8,128)(2,1)}, bf16[512,2048]{1,0:T(8,128)(2,1)}) custom-call(s32[5]{0:T(128)} %stack.83.sc, bf16[128,2048]{1,0:T(8,128)(2,1)} %get-tuple-element.967.refs_0_, bf16[128,2048]{1,0:T(8,128)(2,1)} %copy-done.59, ...), custom_call_target="tpu_custom_call" | custom-call | flops 6000000000 | bytes 1024 | tf_op jit(solution)/shard_map/pallas_call | solution.py:551
  287.3 8.2 %shard_map.254 = (bf16[256,1408]{1,0:T(8,128)(2,1)}, bf16[256,1408]{1,0:T(8,128)(2,1)}, bf16[512,1408]{1,0:T(8,128)(2,1)}) custom-call(s32[5]{0:T(128)} %stack.83.sc, bf16[1024,2048]{1,0:T(8,128)(2,1)} %get-tuple-element.1029.h, bf16[1024,1408]{1,0:T(8,128)(2,1)} %get-tuple-element.1020.d), custom_call_target="tpu_custom_call" | custom-call | flops 1400000000 | bytes 1024 | tf_op jit(solution)/shard_map/pallas_call | solution.py:761
  302.6 8.1 %shard_map.256 = (bf16[256,1408]{1,0:T(8,128)(2,1)}, bf16[256,1408]{1,0:T(8,128)(2,1)}, bf16[512,1408]{1,0:T(8,128)(2,1)}) custom-call(s32[5]{0:T(128)} %stack.83.sc, bf16[1024,2048]{1,0:T(8,128)(2,1)} %get-tuple-element.1029.h, bf16[1024,1408]{1,0:T(8,128)(2,1)} %get-tuple-element.1020.d), custom_call_target="tpu_custom_call" | custom-call | flops 1400000000 | bytes 1024 | tf_op jit(solution)/shard_map/pallas_call | solution.py:761
  310.7 9.8 %shard_map.257 = (bf16[512,2048]{1,0:T(8,128)(2,1)}, bf16[512,2048]{1,0:T(8,128)(2,1)}) custom-call(s32[5]{0:T(128)} %stack.83.sc, bf16[1024,704]{1,0:T(8,128)(2,1)} %get-tuple-element.1063.act.a, bf16[176,2048]{1,0:T(8,128)(2,1)} %refs_0_.3, bf16[80,2048]{1,0:T(8,128)(2,1)} %copy-done.79, bf16[96,2048]{1,0:T(8,128)(2,1)} %copy-done.73, ...), custom_call_target="tpu_custom_call" | custom-call | flops 1800000000 | bytes 1024 | tf_op jit(solution)/shard_map/pallas_call | solution.py:605
  330.1 10.0 %shard_map.258 = (bf16[176,2048]{1,0:T(8,128)(2,1)}, bf16[176,2048]{1,0:T(8,128)(2,1)}, bf16[176,2048]{1,0:T(8,128)(2,1)}, bf16[176,2048]{1,0:T(8,128)(2,1)}) custom-call(s32[5]{0:T(128)} %stack.83.sc, bf16[1024,704]{1,0:T(8,128)(2,1)} %get-tuple-element.1063.act.a, bf16[512,2048]{1,0:T(8,128)(2,1)} %bitcast.86, bf16[512,2048]{1,0:T(8,128)(2,1)} %copy-done.67), custom_call_target="tpu_custom_call" | custom-call | flops 1800000000 | bytes 1024 | tf_op jit(solution)/shard_map/pallas_call | solution.py:801
  357.2 9.6 %collective-permute-done.57 = bf16[128,1408]{1,0:T(8,128)(2,1)S(1)} collective-permute-done((bf16[128,1408]{1,0:T(8,128)(2,1)S(1)}, bf16[128,1408]{1,0:T(8,128)(2,1)S(1)}, u32[]{:S(2)}, u32[]{:S(2)}) %collective-permute-start.57) | collective-permute-done | bytes 360480 | tf_op jit(solution)/shard_map/ppermute | solution.py:52
  373.6 9.5 %collective-permute-done.58.refs_3_ = bf16[64,2048]{1,0:T(8,128)(2,1)S(1)} collective-permute-done((bf16[64,2048]{1,0:T(8,128)(2,1)S(1)}, bf16[64,2048]{1,0:T(8,128)(2,1)S(1)}, u32[]{:S(2)}, u32[]{:S(2)}) %collective-permute-start.58) | collective-permute-done | bytes 262176 | tf_op jit(solution)/shard_map/ppermute | solution.py:56
  397.9 25.2 %shard_map.261 = (bf16[1024,768]{1,0:T(8,128)(2,1)}, f32[1,768]{1,0:T(1,128)}, f32[2,2048]{1,0:T(2,128)}, bf16[512,2048]{1,0:T(8,128)(2,1)}, bf16[512,2048]{1,0:T(8,128)(2,1)}) custom-call(s32[5]{0:T(128)} %stack.83.sc, f32[3,512,512]{2,1,0:T(8,128)} %pad_maximum_fusion.tables, s32[2,512]{1,0:T(2,128)} %reshape.395.id_row, s32[1024,1]{1,0:T(8,128)} %copy.40.id_col, ...), custom_call_target="tpu_custom_call" | custom-call | flops 4600000000 | bytes 1024 | tf_op jit(solution)/shard_map/pallas_call | solution.py:702
  430.0 5.6 shard_map.262
  448.0 5.6 shard_map.265
  453.6 7.5 %shard_map.264 = (bf16[64,2048]{1,0:T(8,128)(2,1)}, bf16[64,2048]{1,0:T(8,128)(2,1)}, bf16[64,2048]{1,0:T(8,128)(2,1)}, bf16[64,2048]{1,0:T(8,128)(2,1)}) custom-call(s32[5]{0:T(128)} %stack.83.sc, bf16[1024,256]{1,0:T(8,128)(2,1)} %get-tuple-element.1290.a, bf16[128,2048]{1,0:T(8,128)(2,1)} %get-tuple-element.1260.refs_0_, bf16[128,2048]{1,0:T(8,128)(2,1)} %copy-done.14, ...), custom_call_target="tpu_custom_call" | custom-call | flops 1800000000 | bytes 1024 | tf_op jit(solution)/shard_map/pallas_call | solution.py:801
  476.3 7.0 %collective-permute-done.77 = f32[7,1024]{1,0:T(8,128)} collective-permute-done((f32[7,1024]{1,0:T(8,128)}, f32[7,1024]{1,0:T(8,128)}, u32[]{:S(2)}, u32[]{:S(2)}) %collective-permute-start.77) | collective-permute-done | bytes 28704 | tf_op jit(solution)/shard_map/ppermute | solution.py:48
  537.6 7.4 %collective-permute-done.87 = f32[7,128]{1,0:T(8,128)S(1)} collective-permute-done((f32[7,128]{1,0:T(8,128)S(1)}, f32[7,128]{1,0:T(8,128)S(1)}, u32[]{:S(2)}, u32[]{:S(2)}) %collective-permute-start.87) | collective-permute-done | bytes 3616 | tf_op jit(solution)/shard_map/ppermute | solution.py:52
  546.8 9.3 %collective-permute-done.86 = bf16[64,2048]{1,0:T(8,128)(2,1)S(1)} collective-permute-done((bf16[64,2048]{1,0:T(8,128)(2,1)S(1)}, bf16[64,2048]{1,0:T(8,128)(2,1)S(1)}, u32[]{:S(2)}, u32[]{:S(2)}) %collective-permute-start.86) | collective-permute-done | bytes 262176 | tf_op jit(solution)/shard_map/ppermute | solution.py:52
  (467 shorter events, 279.7 us)
Async XLA Ops:
  5.1 25.6 %collective-permute-start.2 = (bf16[64,2048]{1,0:T(8,128)(2,1)S(1)}, bf16[64,2048]{1,0:T(8,128)(2,1)S(1)}, u32[]{:S(2)}, u32[]{:S(2)}) collective-permute-start(bf16[64,2048]{1,0:T(8,128)(2,1)S(1)} %copy-done.54), channel_id=1, source_target_pairs={{0,2},{2,0},{1,3},{3,1},{4,6},{6,4},{5,7},{7,5},{8,10},{10,8},{9,1... | collective-permute-start | bytes 786440 | tf_op jit(solution)/shard_map/ppermute | solution.py:52
  31.5 53.9 %collective-permute-start.5 = (bf16[4,2,72,768]{3,2,1,0:T(8,128)(2,1)S(1)}, bf16[4,2,72,768]{3,2,1,0:T(8,128)(2,1)}, u32[]{:S(2)}, u32[]{:S(2)}) collective-permute-start(bf16[4,2,72,768]{3,2,1,0:T(8,128)(2,1)S(1)} %bitcast.80), channel_id=1, source_target_pairs={{0,2},{2,0},{1,3},{3,1},{4,6},{6,4},{5,7},{7,5},{8,10},{10,8},{9,1... | collective-permute-start | bytes 2654216 | tf_op jit(solution)/shard_map/ppermute | solution.py:52
  31.5 53.9 %collective-permute-start.6 = (bf16[4,2,72,768]{3,2,1,0:T(8,128)(2,1)S(1)}, bf16[4,2,72,768]{3,2,1,0:T(8,128)(2,1)}, u32[]{:S(2)}, u32[]{:S(2)}) collective-permute-start(bf16[4,2,72,768]{3,2,1,0:T(8,128)(2,1)S(1)} %bitcast.81), channel_id=1, source_target_pairs={{0,16},{16,0},{1,17},{17,1},{2,18},{18,2},{3,19},{19,3},{4,20},{20... | collective-permute-start | bytes 2654216 | tf_op jit(solution)/shard_map/ppermute | solution.py:48
  33.0 52.4 %all-to-all-start.1 = ((bf16[8,64,1408]{2,1,0:T(8,128)(2,1)}), bf16[8,64,1408]{2,1,0:T(8,128)(2,1)S(1)}, u32[]{:S(2)}, u32[]{:S(2)}) async-start(bf16[8,64,1408]{2,1,0:T(8,128)(2,1)} %shard_map.248), calls=%async_computation.1 | async-start | bytes 2883584 | tf_op jit(solution)/shard_map/all_to_all | solution.py:919
  38.4 27.1 %collective-permute-start.7 = (bf16[128,2048]{1,0:T(8,128)(2,1)S(1)}, bf16[128,2048]{1,0:T(8,128)(2,1)}, u32[]{:S(2)}, u32[]{:S(2)}) collective-permute-start(bf16[128,2048]{1,0:T(8,128)(2,1)S(1)} %pad_maximum_fusion.4.refs_0_.x), channel_id=1, source_target_pairs={{0,8},{8,0},{1,9},{9,1},{2,10},{10,2},{3,11},{11,3},{4,12},{12,4},... | collective-permute-start | bytes 1572872 | tf_op jit(solution)/shard_map/ppermute | solution.py:65
  40.4 45.0 %collective-permute-start.8 = (bf16[128,2048]{1,0:T(8,128)(2,1)S(1)}, bf16[128,2048]{1,0:T(8,128)(2,1)}, u32[]{:S(2)}, u32[]{:S(2)}) collective-permute-start(bf16[128,2048]{1,0:T(8,128)(2,1)S(1)} %pad_maximum_fusion.4.refs_0_.x), channel_id=1, source_target_pairs={{0,1},{1,0},{2,3},{3,2},{4,5},{5,4},{6,7},{7,6},{8,9},{9,8},{10,11... | collective-permute-start | bytes 1572872 | tf_op jit(solution)/shard_map/ppermute | solution.py:56
  58.1 27.3 %collective-permute-start.9 = (bf16[128,2048]{1,0:T(8,128)(2,1)S(1)}, bf16[128,2048]{1,0:T(8,128)(2,1)}, u32[]{:S(2)}, u32[]{:S(2)}) collective-permute-start(bf16[128,2048]{1,0:T(8,128)(2,1)S(1)} %pad_maximum_fusion.4.refs_0_.x), channel_id=1, source_target_pairs={{0,4},{4,0},{1,5},{5,1},{2,6},{6,2},{3,7},{7,3},{8,12},{12,8},{9,1... | collective-permute-start | bytes 1572872 | tf_op jit(solution)/shard_map/ppermute | solution.py:60
  88.2 23.1 %collective-permute-start.14 = (bf16[128,2048]{1,0:T(8,128)(2,1)}, bf16[128,2048]{1,0:T(8,128)(2,1)}, u32[]{:S(2)}, u32[]{:S(2)}) collective-permute-start(bf16[128,2048]{1,0:T(8,128)(2,1)} %collective-permute-done.7.refs_1_), channel_id=1, source_target_pairs={{0,4},{4,0},{1,5},{5,1},{2,6},{6,2},{3,7},{7,3},{8,12},{12,8},{9,1... | collective-permute-start | bytes 1572872 | tf_op jit(solution)/shard_map/ppermute | solution.py:60
  112.7 44.5 %all-to-all-start.2 = ((bf16[4,128,2048]{2,1,0:T(8,128)(2,1)}), bf16[4,128,2048]{2,1,0:T(8,128)(2,1)S(1)}, u32[]{:S(2)}, u32[]{:S(2)}) async-start(bf16[4,128,2048]{2,1,0:T(8,128)(2,1)} %broadcast_in_dim.70), calls=%async_computation.2 | async-start | bytes 4194304 | tf_op jit(solution)/shard_map/all_to_all | solution.py:69
  116.9 38.2 %collective-permute-start.19 = (bf16[4,2,64,1408]{3,2,1,0:T(8,128)(2,1)S(1)}, bf16[4,2,64,1408]{3,2,1,0:T(8,128)(2,1)}, u32[]{:S(2)}, u32[]{:S(2)}) collective-permute-start(bf16[4,2,64,1408]{3,2,1,0:T(8,128)(2,1)S(1)} %bitcast.75), channel_id=1, source_target_pairs={{0,16},{16,0},{1,17},{17,1},{2,18},{18,2},{3,19},{19,3},{4,20},{20... | collective-permute-start | bytes 4325384 | tf_op jit(solution)/shard_map/ppermute | solution.py:48
  117.4 37.7 %collective-permute-start.18 = (bf16[2,2,64,1408]{3,2,1,0:T(8,128)(2,1)}, bf16[2,2,64,1408]{3,2,1,0:T(8,128)(2,1)}, u32[]{:S(2)}, u32[]{:S(2)}) collective-permute-start(bf16[2,2,64,1408]{3,2,1,0:T(8,128)(2,1)} %slice.115), channel_id=1, source_target_pairs={{0,2},{2,0},{1,3},{3,1},{4,6},{6,4},{5,7},{7,5},{8,10},{10,8},{9,1... | collective-permute-start | bytes 2162696 | tf_op jit(solution)/shard_map/ppermute | solution.py:52
  164.7 28.2 %collective-permute-start.26 = (bf16[2,2,64,1408]{3,2,1,0:T(8,128)(2,1)}, bf16[2,2,64,1408]{3,2,1,0:T(8,128)(2,1)}, u32[]{:S(2)}, u32[]{:S(2)}) collective-permute-start(bf16[2,2,64,1408]{3,2,1,0:T(8,128)(2,1)} %collective-permute-done.18.refs_15_), channel_id=1, source_target_pairs={{0,16},{16,0},{1,17},{17,1},{2,18},{18,2},{3,19},{19,3},{4,20},{20... | collective-permute-start | bytes 2162696 | tf_op jit(solution)/shard_map/ppermute | solution.py:48
  192.9 24.8 %collective-permute-start.28 = (bf16[176,2048]{1,0:T(8,128)(2,1)S(1)}, bf16[176,2048]{1,0:T(8,128)(2,1)S(1)}, u32[]{:S(2)}, u32[]{:S(2)}) collective-permute-start(bf16[176,2048]{1,0:T(8,128)(2,1)S(1)} %copy-done.21), channel_id=1, source_target_pairs={{0,16},{16,0},{1,17},{17,1},{2,18},{18,2},{3,19},{19,3},{4,20},{20... | collective-permute-start | bytes 2162696 | tf_op jit(solution)/shard_map/ppermute | solution.py:48
  193.7 24.0 %collective-permute-start.27 = (bf16[96,2048]{1,0:T(8,128)(2,1)}, bf16[96,2048]{1,0:T(8,128)(2,1)S(1)}, u32[]{:S(2)}, u32[]{:S(2)}) collective-permute-start(bf16[96,2048]{1,0:T(8,128)(2,1)} %slice.111), channel_id=1, source_target_pairs={{0,2},{2,0},{1,3},{3,1},{4,6},{6,4},{5,7},{7,5},{8,10},{10,8},{9,1... | collective-permute-start | bytes 1179656 | tf_op jit(solution)/shard_map/ppermute | solution.py:52
  295.4 25.1 %collective-permute-start.47 = (bf16[256,1408]{1,0:T(8,128)(2,1)}, bf16[256,1408]{1,0:T(8,128)(2,1)S(1)}, u32[]{:S(2)}, u32[]{:S(2)}) collective-permute-start(bf16[256,1408]{1,0:T(8,128)(2,1)} %get-tuple-element.1027), channel_id=1, source_target_pairs={{0,16},{16,0},{1,17},{17,1},{2,18},{18,2},{3,19},{19,3},{4,20},{20... | collective-permute-start | bytes 2162696 | tf_op jit(solution)/shard_map/ppermute | solution.py:48
  320.5 22.5 %collective-permute-start.52 = (bf16[512,2048]{1,0:T(8,128)(2,1)}, bf16[512,2048]{1,0:T(8,128)(2,1)}, u32[]{:S(2)}, u32[]{:S(2)}) collective-permute-start(bf16[512,2048]{1,0:T(8,128)(2,1)} %get-tuple-element.1103), channel_id=1, source_target_pairs={{0,4},{4,0},{1,5},{5,1},{2,6},{6,2},{3,7},{7,3},{8,12},{12,8},{9,1... | collective-permute-start | bytes 6291464 | tf_op jit(solution)/shard_map/ppermute | solution.py:60
  391.7 38.1 %all-to-all-start.3 = ((bf16[4,128,2048]{2,1,0:T(8,128)(2,1)}), bf16[4,128,2048]{2,1,0:T(8,128)(2,1)S(1)}, u32[]{:S(2)}, u32[]{:S(2)}) async-start(bf16[4,128,2048]{2,1,0:T(8,128)(2,1)} %bitcast.29), calls=%async_computation.3 | async-start | bytes 4194304 | tf_op jit(solution)/shard_map/all_to_all | solution.py:69
  395.5 34.3 %collective-permute-start.66 = (bf16[512,1408]{1,0:T(8,128)(2,1)}, bf16[512,1408]{1,0:T(8,128)(2,1)S(1)}, u32[]{:S(2)}, u32[]{:S(2)}) collective-permute-start(bf16[512,1408]{1,0:T(8,128)(2,1)} %get-tuple-element.1211), channel_id=1, source_target_pairs={{0,16},{16,0},{1,17},{17,1},{2,18},{18,2},{3,19},{19,3},{4,20},{20... | collective-permute-start | bytes 4325384 | tf_op jit(solution)/shard_map/ppermute | solution.py:48
  397.3 29.4 %collective-permute-start.67 = (bf16[128,1408]{1,0:T(8,128)(2,1)}, bf16[128,1408]{1,0:T(8,128)(2,1)S(1)}, u32[]{:S(2)}, u32[]{:S(2)}) collective-permute-start(bf16[128,1408]{1,0:T(8,128)(2,1)} %get-tuple-element.1210), channel_id=1, source_target_pairs={{0,2},{2,0},{1,3},{3,1},{4,6},{6,4},{5,7},{7,5},{8,10},{10,8},{9,1... | collective-permute-start | bytes 1081352 | tf_op jit(solution)/shard_map/ppermute | solution.py:52
  435.5 26.2 %collective-permute-start.69 = (bf16[96,2048]{1,0:T(8,128)(2,1)}, bf16[96,2048]{1,0:T(8,128)(2,1)}, u32[]{:S(2)}, u32[]{:S(2)}) collective-permute-start(bf16[96,2048]{1,0:T(8,128)(2,1)} %slice.147), channel_id=1, source_target_pairs={{0,2},{2,0},{1,3},{3,1},{4,6},{6,4},{5,7},{7,5},{8,10},{10,8},{9,1... | collective-permute-start | bytes 1179656 | tf_op jit(solution)/shard_map/ppermute | solution.py:52
  463.8 22.9 %collective-permute-start.75 = (bf16[512,768]{1,0:T(8,128)(2,1)}, bf16[512,768]{1,0:T(8,128)(2,1)S(1)}, u32[]{:S(2)}, u32[]{:S(2)}) collective-permute-start(bf16[512,768]{1,0:T(8,128)(2,1)} %get-tuple-element.1327), channel_id=1, source_target_pairs={{0,16},{16,0},{1,17},{17,1},{2,18},{18,2},{3,19},{19,3},{4,20},{20... | collective-permute-start | bytes 2359304 | tf_op jit(solution)/shard_map/ppermute | solution.py:48
  487.8 31.3 %all-to-all-start.4 = ((bf16[8,64,1408]{2,1,0:T(8,128)(2,1)}), bf16[8,64,1408]{2,1,0:T(8,128)(2,1)S(1)}, u32[]{:S(2)}, u32[]{:S(2)}) async-start(bf16[8,64,1408]{2,1,0:T(8,128)(2,1)} %bitcast.77), calls=%async_computation.4 | async-start | bytes 2883584 | tf_op jit(solution)/shard_map/all_to_all | solution.py:919
  527.5 28.6 %collective-permute-start.84 = (bf16[80,2048]{1,0:T(8,128)(2,1)S(1)}, bf16[80,2048]{1,0:T(8,128)(2,1)S(1)}, u32[]{:S(2)}, u32[]{:S(2)}) collective-permute-start(bf16[80,2048]{1,0:T(8,128)(2,1)S(1)} %copy-done.43), channel_id=1, source_target_pairs={{0,2},{2,0},{1,3},{3,1},{4,6},{6,4},{5,7},{7,5},{8,10},{10,8},{9,1... | collective-permute-start | bytes 983048 | tf_op jit(solution)/shard_map/ppermute | solution.py:52
  529.8 28.0 %all-to-all-start.5 = ((bf16[8,64,768]{2,1,0:T(8,128)(2,1)}), bf16[8,64,768]{2,1,0:T(8,128)(2,1)S(1)}, u32[]{:S(2)}, u32[]{:S(2)}) async-start(bf16[8,64,768]{2,1,0:T(8,128)(2,1)} %bitcast.41), calls=%async_computation.5 | async-start | bytes 1572864 | tf_op jit(solution)/shard_map/all_to_all | solution.py:919
  (161 other events, 1891.6 us)
